TPU v7x, 32 devices: a whole 2x2x4 slice. The times are simulated.
32 devices in a mesh: mem: 8 (over z, x), sub: 4 (over y, core).
Axes of the slice: x: 2, y: 2, z: 4, core: 2. Of those that a mesh axis runs over, the one named last changes fastest.
Arguments:
- ensemble: float32 [32, 3, 128, 2048], P('mem', None, 'sub'), may hold values from -6 to 6
- sea_depth: float32 [128, 2048], P('sub'), may hold values from 0.5 to 2
- cutoff: int32 [128, 2048], P('sub', 'mem'), may hold values from 16 to 64
- obs_index: int32 [4, 256], replicated, may hold values from 0 to 262143
- obs_value: float32 [4, 256], replicated, may hold values from -6 to 6
- obs_var: float32 [4, 256], replicated, may hold values from 0.5 to 2
Outputs:
- analysis: float32 [32, 3, 128, 2048], P(None, None, 'sub', 'mem')
All inputs are finite; a program needn't handle non-finite values.
Results may differ from a plain program's by a relative error of at most 0.0001.
Values sent between devices are 32-bit elements; how exact they have to be, the bound alone decides.
No kernel may reach another device: no remote copies, remote signals or barrier semaphores. Data moves between devices by JAX's collectives and lax.ppermute only.
A program may use at most 192 MiB of HBM per device.

v0:
```python
import jax
import jax.numpy as jnp
from jax import lax
from jax.sharding import PartitionSpec as P

STEPS = 4
BATCHES = 4


step_size = 0.3
coriolis = 0.2
highest = lax.Precision.HIGHEST


def padded(shard, sides, width):
    for axis, dim in sides:
        peers, length = (lax.axis_size(axis), shard.shape[dim])
        up = [(i, (i + 1) % peers) for i in range(peers)]
        down = [(j, i) for i, j in up]
        last = lax.slice_in_dim(shard, length - width, length, axis=dim)
        leading = lax.slice_in_dim(shard, 0, width, axis=dim)
        before = lax.ppermute(last, axis, up)
        after = lax.ppermute(leading, axis, down)
        shard = jnp.concatenate([before, shard, after], axis=dim)
    return shard


def across_cols(field):
    return (jnp.roll(field, -1, 2) - jnp.roll(field, 1, 2)) * 0.5


def momentum(height, east_wind, north_wind):
    height_ext = padded(height, (("sub", 1),), 1)
    height_dx = (height_ext[:, 2:] - height_ext[:, :-2]) * 0.5
    east_new = east_wind + step_size * (coriolis * north_wind - height_dx)
    north_new = north_wind + step_size * (-coriolis * east_wind - across_cols(height))
    return (east_new, north_new)


def continuity(height, east_wind, north_wind, sea_depth):
    flux_ext = padded(sea_depth * east_wind, (("sub", 1),), 1)
    divergence = (flux_ext[:, 2:] - flux_ext[:, :-2]) * 0.5 + across_cols(sea_depth * north_wind)
    return height - step_size * divergence


def localize(obs_x, obs_y, cell_x, cell_y, radius_sq, size_x, size_y):
    gap_x = jnp.abs(cell_x[None, :] - obs_x[:, None])
    gap_x = jnp.minimum(gap_x, size_x - gap_x)
    gap_y = jnp.abs(cell_y[None, :] - obs_y[:, None])
    gap_y = jnp.minimum(gap_y, size_y - gap_y)
    dist_sq = (gap_x * gap_x + gap_y * gap_y).astype(jnp.float32)
    dist_ratio = dist_sq / radius_sq[None, :]
    return jnp.square(jnp.maximum(1.0 - dist_ratio, 0.0))


def analysis_weights(prior_obs, values, variance):
    member_count = prior_obs.shape[1]
    obs_mean = jnp.mean(prior_obs, 1)
    obs_anom = prior_obs - obs_mean[:, None]
    innov_cov = jnp.dot(obs_anom, obs_anom.T, precision=highest) / (member_count - 1) + jnp.diag(
        variance
    )
    factor = jnp.linalg.cholesky(innov_cov)
    right_side = jnp.concatenate([(values - obs_mean)[:, None], obs_anom], 1)
    solved = jax.scipy.linalg.cho_solve((factor, True), right_side)
    return (obs_anom, solved[:, :1] - 0.5 * solved[:, 1:])


def update_state(members, obs_anom, weights_mix, loc_weight, cell_count):
    member_count = members.shape[0]
    obs_count = obs_anom.shape[0]
    state_anom = members - jnp.mean(members, 0)
    cross_cov = jnp.dot(obs_anom, state_anom, precision=highest) / (member_count - 1)
    loc_gain = (cross_cov.reshape(obs_count, 3, cell_count) * loc_weight[:, None, :]).reshape(
        obs_count, 3 * cell_count
    )
    return members + jnp.dot(weights_mix.T, loc_gain, precision=highest)


def local(ensemble, sea_depth, cutoff, obs_index, obs_value, obs_var):
    height = ensemble[:, 0]
    east_wind = ensemble[:, 1]
    north_wind = ensemble[:, 2]
    for step_id in range(STEPS - 1):
        east_wind, north_wind = momentum(height, east_wind, north_wind)
        height = continuity(height, east_wind, north_wind, sea_depth)
    east_wind, north_wind = momentum(height, east_wind, north_wind)
    height = continuity(height, east_wind, north_wind, sea_depth)
    point_state = lax.all_to_all(
        jnp.stack([height, east_wind, north_wind], 1),
        "mem",
        split_axis=3,
        concat_axis=0,
        tiled=True,
    )
    member_count = point_state.shape[0]
    row_count, col_block = cutoff.shape
    x_start = lax.axis_index("sub") * row_count
    y_start = lax.axis_index("mem") * col_block
    size_x = row_count * lax.axis_size("sub")
    size_y = col_block * lax.axis_size("mem")
    cell_count = row_count * col_block
    cell_ids = jnp.arange(cell_count, dtype=jnp.int32)
    cell_x = x_start + cell_ids // col_block
    cell_y = y_start + cell_ids % col_block
    radius_sq = jnp.square(cutoff.reshape(cell_count).astype(jnp.float32))
    members = point_state.reshape(member_count, 3 * cell_count)
    for batch_id in range(BATCHES):
        obs_cell = obs_index[batch_id]
        obs_x = obs_cell // size_y
        obs_y = obs_cell % size_y
        select_obs_x = obs_cell // size_y
        select_obs_y = obs_cell % size_y
        inside = (
            (select_obs_x >= x_start)
            & (select_obs_x < x_start + row_count)
            & (select_obs_y >= y_start)
            & (select_obs_y < y_start + col_block)
        )
        local_id = (select_obs_x - x_start) * col_block + (select_obs_y - y_start)
        local_part = lax.dot_general(
            ((local_id[:, None] == cell_ids[None, :]) & inside[:, None]).astype(jnp.float32),
            members[:, :cell_count],
            (((1,), (1,)), ((), ())),
            precision=highest,
        )
        prior_obs = lax.psum(local_part, ("mem", "sub"))
        obs_anom, weights_mix = analysis_weights(prior_obs, obs_value[batch_id], obs_var[batch_id])
        loc_weight = localize(obs_x, obs_y, cell_x, cell_y, radius_sq, size_x, size_y)
        members = update_state(members, obs_anom, weights_mix, loc_weight, cell_count)
    return members.reshape(member_count, 3, row_count, col_block)


def solution(mesh):
    return jax.shard_map(
        local,
        mesh=mesh,
        in_specs=(P("mem", None, "sub", None), P("sub", None), P("sub", "mem"), P(), P(), P()),
        out_specs=P(None, None, "sub", "mem"),
        check_vma=False,
    )
```

profile of v0, /device:TPU:0, one launch (start us, length us, event | category | flops | bytes accessed | tf_op | source)
XLA Modules:
  0.0 978.0 jit_solution(10081739926307667081)
XLA Ops:
  0.0 3.1 fusion.230
  4.4 2.4 collective-permute-start
  6.8 2.0 fusion.253
  14.1 5.2 broadcast_multiply_fusion.7
  31.3 2.5 broadcast_multiply_fusion.5
  41.6 2.2 collective-permute-done.9
  43.8 2.4 broadcast_multiply_fusion.3
  56.0 2.5 broadcast_multiply_fusion.1
  64.5 9.0 copy.119
  73.5 12.3 %reshape.856 = f32[8,1,98304]{2,1,0:T(1,128)} reshape(f32[2048,3,4,32]{3,2,1,0:T(4,128)} %bitcast.232) | data formatting | bytes 6291456
  85.8 5.8 all-to-all-start
  91.7 26.8 %fusion.34 = (f32[256,8192]{0,1:T(8,128)}, f32[256,8192]{0,1:T(8,128)}, f32[256,8192]{0,1:T(8,128)}, f32[256,8192]{0,1:T(8,128)S(1)}) fusion(s32[256]{0:T(256)S(1)} %get-tuple-element.71, s32[256]{0:T(256)S(1)} %get-tuple-element.70, f32[8192]{0:T(1024)S(1)} %bitcast.244, s32[8192]{0:T(1024)S(1)} %copy-done.15, s32[8192]{0:T(1024)S(1)} %copy-done.14, ...), kind=kLoop, calls=%fused_computation.58 | loop fusion | flops 134217728 | bytes 33660928 | tf_op jit(solution)/shard_map/square | solution.py:53
  118.5 8.6 mul.346
  127.1 24.7 %copy.123 = f32[256,24576]{1,0:T(8,128)} copy(f32[256,24576]{0,1:T(8,128)} %bitcast.228) | data formatting | bytes 50331648 | tf_op jit(solution)/shard_map/mul | solution.py:74
  151.8 11.7 %mul.353 = f32[256,3,8192]{0,2,1:T(8,128)} broadcast(f32[256,8192]{0,1:T(8,128)} %get-tuple-element.165), dimensions={0,2} | broadcast | bytes 33554432 | tf_op jit(solution)/shard_map/mul | solution.py:74
  163.5 24.7 %copy.126 = f32[256,24576]{1,0:T(8,128)} copy(f32[256,24576]{0,1:T(8,128)} %bitcast.229) | data formatting | bytes 50331648 | tf_op jit(solution)/shard_map/mul | solution.py:74
  188.2 11.9 %mul.360 = f32[256,3,8192]{0,2,1:T(8,128)} broadcast(f32[256,8192]{0,1:T(8,128)} %get-tuple-element.166), dimensions={0,2} | broadcast | bytes 33554432 | tf_op jit(solution)/shard_map/mul | solution.py:74
  200.1 24.7 %copy.129 = f32[256,24576]{1,0:T(8,128)} copy(f32[256,24576]{0,1:T(8,128)} %bitcast.230) | data formatting | bytes 50331648 | tf_op jit(solution)/shard_map/mul | solution.py:74
  224.8 11.9 %mul.367 = f32[256,3,8192]{0,2,1:T(8,128)} broadcast(f32[256,8192]{0,1:T(8,128)} %get-tuple-element.164), dimensions={0,2} | broadcast | bytes 33554432 | tf_op jit(solution)/shard_map/mul | solution.py:74
  236.6 24.8 %copy.132 = f32[256,24576]{1,0:T(8,128)} copy(f32[256,24576]{0,1:T(8,128)} %bitcast.231) | data formatting | bytes 50331648 | tf_op jit(solution)/shard_map/mul | solution.py:74
  264.9 11.1 %reduce.9 = f32[8,98304]{1,0:T(8,128)} reduce(f32[8,1,98304]{2,1,0:T(1,128)S(1)} %all-to-all-done, f32[]{:T(128)} %broadcast.1324), dimensions={1}, to_apply=%all_to_all.11.reduce_sub_computation | reduce | bytes 6291460 | tf_op jit(solution)/shard_map/all_to_all | solution.py:89
  276.0 13.2 %reshape.857 = f32[2048,3,4,32]{3,2,1,0:T(4,128)} reshape(f32[8,98304]{1,0:T(8,128)} %reduce.9) | data formatting | bytes 6291456
  289.2 9.9 %copy.120 = f32[4,3,32,8,256]{4,2,1,0,3:T(8,128)S(1)} copy(f32[4,3,32,8,256]{2,0,1,4,3:T(4,128)} %bitcast.233) | data formatting | bytes 6291456 | tf_op jit(solution)/shard_map/all_to_all | solution.py:89
  299.3 2.0 reshape.826
  301.3 5.9 fusion.46
  307.2 40.4 %psum.28 = f32[256,32]{0,1:T(8,128)S(1)} all-reduce(f32[256,32]{0,1:T(8,128)S(1)} %fusion.46), channel_id=1, replica_groups=mesh['mem'=8,'sub'=4] {'mem','sub'}, use_global_device_ids=true, to_apply=%region_0.1 | all-reduce | flops 8192 | bytes 65536 | tf_op jit(solution)/shard_map/psum | solution.py:127
  351.2 11.7 %cholesky.214 = f32[128,128]{1,0:T(8,128)S(1)} custom-call(f32[128,128]{1,0:T(8,128)S(1)} %cholesky.346), custom_call_target="Cholesky" | custom-call | tf_op jit(solution)/shard_map/jit(cholesky)/cholesky | solution.py:63
  365.6 11.3 %custom-call.19 = f32[1,128,128]{1,2,0:T(8,128)} custom-call(f32[1,128,128]{2,1,0:T(8,128)} %get-tuple-element.183), custom_call_target="InvertDiagBlocksLowerTriangular" | custom-call | tf_op jit(solution)/shard_map/jit(cholesky)/cholesky | solution.py:63
  379.7 13.2 %cholesky.231 = f32[128,128]{1,0:T(8,128)} custom-call(f32[128,128]{1,0:T(8,128)} %convolution_subtract_fusion.3), custom_call_target="Cholesky" | custom-call | tf_op jit(solution)/shard_map/jit(cholesky)/cholesky | solution.py:63
  399.3 6.3 while.8
  405.6 21.3 %custom-call.20 = f32[2,128,128]{1,2,0:T(8,128)} custom-call(f32[2,128,128]{2,1,0:T(8,128)} %get-tuple-element.33), custom_call_target="InvertDiagBlocksLowerTriangular" | custom-call | tf_op jit(solution)/shard_map/jit(_cho_solve)/triangular_solve | solution.py:65
  432.4 26.1 %fusion = f32[256,24576]{1,0:T(8,128)} fusion(f32[256,24576]{1,0:T(8,128)} %copy.123, f32[256,32]{0,1:T(8,128)S(1)} %broadcast_subtract_fusion.3, f32[32,24576]{1,0:T(8,128)S(1)} %copy-done, f32[24576]{0:T(1024)S(1)} %bitcast.242), kind=kOutput, calls=%fused_computation.12 | convolution fusion | flops 2429288448 | bytes 53608448 | tf_op jit(solution)/shard_map/dot_general | solution.py:73
  458.5 17.5 %fusion.257 = (f32[24576]{0:T(1024)S(1)}, f32[32,24576]{1,0:T(8,128)S(1)}) fusion(f32[32,24576]{1,0:T(8,128)S(1)} %copy-done, f32[256,24576]{1,0:T(8,128)} %fusion, f32[128,33]{0,1:T(8,128)S(1)} %fusion.147, f32[128,33]{0,1:T(8,128)S(1)} %fusion.145, f32[256]{0:T(256)S(1)} %bitcast.253), kind=kOutput, calls=%fused_computation.444 | convolution fusion | flops 2417491968 | bytes 31590400 | tf_op jit(solution)/shard_map/dot_general | solution.py:77
  477.7 4.5 fusion.44
  482.2 41.6 %psum.29 = f32[256,32]{0,1:T(8,128)S(1)} all-reduce(f32[256,32]{0,1:T(8,128)S(1)} %fusion.44), channel_id=1, replica_groups=mesh['mem'=8,'sub'=4] {'mem','sub'}, use_global_device_ids=true, to_apply=%region_7.10 | all-reduce | flops 8192 | bytes 65536 | tf_op jit(solution)/shard_map/psum | solution.py:127
  524.5 11.7 %cholesky.248 = f32[128,128]{1,0:T(8,128)S(1)} custom-call(f32[128,128]{1,0:T(8,128)S(1)} %cholesky.349), custom_call_target="Cholesky" | custom-call | tf_op jit(solution)/shard_map/jit(cholesky)/cholesky | solution.py:63
  536.2 9.8 %custom-call.21 = f32[1,128,128]{1,2,0:T(8,128)S(1)} custom-call(f32[1,128,128]{2,1,0:T(8,128)S(1)} %get-tuple-element.179), custom_call_target="InvertDiagBlocksLowerTriangular" | custom-call | tf_op jit(solution)/shard_map/jit(cholesky)/cholesky | solution.py:63
  546.5 11.7 %cholesky.265 = f32[128,128]{1,0:T(8,128)S(1)} custom-call(f32[128,128]{1,0:T(8,128)S(1)} %convolution_subtract_fusion.2), custom_call_target="Cholesky" | custom-call | tf_op jit(solution)/shard_map/jit(cholesky)/cholesky | solution.py:63
  560.9 4.0 while.9
  564.9 19.9 %custom-call.22 = f32[2,128,128]{1,2,0:T(8,128)S(1)} custom-call(f32[2,128,128]{2,1,0:T(8,128)S(1)} %get-tuple-element.34), custom_call_target="InvertDiagBlocksLowerTriangular" | custom-call | tf_op jit(solution)/shard_map/jit(_cho_solve)/triangular_solve | solution.py:65
  586.8 27.8 %fusion.1 = f32[256,24576]{1,0:T(8,128)} fusion(f32[256,24576]{1,0:T(8,128)} %copy.126, f32[256,32]{0,1:T(8,128)S(1)} %broadcast_subtract_fusion.2, f32[32,24576]{1,0:T(8,128)} %copy-done.1, f32[24576]{0:T(1024)S(1)} %broadcast_multiply_fusion.10), kind=kOutput, calls=%fused_computation.13 | convolution fusion | flops 2429288448 | bytes 53608448 | tf_op jit(solution)/shard_map/dot_general | solution.py:73
  614.7 17.5 %fusion.258 = (f32[24576]{0:T(1024)S(1)}, f32[32,24576]{1,0:T(8,128)S(1)}) fusion(f32[32,24576]{1,0:T(8,128)S(1)} %copy-done.2, f32[256,24576]{1,0:T(8,128)} %fusion.1, f32[128,33]{0,1:T(8,128)S(1)} %fusion.151, f32[128,33]{0,1:T(8,128)S(1)} %fusion.149, f32[256]{0:T(256)S(1)} %bitcast.254), kind=kOutput, calls=%fused_computation.445 | convolution fusion | flops 2417491968 | bytes 31590400 | tf_op jit(solution)/shard_map/dot_general | solution.py:77
  632.2 4.5 fusion.42
  636.7 39.6 %psum.30 = f32[256,32]{0,1:T(8,128)S(1)} all-reduce(f32[256,32]{0,1:T(8,128)S(1)} %fusion.42), channel_id=1, replica_groups=mesh['mem'=8,'sub'=4] {'mem','sub'}, use_global_device_ids=true, to_apply=%region_10.13 | all-reduce | flops 8192 | bytes 65536 | tf_op jit(solution)/shard_map/psum | solution.py:127
  679.3 11.7 %cholesky.282 = f32[128,128]{1,0:T(8,128)S(1)} custom-call(f32[128,128]{1,0:T(8,128)S(1)} %cholesky.352), custom_call_target="Cholesky" | custom-call | tf_op jit(solution)/shard_map/jit(cholesky)/cholesky | solution.py:63
  693.2 11.3 %custom-call.23 = f32[1,128,128]{1,2,0:T(8,128)} custom-call(f32[1,128,128]{2,1,0:T(8,128)} %get-tuple-element.175), custom_call_target="InvertDiagBlocksLowerTriangular" | custom-call | tf_op jit(solution)/shard_map/jit(cholesky)/cholesky | solution.py:63
  707.3 13.2 %cholesky.299 = f32[128,128]{1,0:T(8,128)} custom-call(f32[128,128]{1,0:T(8,128)} %convolution_subtract_fusion.1), custom_call_target="Cholesky" | custom-call | tf_op jit(solution)/shard_map/jit(cholesky)/cholesky | solution.py:63
  725.5 6.6 while.10
  730.1 2.0 bitcast_dynamic-update-slice_fusion.10
  732.1 21.3 %custom-call.24 = f32[2,128,128]{1,2,0:T(8,128)} custom-call(f32[2,128,128]{2,1,0:T(8,128)} %get-tuple-element.35), custom_call_target="InvertDiagBlocksLowerTriangular" | custom-call | tf_op jit(solution)/shard_map/jit(_cho_solve)/triangular_solve | solution.py:65
  758.1 26.2 %fusion.2 = f32[256,24576]{1,0:T(8,128)} fusion(f32[256,24576]{1,0:T(8,128)} %copy.129, f32[256,32]{0,1:T(8,128)S(1)} %broadcast_subtract_fusion.1, f32[32,24576]{1,0:T(8,128)S(1)} %get-tuple-element.199, f32[24576]{0:T(1024)S(1)} %broadcast_multiply_fusion.9), kind=kOutput, calls=%fused_computation.14 | convolution fusion | flops 2429288448 | bytes 53608448 | tf_op jit(solution)/shard_map/dot_general | solution.py:73
  784.3 19.3 %fusion.259 = (f32[24576]{0:T(1024)S(1)}, f32[32,24576]{1,0:T(8,128)S(1)}) fusion(f32[32,24576]{1,0:T(8,128)} %copy-done.3, f32[256,24576]{1,0:T(8,128)} %fusion.2, f32[128,33]{0,1:T(8,128)S(1)} %fusion.155, f32[128,33]{0,1:T(8,128)S(1)} %fusion.153, f32[256]{0:T(256)S(1)} %bitcast.255), kind=kOutput, calls=%fused_computation.446 | convolution fusion | flops 2417491968 | bytes 31590400 | tf_op jit(solution)/shard_map/dot_general | solution.py:77
  803.7 4.5 fusion.40
  808.2 41.5 %psum.31 = f32[256,32]{0,1:T(8,128)S(1)} all-reduce(f32[256,32]{0,1:T(8,128)S(1)} %fusion.40), channel_id=1, replica_groups=mesh['mem'=8,'sub'=4] {'mem','sub'}, use_global_device_ids=true, to_apply=%region_13.16 | all-reduce | flops 8192 | bytes 65536 | tf_op jit(solution)/shard_map/psum | solution.py:127
  852.8 11.7 %cholesky.316 = f32[128,128]{1,0:T(8,128)S(1)} custom-call(f32[128,128]{1,0:T(8,128)S(1)} %cholesky.355), custom_call_target="Cholesky" | custom-call | tf_op jit(solution)/shard_map/jit(cholesky)/cholesky | solution.py:63
  866.6 11.3 %custom-call.25 = f32[1,128,128]{1,2,0:T(8,128)} custom-call(f32[1,128,128]{2,1,0:T(8,128)} %get-tuple-element.171), custom_call_target="InvertDiagBlocksLowerTriangular" | custom-call | tf_op jit(solution)/shard_map/jit(cholesky)/cholesky | solution.py:63
  880.7 13.2 %cholesky.333 = f32[128,128]{1,0:T(8,128)} custom-call(f32[128,128]{1,0:T(8,128)} %convolution_subtract_fusion), custom_call_target="Cholesky" | custom-call | tf_op jit(solution)/shard_map/jit(cholesky)/cholesky | solution.py:63
  899.1 6.6 while.11
  900.3 2.0 bitcast_dynamic-update-slice_fusion.11
  903.6 2.0 bitcast_dynamic-update-slice_fusion.11
  905.7 21.2 %custom-call.26 = f32[2,128,128]{1,2,0:T(8,128)} custom-call(f32[2,128,128]{2,1,0:T(8,128)} %get-tuple-element.36), custom_call_target="InvertDiagBlocksLowerTriangular" | custom-call | tf_op jit(solution)/shard_map/jit(_cho_solve)/triangular_solve | solution.py:65
  931.7 26.1 %fusion.3 = f32[256,24576]{1,0:T(8,128)} fusion(f32[256,24576]{1,0:T(8,128)} %copy.132, f32[256,32]{0,1:T(8,128)S(1)} %broadcast_subtract_fusion, f32[32,24576]{1,0:T(8,128)S(1)} %get-tuple-element.203, f32[24576]{0:T(1024)S(1)} %broadcast_multiply_fusion.8), kind=kOutput, calls=%fused_computation.15 | convolution fusion | flops 2429288448 | bytes 53608448 | tf_op jit(solution)/shard_map/dot_general | solution.py:73
  957.8 17.3 %convolution_add_fusion = f32[32,24576]{1,0:T(8,128)S(1)} fusion(f32[32,24576]{1,0:T(8,128)S(1)} %get-tuple-element.203, f32[256,24576]{1,0:T(8,128)} %fusion.3, f32[128,33]{0,1:T(8,128)S(1)} %fusion.159, f32[128,33]{0,1:T(8,128)S(1)} %fusion.157, f32[256]{0:T(256)S(1)} %bitcast.256), kind=kOutput, calls=%fused_computation.16 | convolution fusion | flops 2416730112 | bytes 31492096 | tf_op jit(solution)/shard_map/dot_general | solution.py:77
  975.1 2.6 copy.142
  (261 shorter events, 122.0 us)
Async XLA Ops:
  0.0 8.9 copy-start.22
  0.0 14.1 %copy-start.4 = (f32[32,2048]{1,0:T(8,128)S(1)}, f32[32,2048]{1,0:T(8,128)}, u32[]{:S(2)}) copy-start(f32[32,2048]{1,0:T(8,128)} %param.10) | copy-start | bytes 786436
  4.4 9.7 collective-permute-start
  6.8 7.3 collective-permute-start.1
  20.0 3.6 collective-permute-start.2
  21.8 3.3 collective-permute-start.3
  27.3 2.3 collective-permute-start.4
  28.0 3.3 collective-permute-start.5
  34.5 1.8 collective-permute-start.6
  34.7 3.3 collective-permute-start.7
  39.8 1.8 collective-permute-start.8
  40.0 3.8 collective-permute-start.9
  46.9 1.8 collective-permute-start.10
  46.9 3.4 collective-permute-start.11
  52.0 2.2 collective-permute-start.12
  52.6 3.3 collective-permute-start.13
  59.1 1.8 collective-permute-start.14
  59.3 3.3 collective-permute-start.15
  73.5 18.2 %copy-start.14 = (s32[8192]{0:T(1024)S(1)}, s32[8192]{0:T(1024)}, u32[]{:S(2)}) copy-start(s32[8192]{0:T(1024)} %get-tuple-element.209) | copy-start | bytes 98308
  73.5 18.2 %copy-start.15 = (s32[8192]{0:T(1024)S(1)}, s32[8192]{0:T(1024)}, u32[]{:S(2)}) copy-start(s32[8192]{0:T(1024)} %get-tuple-element.210) | copy-start | bytes 98308
  73.5 18.2 %copy-start.16 = (f32[4,2,8,128]{3,1,2,0:T(2,128)S(1)}, f32[4,2,8,128]{3,1,2,0:T(2,128)}, u32[]{:S(2)}) copy-start(f32[4,2,8,128]{3,1,2,0:T(2,128)} %copy.141) | copy-start | bytes 98308
  73.5 18.2 %copy-start.17 = (s32[256]{0:T(256)S(1)}, s32[256]{0:T(256)}, u32[]{:S(2)}) copy-start(s32[256]{0:T(256)} %get-tuple-element.79) | copy-start | bytes 3076
  73.5 18.2 %copy-start.18 = (s32[256]{0:T(256)S(1)}, s32[256]{0:T(256)}, u32[]{:S(2)}) copy-start(s32[256]{0:T(256)} %get-tuple-element.80) | copy-start | bytes 3076
  73.5 18.2 %copy-start.19 = (s32[256]{0:T(256)S(1)}, s32[256]{0:T(256)}, u32[]{:S(2)}) copy-start(s32[256]{0:T(256)} %get-tuple-element.76) | copy-start | bytes 3076
  73.5 18.2 %copy-start.20 = (s32[256]{0:T(256)S(1)}, s32[256]{0:T(256)}, u32[]{:S(2)}) copy-start(s32[256]{0:T(256)} %get-tuple-element.77) | copy-start | bytes 3076
  85.8 178.5 %all-to-all-start = ((f32[8,1,98304]{2,1,0:T(1,128)}), f32[8,1,98304]{2,1,0:T(1,128)S(1)}, u32[]{:S(2)}, u32[]{:S(2)}) async-start(f32[8,1,98304]{2,1,0:T(1,128)} %reshape.856), calls=%async_computation | async-start | bytes 6291456 | tf_op jit(solution)/shard_map/all_to_all | solution.py:89
  236.6 27.1 %copy-start.23 = (f32[4,256]{1,0:T(4,128)S(1)}, f32[4,256]{1,0:T(4,128)}, u32[]{:S(2)}) copy-start(f32[4,256]{1,0:T(4,128)} %param.14) | copy-start | bytes 12292
  299.1 2.2 copy-start.30
  301.3 131.1 %copy-start = (f32[32,24576]{1,0:T(8,128)S(1)}, f32[32,24576]{1,0:T(8,128)}, u32[]{:S(2)}) copy-start(f32[32,24576]{1,0:T(8,128)} %reshape.826) | copy-start | bytes 9437188
  350.5 0.7 copy-start.8
  362.9 0.6 copy-start.11
  393.8 2.6 copy-start.5
  458.5 19.2 %copy-start.26 = (s32[256]{0:T(256)S(1)}, s32[256]{0:T(256)}, u32[]{:S(2)}) copy-start(s32[256]{0:T(256)} %subtract_add_fusion.2) | copy-start | bytes 3076
  458.5 19.2 %copy-start.29 = (pred[256]{0:T(512)(128)(4,1)S(1)}, pred[256]{0:T(512)(128)(4,1)}, u32[]{:S(2)}) copy-start(pred[256]{0:T(512)(128)(4,1)} %get-tuple-element.75) | copy-start | bytes 772
  476.0 1.7 copy-start.1
  476.0 84.9 %copy-start.31 = (s32[2,2]{1,0:T(2,128)S(1)}, s32[2,2]{1,0:T(2,128)}, u32[]{:S(2)}) copy-start(s32[2,2]{1,0:T(2,128)} %get-tuple-element.424) | copy-start | bytes 52
  586.8 27.8 %copy-start.2 = (f32[32,24576]{1,0:T(8,128)S(1)}, f32[32,24576]{1,0:T(8,128)}, u32[]{:S(2)}) copy-start(f32[32,24576]{1,0:T(8,128)} %copy-done.1) | copy-start | bytes 9437188
  614.6 17.5 %copy-start.25 = (s32[256]{0:T(256)S(1)}, s32[256]{0:T(256)}, u32[]{:S(2)}) copy-start(s32[256]{0:T(256)} %subtract_add_fusion.1) | copy-start | bytes 3076
  614.7 17.5 %copy-start.28 = (pred[256]{0:T(512)(128)(4,1)S(1)}, pred[256]{0:T(512)(128)(4,1)}, u32[]{:S(2)}) copy-start(pred[256]{0:T(512)(128)(4,1)} %get-tuple-element.206) | copy-start | bytes 772
  632.2 152.2 %copy-start.3 = (f32[32,24576]{1,0:T(8,128)}, f32[32,24576]{1,0:T(8,128)S(1)}, u32[]{:S(2)}) copy-start(f32[32,24576]{1,0:T(8,128)S(1)} %get-tuple-element.199) | copy-start | bytes 9437188
  632.2 121.2 %copy-start.21 = (f32[4,256]{1,0:T(4,128)S(1)}, f32[4,256]{1,0:T(4,128)}, u32[]{:S(2)}) copy-start(f32[4,256]{1,0:T(4,128)} %param.13) | copy-start | bytes 12292
  678.6 0.7 copy-start.9
  691.1 0.6 copy-start.12
  721.3 2.5 copy-start.6
  784.3 19.4 %copy-start.24 = (s32[256]{0:T(256)S(1)}, s32[256]{0:T(256)}, u32[]{:S(2)}) copy-start(s32[256]{0:T(256)} %subtract_add_fusion) | copy-start | bytes 3076
  784.3 19.4 %copy-start.27 = (pred[256]{0:T(512)(128)(4,1)S(1)}, pred[256]{0:T(512)(128)(4,1)}, u32[]{:S(2)}) copy-start(pred[256]{0:T(512)(128)(4,1)} %get-tuple-element.69) | copy-start | bytes 772
  852.0 0.7 copy-start.10
  864.5 0.6 copy-start.13
  894.7 2.7 copy-start.7
where the time goes:
time: 991 us; the launch traced here: 978 us
  other arithmetic  306 us (31%)
  local copies, waits for them, and re-layouts  244 us (25%)
  matrix products  224 us (23%)
  blocking collectives  163 us (16%)
  waiting for transfers between devices  21.3 us (2%)
  starting transfers between devices  14 us (1%)
    psum x4, blocking collectives, local(): prior_obs = lax.psum(local_part, ('mem', 'sub'))  163 us
    another operation x27, other arithmetic, analysis_weights(): factor = jnp.linalg.cholesky(innov_cov)  152 us
    mul x8, local copies, waits for them, and re-layouts, update_state(): cross_cov.reshape(obs_count, 3, cell_count) * loc_weight[:, None, :]  143 us
    dot_general x4, matrix products, update_state(): jnp.dot(obs_anom, state_anom, precision=highest) / (member_count - 1)  106 us
    another operation x9, other arithmetic, analysis_weights(): solved = jax.scipy.linalg.cho_solve((factor, True), right_side)  87.2 us
    dot_general x4, matrix products, update_state(): return members + jnp.dot(weights_mix.T, loc_gain, precision=highest)  71.7 us
    unnamed x70, local copies, waits for them, and re-layouts  35.9 us
    square x1, other arithmetic, localize(): return jnp.square(jnp.maximum(1.0 - dist_ratio, 0.0))  26.8 us
  transfers between devices with their start and end apart: 17, of which 14 were waited for; matrix products, arithmetic and copies ran while one was open for 18% of the time, Pallas kernels for 0%

commit v1 on v0

v1 whole, which is shorter than its diff:
```python
import functools

import jax
import jax.numpy as jnp
from jax import lax
from jax.experimental import pallas as pl
from jax.experimental.pallas import tpu as pltpu
from jax.sharding import PartitionSpec as P

STEPS = 4
HALO = 2 * STEPS
LANES = 128
OBS_BLOCK = 64
ROW_TILE = 8
VMEM_LIMIT = 48 * 2**20

step_size = 0.3
coriolis = 0.2
highest = lax.Precision.HIGHEST

NT = (((1,), (1,)), ((), ()))
TN = (((0,), (0,)), ((), ()))


def params():
    return pltpu.CompilerParams(vmem_limit_bytes=VMEM_LIMIT)


def vmem(count=1):
    return [pl.BlockSpec(memory_space=pltpu.VMEM)] * count


def smem(count=1):
    return [pl.BlockSpec(memory_space=pltpu.SMEM)] * count


def split_bf16(value):
    high = value.astype(jnp.bfloat16)
    low = (value - high.astype(jnp.float32)).astype(jnp.bfloat16)
    return high, low


def centred(field, axis):
    length = field.shape[axis]
    return pltpu.roll(field, length - 1, axis) - pltpu.roll(field, 1, axis)


def forecast_kernel(ens_ref, up_ref, down_ref, depth_ref, out_ref):
    height, east, north = [
        jnp.concatenate([up_ref[0, f], ens_ref[0, f], down_ref[0, f]], 0) for f in range(3)
    ]
    depth = depth_ref[...]
    half = 0.5 * step_size
    turn = step_size * coriolis
    for _ in range(STEPS):
        east_new = east + turn * north - half * centred(height, 0)
        north_new = north - turn * east - half * centred(height, 1)
        height = height - half * (centred(depth * east_new, 0) + centred(depth * north_new, 1))
        east, north = east_new, north_new
    rows = ens_ref.shape[2]
    blocks, _, _, tiles = out_ref.shape[:4]
    for f, field in enumerate((height, east, north)):
        for d in range(blocks):
            for t in range(tiles):
                first = (d * tiles + t) * LANES
                out_ref[d, 0, f, t] = field[HALO : HALO + rows, first : first + LANES]


def forecast(ensemble, up, down, depth, blocks):
    members, fields, rows, columns = ensemble.shape
    tiles = columns // blocks // LANES
    return pl.pallas_call(
        forecast_kernel,
        grid=(members,),
        in_specs=[
            pl.BlockSpec((1, fields, rows, columns), lambda m: (m, 0, 0, 0)),
            pl.BlockSpec((1, fields, HALO, columns), lambda m: (m, 0, 0, 0)),
            pl.BlockSpec((1, fields, HALO, columns), lambda m: (m, 0, 0, 0)),
            pl.BlockSpec((rows + 2 * HALO, columns), lambda m: (0, 0)),
        ],
        out_specs=pl.BlockSpec(
            (blocks, 1, fields, tiles, rows, LANES), lambda m: (0, m, 0, 0, 0, 0)
        ),
        out_shape=jax.ShapeDtypeStruct(
            (blocks, members, fields, tiles, rows, LANES), jnp.float32
        ),
        compiler_params=params(),
        name="forecast",
    )(ensemble, up, down, depth)


def pick_kernel(base_ref, lane_ref, place_ref, height_ref, out_ref):
    blocks, members, _, tiles, rows, _ = height_ref.shape
    flat = height_ref.reshape(blocks * members * tiles * rows, LANES)
    lanes = lax.broadcasted_iota(jnp.int32, (members, LANES), 1)
    unroll = 16

    def group(g, _):
        def some(i, acc):
            for j in range(unroll):
                k = i * unroll + j
                o = g * LANES + k
                row = flat[pl.ds(base_ref[o], members, stride=tiles * rows), :]
                row = pltpu.roll(row, lane_ref[o], 1)
                acc = jnp.where(lanes == place_ref[o], row, acc)
            return acc

        acc = lax.fori_loop(
            0, LANES // unroll, some, jnp.zeros((members, LANES), jnp.float32)
        )
        out_ref[:, pl.ds(pl.multiple_of(g * LANES, LANES), LANES)] = acc
        return 0

    lax.fori_loop(0, out_ref.shape[1] // LANES, group, 0)


def pick_heights(sent, obs_x, obs_y, x_start):
    blocks, members, fields, tiles, rows, _ = sent.shape
    count = obs_x.shape[0]
    col_block = tiles * LANES
    local_x = obs_x - x_start
    inside = (local_x >= 0) & (local_x < rows)
    safe_x = jnp.where(inside, local_x, 0)
    block = obs_y // col_block
    tile = (obs_y % col_block) // LANES
    base = (block * members * tiles + tile) * rows + safe_x
    place = jnp.arange(count, dtype=jnp.int32) % LANES
    shift = (place - obs_y % LANES) % LANES
    place = jnp.where(inside, place, -1)
    return pl.pallas_call(
        pick_kernel,
        grid=(1,),
        in_specs=smem(3)
        + [pl.BlockSpec((blocks, members, 1, tiles, rows, LANES), lambda i: (0,) * 6)],
        out_specs=pl.BlockSpec((members, count), lambda i: (0, 0)),
        out_shape=jax.ShapeDtypeStruct((members, count), jnp.float32),
        compiler_params=params(),
        name="pick",
    )(base, shift, place, sent)


def pick_radius(cutoff, obs_x, obs_y, x_start, y_start):
    rows, columns = cutoff.shape
    radius_sq = jnp.square(cutoff.astype(jnp.float32))
    row_is = (obs_x[:, None] - x_start == jnp.arange(rows)[None, :]).astype(jnp.float32)
    col_is = obs_y[:, None] - y_start == jnp.arange(columns)[None, :]
    by_row = jnp.dot(row_is, radius_sq, precision=highest)
    return jnp.sum(jnp.where(col_is, by_row, 0.0), 1)


def exchange(value, axis, distance):
    size = lax.axis_size(axis)
    return lax.ppermute(value, axis, [(i, i ^ distance) for i in range(size)])


def sum_over(value, axis):
    distance = 1
    while distance < lax.axis_size(axis):
        value = value + exchange(value, axis, distance)
        distance *= 2
    return value


def gather_over(value, axis):
    here = lax.axis_index(axis)
    distance = 1
    while distance < lax.axis_size(axis):
        other = exchange(value, axis, distance)
        lower = (here & distance) == 0
        value = jnp.where(
            lower, jnp.concatenate([value, other], 0), jnp.concatenate([other, value], 0)
        )
        distance *= 2
    return value


def apart_sq(a, b, size):
    gap = jnp.abs(a - b)
    gap = jnp.minimum(gap, size - gap)
    return gap * gap


def chain_kernel(
    sizes,
    start_ref,
    heights_ref,
    radius_ref,
    row_ref,
    col_ref,
    value_ref,
    variance_ref,
    cutoff_ref,
    lhs1_ref,
    lhs2_ref,
    place_ref,
    count_ref,
):
    size_x, size_y = sizes
    members = heights_ref.shape[0]
    batches, count = value_ref.shape
    rows, columns = cutoff_ref.shape
    x_start = start_ref[0]
    y_start = start_ref[1]
    reach = jnp.max(cutoff_ref[...])
    reach_sq = reach * reach

    heights = heights_ref[...]
    before = (
        lax.broadcasted_iota(jnp.int32, (count, count), 0)
        <= lax.broadcasted_iota(jnp.int32, (count, count), 1)
    ).astype(jnp.bfloat16)
    slot = lax.broadcasted_iota(jnp.int32, (count, count), 0)
    member_row = lax.broadcasted_iota(jnp.int32, (members, LANES + count), 0)
    eye = (
        lax.broadcasted_iota(jnp.int32, (members, members), 0)
        == lax.broadcasted_iota(jnp.int32, (members, members), 1)
    ).astype(jnp.float32)

    for b in range(batches):
        here = slice(b * count, (b + 1) * count)
        prior = heights[:, here]
        mean = jnp.mean(prior, 0, keepdims=True)
        anom = prior - mean
        precision = 1.0 / variance_ref[b : b + 1, :]
        innov = value_ref[b : b + 1, :] - mean
        scaled = anom * precision
        inner = eye + lax.dot_general(
            scaled, anom, NT, precision=highest, preferred_element_type=jnp.float32
        ) / (members - 1)
        proj = jnp.sum(scaled * innov, 1, keepdims=True)
        system = jnp.concatenate(
            [inner, proj, jnp.zeros((members, LANES - members - 1), jnp.float32), scaled], 1
        )
        for k in range(members):
            pivot_row = system[k : k + 1, :] / system[k : k + 1, k : k + 1]
            system = jnp.where(
                member_row == k, pivot_row, system - system[:, k : k + 1] * pivot_row
            )
        solved_proj = system[:, members : members + 1]
        solved_anom = system[:, LANES:]
        solved_innov = precision * (
            innov - jnp.sum(anom * solved_proj, 0, keepdims=True) / (members - 1)
        )
        mix = (solved_innov - 0.5 * solved_anom) / (members - 1)

        obs_x = row_ref[0:1, here]
        obs_y = row_ref[1:2, here]
        off_x = jnp.where(obs_x >= x_start, obs_x - x_start, obs_x - x_start + size_x)
        off_y = jnp.where(obs_y >= y_start, obs_y - y_start, obs_y - y_start + size_y)
        gap_x = jnp.where(off_x < rows, 0, jnp.minimum(off_x - (rows - 1), size_x - off_x))
        gap_y = jnp.where(off_y < columns, 0, jnp.minimum(off_y - (columns - 1), size_y - off_y))
        reaches = gap_x * gap_x + gap_y * gap_y < reach_sq
        flags = jnp.broadcast_to(reaches.astype(jnp.float32), (8, count))
        ranks = jnp.dot(
            flags.astype(jnp.bfloat16), before, preferred_element_type=jnp.float32
        )
        rank = jnp.where(reaches, ranks[0:1, :].astype(jnp.int32) - 1, -1)
        chosen = (slot == rank).astype(jnp.float32)
        count_ref[b] = jnp.sum(flags[0:1, :]).astype(jnp.int32)

        near_anom = lax.dot_general(
            chosen, anom, NT, precision=highest, preferred_element_type=jnp.float32
        )
        high, low = split_bf16(near_anom)
        lhs1_ref[b] = jnp.concatenate([high, high, low], 1)
        near_mix = lax.dot_general(
            mix, chosen, NT, precision=highest, preferred_element_type=jnp.float32
        )
        high, low = split_bf16(near_mix)
        for k in range(count // OBS_BLOCK):
            part = slice(k * OBS_BLOCK, (k + 1) * OBS_BLOCK)
            lhs2_ref[b, k] = jnp.concatenate([high[:, part], high[:, part], low[:, part]], 1)
        where = jnp.concatenate(
            [
                jnp.broadcast_to(obs_x, (LANES, count)),
                jnp.broadcast_to(obs_y, (LANES, count)),
            ],
            0,
        ).astype(jnp.float32)
        place_ref[b] = lax.dot_general(
            chosen, where, NT, precision=highest, preferred_element_type=jnp.float32
        )

        if b + 1 < batches:
            later = slice((b + 1) * count, batches * count)
            ahead = heights[:, later]
            ahead_anom = ahead - jnp.mean(ahead, 0, keepdims=True)
            cross = lax.dot_general(
                anom, ahead_anom, TN, precision=highest, preferred_element_type=jnp.float32
            )
            dist_sq = apart_sq(col_ref[:, b : b + 1], row_ref[0:1, later], size_x) + apart_sq(
                col_ref[:, batches + b : batches + b + 1], row_ref[1:2, later], size_y
            )
            ratio = dist_sq.astype(jnp.float32) / radius_ref[:, later]
            gain = cross * jnp.square(jnp.maximum(1.0 - ratio, 0.0))
            ahead = ahead + jnp.dot(
                mix, gain, precision=highest, preferred_element_type=jnp.float32
            )
            heights = jnp.concatenate([heights[:, : (b + 1) * count], ahead], 1)


def chain(start, heights, radius_sq, obs_x, obs_y, values, variance, cutoff, sizes):
    members = heights.shape[0]
    batches, count = values.shape
    row_form = jnp.stack([obs_x.reshape(-1), obs_y.reshape(-1)], 0)
    col_form = jnp.concatenate([obs_x, obs_y], 0).T
    return pl.pallas_call(
        functools.partial(chain_kernel, sizes),
        in_specs=smem() + vmem(7),
        out_specs=vmem(3) + smem(),
        out_shape=[
            jax.ShapeDtypeStruct((batches, count, 3 * members), jnp.bfloat16),
            jax.ShapeDtypeStruct(
                (batches, count // OBS_BLOCK, members, 3 * OBS_BLOCK), jnp.bfloat16
            ),
            jax.ShapeDtypeStruct((batches, count, 2 * LANES), jnp.float32),
            jax.ShapeDtypeStruct((batches,), jnp.int32),
        ],
        compiler_params=params(),
        name="chain",
    )(start, heights, radius_sq, row_form, col_form, values, variance, cutoff)


def update_kernel(
    sizes,
    start_ref,
    count_ref,
    state_ref,
    cutoff_ref,
    lhs1_ref,
    lhs2_ref,
    place_ref,
    out_ref,
    members_ref,
    rhs_ref,
    back_ref,
):
    size_x, size_y = float(sizes[0]), float(sizes[1])
    members, fields, tiles, rows, _ = state_ref.shape
    batches = lhs1_ref.shape[0]
    cells = rows * LANES
    flat = state_ref.reshape(members * fields * tiles * rows, LANES)
    flat_back = back_ref.reshape(members * fields * rows, LANES)
    row0 = (start_ref[0] + pl.program_id(0) * rows).astype(jnp.float32)
    lane = lax.broadcasted_iota(jnp.int32, (1, LANES), 1).astype(jnp.float32)

    def contribution(b, k, t):
        first = k * OBS_BLOCK
        if not isinstance(k, int):
            first = pl.multiple_of(first, OBS_BLOCK)
        part = pl.ds(first, OBS_BLOCK)
        obs_x = place_ref[b, part, :LANES]
        obs_y = place_ref[b, part, LANES:]
        col0 = (start_ref[1] + t * LANES).astype(jnp.float32)
        dist_y = apart_sq(obs_y, lane + col0, size_y)
        weights = []
        for r in range(rows):
            radius = cutoff_ref[r : r + 1, t * LANES : (t + 1) * LANES].astype(jnp.float32)
            ratio = (dist_y + apart_sq(obs_x, row0 + r, size_x)) * (1.0 / (radius * radius))
            weights.append(jnp.square(jnp.maximum(1.0 - ratio, 0.0)))
        weights = jnp.concatenate(weights, 1)
        cross = jnp.dot(
            lhs1_ref[b, part, :], rhs_ref[...], preferred_element_type=jnp.float32
        )
        gain = cross * jnp.concatenate([weights] * fields, 1)
        high, low = split_bf16(gain)
        return jnp.dot(
            lhs2_ref[b, k],
            jnp.concatenate([high, low, high], 0),
            preferred_element_type=jnp.float32,
        )

    for t in range(tiles):
        for f in range(fields):
            for r in range(rows):
                place = f * cells + r * LANES
                members_ref[:, place : place + LANES] = flat[
                    pl.ds((f * tiles + t) * rows + r, members, stride=fields * tiles * rows), :
                ]
        for b in range(batches):
            state = members_ref[...]
            high, low = split_bf16(state - jnp.mean(state, 0, keepdims=True))
            rhs_ref[...] = jnp.concatenate([high, low, high], 0)
            members_ref[...] = state + contribution(b, 0, t)

            def more(k, _):
                members_ref[...] += contribution(b, k, t)
                return 0

            blocks = (count_ref[b] + (OBS_BLOCK - 1)) // OBS_BLOCK
            lax.fori_loop(1, blocks, more, 0)
        for f in range(fields):
            for r in range(rows):
                place = f * cells + r * LANES
                flat_back[pl.ds(f * rows + r, members, stride=fields * rows), :] = members_ref[
                    :, place : place + LANES
                ]
        out_ref[:, :, :, t * LANES : (t + 1) * LANES] = back_ref[...]


def update(start, counts, state, cutoff, lhs1, lhs2, place, sizes):
    members, fields, tiles, rows, _ = state.shape
    columns = tiles * LANES
    width = fields * ROW_TILE * LANES

    def whole(array):
        return pl.BlockSpec(array.shape, lambda i: (0,) * array.ndim)

    return pl.pallas_call(
        functools.partial(update_kernel, sizes),
        grid=(rows // ROW_TILE,),
        in_specs=smem(2)
        + [
            pl.BlockSpec(
                (members, fields, tiles, ROW_TILE, LANES), lambda i: (0, 0, 0, i, 0)
            ),
            pl.BlockSpec((ROW_TILE, columns), lambda i: (i, 0)),
            whole(lhs1),
            whole(lhs2),
            whole(place),
        ],
        out_specs=pl.BlockSpec(
            (members, fields, ROW_TILE, columns), lambda i: (0, 0, i, 0)
        ),
        out_shape=jax.ShapeDtypeStruct((members, fields, rows, columns), jnp.float32),
        scratch_shapes=[
            pltpu.VMEM((members, width), jnp.float32),
            pltpu.VMEM((3 * members, width), jnp.bfloat16),
            pltpu.VMEM((members, fields, ROW_TILE, LANES), jnp.float32),
        ],
        compiler_params=params(),
        name="update",
    )(start, counts, state, cutoff, lhs1, lhs2, place)


def row_halos(block, axis):
    size = lax.axis_size(axis)
    onward = [(i, (i + 1) % size) for i in range(size)]
    backward = [(j, i) for i, j in onward]
    rows = block.shape[-2]
    last = lax.slice_in_dim(block, rows - HALO, rows, axis=block.ndim - 2)
    leading = lax.slice_in_dim(block, 0, HALO, axis=block.ndim - 2)
    return lax.ppermute(last, axis, onward), lax.ppermute(leading, axis, backward)


def local(ensemble, sea_depth, cutoff, obs_index, obs_value, obs_var):
    blocks = lax.axis_size("mem")
    members, fields, rows, size_y = ensemble.shape
    col_block = size_y // blocks
    size_x = rows * lax.axis_size("sub")
    sizes = (size_x, size_y)
    x_start = lax.axis_index("sub") * rows
    y_start = lax.axis_index("mem") * col_block
    start = jnp.stack([x_start, y_start]).astype(jnp.int32)
    obs_x = obs_index // size_y
    obs_y = obs_index % size_y
    flat_x = obs_x.reshape(-1)
    flat_y = obs_y.reshape(-1)

    up, down = row_halos(ensemble, "sub")
    depth_up, depth_down = row_halos(sea_depth, "sub")
    depth = jnp.concatenate([depth_up, sea_depth, depth_down], 0)
    sent = forecast(ensemble, up, down, depth, blocks)

    radius_part = pick_radius(cutoff, flat_x, flat_y, x_start, y_start)
    heights_part = pick_heights(sent, flat_x, flat_y, x_start)
    part = jnp.concatenate([heights_part, radius_part[None, :]], 0)
    part = jnp.pad(part, ((0, -part.shape[0] % 8), (0, 0)))
    every = gather_over(sum_over(part, "sub")[None], "mem")
    heights = every[:, :members].reshape(blocks * members, -1)
    radius_sq = jnp.sum(every[:, members], 0)[None, :]

    received = lax.all_to_all(sent, "mem", split_axis=0, concat_axis=0, tiled=True)
    state = received.reshape((blocks * members,) + received.shape[2:])
    lhs1, lhs2, place, counts = chain(
        start, heights, radius_sq, obs_x, obs_y, obs_value, obs_var, cutoff, sizes
    )
    return update(start, counts, state, cutoff, lhs1, lhs2, place, sizes)


def solution(mesh):
    return jax.shard_map(
        local,
        mesh=mesh,
        in_specs=(P("mem", None, "sub", None), P("sub", None), P("sub", "mem"), P(), P(), P()),
        out_specs=P(None, None, "sub", "mem"),
        check_vma=False,
    )
```

time: 991 us -> 167 us (0.17); the launches traced: 978 us -> 166 us
  other arithmetic: 306 us -> 2.22 us
  local copies, waits for them, and re-layouts: 244 us -> 9.49 us
  matrix products: 224 us -> 0.81 us
  blocking collectives: 163 us -> 0 us
  Pallas kernels: 0 us -> 58.2 us
  waiting for transfers between devices: 21.3 us -> 76.2 us
    another operation x38 -> x2, other arithmetic: 241 us -> 0.09 us  [the longest x1 0.07 us: local(): start = jnp.stack([x_start, y_start]).astype(jnp.int32)]
    dot_general x16 -> x1, matrix products: 200 us -> 0.81 us  [pick_radius(): by_row = jnp.dot(row_is, radius_sq, precision=highest)]
    psum x4 -> x0, blocking collectives: 163 us -> none  [local(): prior_obs = lax.psum(local_part, ('mem', 'sub'))]
    mul x8 -> x0, local copies, waits for them, and re-layouts: 143 us -> none  [update_state(): cross_cov.reshape(obs_count, 3, cell_count) * loc_weight[:, None, :]]
    pallas_call x0 -> x4, Pallas kernels: none -> 58.2 us  [the longest x1 21.7 us: update(): pl.pallas_call(functools.partial(update_kernel, sizes), grid=(rows // ROW...]
    ppermute x16 -> x9, waiting for transfers between devices: 21.3 us -> 76.2 us  [the longest x5 57.8 us: exchange(): return lax.ppermute(value, axis, [(i, i ^ distance) for i in range(size)])]
    another operation x38 -> x0, local copies, waits for them, and re-layouts: 38.3 us -> none  [the longest x29 26.8 us: analysis_weights(): solved = jax.scipy.linalg.cho_solve((factor, True), right_side)]
    unnamed x70 -> x28, local copies, waits for them, and re-layouts: 35.9 us -> 6.24 us
  transfers between devices with their start and end apart: 17 -> 10, of which waited for: 14 -> 6; matrix products, arithmetic and copies ran while one was open for 18% -> 3% of each run, Pallas kernels for 0% -> 15%
where the time goes in v1:
time: 167 us; the launch traced here: 166 us
  waiting for transfers between devices  76.2 us (46%)
  Pallas kernels  58.2 us (35%)
  starting transfers between devices  19.1 us (11%)
  local copies, waits for them, and re-layouts  9.49 us (6%)
  other arithmetic  2.22 us (1%)
    ppermute x5, waiting for transfers between devices, exchange(): return lax.ppermute(value, axis, [(i, i ^ distance) for i in range(size)])  57.8 us
    pallas_call x1, Pallas kernels, update(): pl.pallas_call(functools.partial(update_kernel, sizes), grid=(rows // ROW...  21.7 us
    ppermute x2, waiting for transfers between devices, row_halos(): lax.ppermute(last, axis, onward)  18.5 us
    pallas_call x1, Pallas kernels, chain(): pl.pallas_call(functools.partial(chain_kernel, sizes), in_specs=smem() +...  17 us
    pallas_call x1, Pallas kernels, forecast(): pl.pallas_call(forecast_kernel, grid=(members,), in_specs=[pl.BlockSpec((...  11.5 us
    ppermute x5, starting transfers between devices, exchange(): return lax.ppermute(value, axis, [(i, i ^ distance) for i in range(size)])  8.86 us
    pallas_call x1, Pallas kernels, pick_heights(): pl.pallas_call(pick_kernel, grid=(1,), in_specs=smem(3) + [pl.BlockSpec((...  7.96 us
    unnamed x28, local copies, waits for them, and re-layouts  6.24 us
  transfers between devices with their start and end apart: 10, of which 6 were waited for; matrix products, arithmetic and copies ran while one was open for 3% of the time, Pallas kernels for 15%

profile of v1, /device:TPU:0, one launch (start us, length us, event | category | flops | bytes accessed | tf_op | source)
XLA Modules:
  0.0 166.3 jit_solution(8169647578153839548)
XLA Ops:
  0.0 0.0 copy-start.10
  0.0 1.5 fusion.20
  1.5 2.5 %collective-permute-start.1 = (f32[4,3,8,2048]{3,2,1,0:T(8,128)S(1)}, f32[4,3,8,2048]{3,2,1,0:T(8,128)S(1)}, u32[]{:S(2)}, u32[]{:S(2)}) collective-permute-start(f32[4,3,8,2048]{3,2,1,0:T(8,128)S(1)} %get-tuple-element.15), channel_id=1, source_target_pairs={{1,0},{2,1},{3,2},{0,3},{5,4},{6,5},{7,6},{4,7},{9,8},{10,9},{11,1... | collective-permute-start | bytes 2359304 | tf_op jit(solution)/shard_map/ppermute | solution.py:443
  4.0 0.0 collective-permute-start
  4.0 0.0 copy-done.10
  4.0 0.8 collective-permute-start.2
  4.8 1.1 collective-permute-start.3
  5.9 18.5 %collective-permute-done.2 = f32[8,2048]{1,0:T(8,128)S(1)} collective-permute-done((f32[8,2048]{1,0:T(8,128)S(1)}, f32[8,2048]{1,0:T(8,128)S(1)}, u32[]{:S(2)}, u32[]{:S(2)}) %collective-permute-start.2) | collective-permute-done | bytes 65568 | tf_op jit(solution)/shard_map/ppermute | solution.py:443
  24.3 0.0 collective-permute-done.3
  24.4 0.0 collective-permute-done.1.down_ref
  24.4 0.0 collective-permute-done.up_ref
  24.4 11.5 %forecast.1.height_ref = f32[8,4,3,2,32,128]{5,4,3,2,1,0:T(8,128)} custom-call(f32[4,3,32,2048]{3,2,1,0:T(8,128)} %ens_ref.1, f32[4,3,8,2048]{3,2,1,0:T(8,128)S(1)} %collective-permute-done.up_ref, f32[4,3,8,2048]{3,2,1,0:T(8,128)S(1)} %collective-permute-done.1.down_ref, f32[48,2048]{1,0:T(8,128)S(1)} %pad_maximum_fusion.depth_ref), custom_call_target="tpu_custom_call" | custom-call | tf_op jit(solution)/shard_map/forecast/pallas_call | solution.py:72
  35.9 0.0 copy-start.11
  35.9 0.0 copy-start.6
  35.9 5.9 %all-to-all-start = ((f32[8,4,3,2,32,128]{5,4,3,2,1,0:T(8,128)}), f32[8,4,3,2,32,128]{5,4,3,2,1,0:T(8,128)S(1)}, u32[]{:S(2)}, u32[]{:S(2)}) async-start(f32[8,4,3,2,32,128]{5,4,3,2,1,0:T(8,128)} %forecast.1.height_ref), calls=%async_computation | async-start | bytes 6291456 | tf_op jit(solution)/shard_map/all_to_all | solution.py:473
  41.9 0.0 copy-done.11
  41.9 0.0 copy-start.7
  41.9 0.0 copy-start.8
  42.0 0.0 copy-done.6
  42.0 0.8 fusion
  42.8 8.0 %pick.1 = f32[4,1024]{1,0:T(4,128)S(1)} custom-call(s32[1024]{0:T(1024)S(1)} %get-tuple-element.20.base_ref, s32[1024]{0:T(1024)S(1)} %get-tuple-element.21.lane_ref, s32[1024]{0:T(1024)S(1)} %get-tuple-element.19.place_ref, f32[8,4,3,2,32,128]{5,4,3,2,1,0:T(8,128)} %forecast.1.height_ref), custom_call_target="tpu_custom_call" | custom-call | tf_op jit(solution)/shard_map/pick/pallas_call | solution.py:130
  50.8 0.1 collective-permute-start.4
  50.9 1.2 collective-permute-done.4
  52.1 1.5 collective-permute-start.5
  53.6 2.5 %collective-permute-done.5 = f32[8,1024]{1,0:T(8,128)S(1)} collective-permute-done((f32[8,1024]{1,0:T(8,128)S(1)}, f32[8,1024]{1,0:T(8,128)S(1)}, u32[]{:S(2)}, u32[]{:S(2)}) %collective-permute-start.5) | collective-permute-done | bytes 32800 | tf_op jit(solution)/shard_map/ppermute | solution.py:153
  56.1 2.0 %collective-permute-start.6 = (f32[1,8,1024]{2,1,0:T(8,128)S(1)}, f32[1,8,1024]{2,1,0:T(8,128)S(1)}, u32[]{:S(2)}, u32[]{:S(2)}) collective-permute-start(f32[1,8,1024]{2,1,0:T(8,128)S(1)} %add_bitcast_fusion), channel_id=1, source_target_pairs={{0,4},{4,0},{8,12},{12,8},{16,20},{20,16},{24,28},{28,24},{1,5},{5... | collective-permute-start | bytes 98312 | tf_op jit(solution)/shard_map/ppermute | solution.py:153
  58.1 9.8 %collective-permute-done.6 = f32[1,8,1024]{2,1,0:T(8,128)S(1)} collective-permute-done((f32[1,8,1024]{2,1,0:T(8,128)S(1)}, f32[1,8,1024]{2,1,0:T(8,128)S(1)}, u32[]{:S(2)}, u32[]{:S(2)}) %collective-permute-start.6) | collective-permute-done | bytes 32800 | tf_op jit(solution)/shard_map/ppermute | solution.py:153
  67.9 1.3 collective-permute-start.7
  69.2 25.0 %collective-permute-done.7 = f32[2,8,1024]{2,1,0:T(8,128)S(1)} collective-permute-done((f32[2,8,1024]{2,1,0:T(8,128)S(1)}, f32[2,8,1024]{2,1,0:T(8,128)S(1)}, u32[]{:S(2)}, u32[]{:S(2)}) %collective-permute-start.7) | collective-permute-done | bytes 65568 | tf_op jit(solution)/shard_map/ppermute | solution.py:153
  94.2 4.0 %collective-permute-start.8 = (f32[4,8,1024]{2,1,0:T(8,128)S(1)}, f32[4,8,1024]{2,1,0:T(8,128)}, u32[]{:S(2)}, u32[]{:S(2)}) collective-permute-start(f32[4,8,1024]{2,1,0:T(8,128)S(1)} %maximum_select_fusion.1), channel_id=1, source_target_pairs={{0,16},{4,20},{8,24},{12,28},{16,0},{20,4},{24,8},{28,12},{1,17},{... | collective-permute-start | bytes 393224 | tf_op jit(solution)/shard_map/ppermute | solution.py:153
  98.2 0.1 pad_add_fusion.2.start_ref
  98.3 0.1 copy.25
  98.4 19.3 %collective-permute-done.8 = f32[4,8,1024]{2,1,0:T(8,128)} collective-permute-done((f32[4,8,1024]{2,1,0:T(8,128)S(1)}, f32[4,8,1024]{2,1,0:T(8,128)}, u32[]{:S(2)}, u32[]{:S(2)}) %collective-permute-start.8) | collective-permute-done | bytes 131104 | tf_op jit(solution)/shard_map/ppermute | solution.py:153
  117.7 1.0 maximum_select_fusion
  118.7 0.0 copy-start.9
  118.7 0.7 copy-done.9
  119.4 0.7 slice.24
  120.1 0.9 reshape.27.heights_ref
  121.0 1.0 slice_reduce_fusion
  122.0 0.0 copy-done.7
  122.1 0.0 copy-done.8
  122.1 17.0 %chain.1 = (bf16[4,256,96]{2,1,0:T(8,128)(2,1)S(1)}, bf16[4,4,32,192]{3,2,1,0:T(8,128)(2,1)S(1)}, f32[4,256,256]{2,1,0:T(8,128)S(1)}, s32[4]{0:T(128)S(1)}) custom-call(s32[2]{0:T(128)S(1)} %pad_add_fusion.2.start_ref, f32[32,1024]{1,0:T(8,128)S(1)} %reshape.27.heights_ref, f32[1,1024]{1,0:T(1,128)S(1)} %bitcast.21, s32[2,1024]{1,0:T(2,128)S(1)} %pad_add_fusion.row_ref, ...), custom_call_target="tpu_custom_call" | custom-call | tf_op jit(solution)/shard_map/chain/pallas_call | solution.py:307
  139.1 0.0 copy-start
  139.1 1.0 copy-done
  140.1 0.0 copy-start.2
  140.1 0.7 copy-done.2
  140.8 0.0 copy-start.4
  140.8 0.7 copy-done.4
  141.5 0.0 all-to-all-done
  141.5 0.0 copy-start.1
  141.5 1.2 copy-done.1
  142.7 0.0 copy-start.3
  142.7 0.9 copy-done.3
  143.7 0.0 copy-start.5
  143.7 0.9 copy-done.5
  144.6 21.7 %update.1 = f32[32,3,32,256]{3,2,1,0:T(8,128)} custom-call(s32[2]{0:T(128)S(1)} %pad_add_fusion.2.start_ref, s32[4]{0:T(128)S(1)} %get-tuple-element.9.count_ref, f32[32,3,2,32,128]{4,3,2,1,0:T(8,128)S(1)} %bitcast.19, s32[32,256]{1,0:T(8,128)S(1)} %copy-done.6, bf16[4,256,96]{2,1,0:T(8,128)(2,1)S(1)} %copy-done.3, bf16[4,4,32,192]{3,2,1,0:T(8,128)(2,1)S(1)} %copy-done.5, ...), custom_call_target="tpu_custom_call" | custom-call | tf_op jit(solution)/shard_map/update/pallas_call | solution.py:409
  (15 shorter events, 0.2 us)
Async XLA Ops:
  0.0 4.0 %copy-start.10 = (f32[32,2048]{1,0:T(8,128)S(1)}, f32[32,2048]{1,0:T(8,128)}, u32[]{:S(2)}) copy-start(f32[32,2048]{1,0:T(8,128)} %param.7) | copy-start | bytes 786436
  1.5 22.9 %collective-permute-start.1 = (f32[4,3,8,2048]{3,2,1,0:T(8,128)S(1)}, f32[4,3,8,2048]{3,2,1,0:T(8,128)S(1)}, u32[]{:S(2)}, u32[]{:S(2)}) collective-permute-start(f32[4,3,8,2048]{3,2,1,0:T(8,128)S(1)} %get-tuple-element.15), channel_id=1, source_target_pairs={{1,0},{2,1},{3,2},{0,3},{5,4},{6,5},{7,6},{4,7},{9,8},{10,9},{11,1... | collective-permute-start | bytes 2359304 | tf_op jit(solution)/shard_map/ppermute | solution.py:443
  4.0 20.4 %collective-permute-start = (f32[4,3,8,2048]{3,2,1,0:T(8,128)S(1)}, f32[4,3,8,2048]{3,2,1,0:T(8,128)S(1)}, u32[]{:S(2)}, u32[]{:S(2)}) collective-permute-start(f32[4,3,8,2048]{3,2,1,0:T(8,128)S(1)} %get-tuple-element.16), channel_id=1, source_target_pairs={{0,1},{1,2},{2,3},{3,0},{4,5},{5,6},{6,7},{7,4},{8,9},{9,10},{10,1... | collective-permute-start | bytes 2359304 | tf_op jit(solution)/shard_map/ppermute | solution.py:443
  4.0 20.3 %collective-permute-start.2 = (f32[8,2048]{1,0:T(8,128)S(1)}, f32[8,2048]{1,0:T(8,128)S(1)}, u32[]{:S(2)}, u32[]{:S(2)}) collective-permute-start(f32[8,2048]{1,0:T(8,128)S(1)} %get-tuple-element.17), channel_id=1, source_target_pairs={{0,1},{1,2},{2,3},{3,0},{4,5},{5,6},{6,7},{7,4},{8,9},{9,10},{10,1... | collective-permute-start | bytes 196616 | tf_op jit(solution)/shard_map/ppermute | solution.py:443
  4.8 19.6 %collective-permute-start.3 = (f32[8,2048]{1,0:T(8,128)S(1)}, f32[8,2048]{1,0:T(8,128)S(1)}, u32[]{:S(2)}, u32[]{:S(2)}) collective-permute-start(f32[8,2048]{1,0:T(8,128)S(1)} %get-tuple-element.18), channel_id=1, source_target_pairs={{1,0},{2,1},{3,2},{0,3},{5,4},{6,5},{7,6},{4,7},{9,8},{10,9},{11,1... | collective-permute-start | bytes 196616 | tf_op jit(solution)/shard_map/ppermute | solution.py:443
  35.9 5.9 %copy-start.11 = (s32[4,256]{1,0:T(4,128)S(1)}, s32[4,256]{1,0:T(4,128)}, u32[]{:S(2)}) copy-start(s32[4,256]{1,0:T(4,128)} %param.9) | copy-start | bytes 12292
  35.9 6.0 %copy-start.6 = (s32[32,256]{1,0:T(8,128)S(1)}, s32[32,256]{1,0:T(8,128)}, u32[]{:S(2)}) copy-start(s32[32,256]{1,0:T(8,128)} %cutoff_ref.3) | copy-start | bytes 98308
  35.9 105.6 %all-to-all-start = ((f32[8,4,3,2,32,128]{5,4,3,2,1,0:T(8,128)}), f32[8,4,3,2,32,128]{5,4,3,2,1,0:T(8,128)S(1)}, u32[]{:S(2)}, u32[]{:S(2)}) async-start(f32[8,4,3,2,32,128]{5,4,3,2,1,0:T(8,128)} %forecast.1.height_ref), calls=%async_computation | async-start | bytes 6291456 | tf_op jit(solution)/shard_map/all_to_all | solution.py:473
  41.9 80.1 %copy-start.7 = (f32[4,256]{1,0:T(4,128)S(1)}, f32[4,256]{1,0:T(4,128)}, u32[]{:S(2)}) copy-start(f32[4,256]{1,0:T(4,128)} %value_ref.1) | copy-start | bytes 12292
  41.9 80.1 %copy-start.8 = (f32[4,256]{1,0:T(4,128)S(1)}, f32[4,256]{1,0:T(4,128)}, u32[]{:S(2)}) copy-start(f32[4,256]{1,0:T(4,128)} %variance_ref.1) | copy-start | bytes 12292
  50.8 1.3 collective-permute-start.4
  52.1 4.0 %collective-permute-start.5 = (f32[8,1024]{1,0:T(8,128)S(1)}, f32[8,1024]{1,0:T(8,128)S(1)}, u32[]{:S(2)}, u32[]{:S(2)}) collective-permute-start(f32[8,1024]{1,0:T(8,128)S(1)} %fusion.19), channel_id=1, source_target_pairs={{0,2},{1,3},{2,0},{3,1},{4,6},{5,7},{6,4},{7,5},{8,10},{9,11},{10,... | collective-permute-start | bytes 98312 | tf_op jit(solution)/shard_map/ppermute | solution.py:153
  56.1 11.8 %collective-permute-start.6 = (f32[1,8,1024]{2,1,0:T(8,128)S(1)}, f32[1,8,1024]{2,1,0:T(8,128)S(1)}, u32[]{:S(2)}, u32[]{:S(2)}) collective-permute-start(f32[1,8,1024]{2,1,0:T(8,128)S(1)} %add_bitcast_fusion), channel_id=1, source_target_pairs={{0,4},{4,0},{8,12},{12,8},{16,20},{20,16},{24,28},{28,24},{1,5},{5... | collective-permute-start | bytes 98312 | tf_op jit(solution)/shard_map/ppermute | solution.py:153
  67.9 26.3 %collective-permute-start.7 = (f32[2,8,1024]{2,1,0:T(8,128)S(1)}, f32[2,8,1024]{2,1,0:T(8,128)S(1)}, u32[]{:S(2)}, u32[]{:S(2)}) collective-permute-start(f32[2,8,1024]{2,1,0:T(8,128)S(1)} %maximum_select_fusion.2), channel_id=1, source_target_pairs={{0,8},{4,12},{8,0},{12,4},{16,24},{20,28},{24,16},{28,20},{1,9},{5... | collective-permute-start | bytes 196616 | tf_op jit(solution)/shard_map/ppermute | solution.py:153
  94.2 23.5 %collective-permute-start.8 = (f32[4,8,1024]{2,1,0:T(8,128)S(1)}, f32[4,8,1024]{2,1,0:T(8,128)}, u32[]{:S(2)}, u32[]{:S(2)}) collective-permute-start(f32[4,8,1024]{2,1,0:T(8,128)S(1)} %maximum_select_fusion.1), channel_id=1, source_target_pairs={{0,16},{4,20},{8,24},{12,28},{16,0},{20,4},{24,8},{28,12},{1,17},{... | collective-permute-start | bytes 393224 | tf_op jit(solution)/shard_map/ppermute | solution.py:153
  118.7 0.7 copy-start.9
  139.1 1.0 copy-start
  140.1 0.7 copy-start.2
  140.8 0.7 copy-start.4
  141.5 1.2 copy-start.1
  142.7 0.9 copy-start.3
  143.7 0.9 copy-start.5

commit v2 on v1

--- a/solution.py
+++ b/solution.py
@@ -45,11 +45,8 @@
     return pltpu.roll(field, length - 1, axis) - pltpu.roll(field, 1, axis)
 
 
-def forecast_kernel(ens_ref, up_ref, down_ref, depth_ref, out_ref):
-    height, east, north = [
-        jnp.concatenate([up_ref[0, f], ens_ref[0, f], down_ref[0, f]], 0) for f in range(3)
-    ]
-    depth = depth_ref[...]
+def forecast_steps(window, depth):
+    height, east, north = window
     half = 0.5 * step_size
     turn = step_size * coriolis
     for _ in range(STEPS):
@@ -57,86 +54,135 @@
         north_new = north - turn * east - half * centred(height, 1)
         height = height - half * (centred(depth * east_new, 0) + centred(depth * north_new, 1))
         east, north = east_new, north_new
-    rows = ens_ref.shape[2]
+    return height, east, north
+
+
+def send_rows(out_ref, fields, pieces):
     blocks, _, _, tiles = out_ref.shape[:4]
-    for f, field in enumerate((height, east, north)):
+    for f, field in enumerate(fields):
         for d in range(blocks):
             for t in range(tiles):
                 first = (d * tiles + t) * LANES
-                out_ref[d, 0, f, t] = field[HALO : HALO + rows, first : first + LANES]
-
-
-def forecast(ensemble, up, down, depth, blocks):
-    members, fields, rows, columns = ensemble.shape
+                for row, length, place in pieces:
+                    out_ref[d, 0, f, t, place : place + length] = field[
+                        row : row + length, first : first + LANES
+                    ]
+
+
+def inner_kernel(ens_ref, depth_ref, out_ref):
+    rows = ens_ref.shape[2]
+    done = forecast_steps([ens_ref[0, f] for f in range(3)], depth_ref[...])
+    send_rows(out_ref, done, [(HALO, rows - 2 * HALO, 0)])
+
+
+def outer_kernel(ens_ref, up_ref, down_ref, depth_ref, out_ref):
+    rows = ens_ref.shape[2]
+    window = [jnp.concatenate([up_ref[0, f], ens_ref[0, f], down_ref[0, f]], 0) for f in range(3)]
+    done = forecast_steps(window, depth_ref[...])
+    send_rows(out_ref, done, [(HALO, HALO, 0), (rows, HALO, HALO)])
+
+
+def forecast(kernel, name, out_rows, depth, blocks, *pieces):
+    members, fields, _, columns = pieces[0].shape
     tiles = columns // blocks // LANES
     return pl.pallas_call(
-        forecast_kernel,
+        kernel,
         grid=(members,),
         in_specs=[
-            pl.BlockSpec((1, fields, rows, columns), lambda m: (m, 0, 0, 0)),
-            pl.BlockSpec((1, fields, HALO, columns), lambda m: (m, 0, 0, 0)),
-            pl.BlockSpec((1, fields, HALO, columns), lambda m: (m, 0, 0, 0)),
-            pl.BlockSpec((rows + 2 * HALO, columns), lambda m: (0, 0)),
-        ],
+            pl.BlockSpec((1,) + piece.shape[1:], lambda m: (m, 0, 0, 0)) for piece in pieces
+        ]
+        + [pl.BlockSpec(depth.shape, lambda m: (0, 0))],
         out_specs=pl.BlockSpec(
-            (blocks, 1, fields, tiles, rows, LANES), lambda m: (0, m, 0, 0, 0, 0)
+            (blocks, 1, fields, tiles, out_rows, LANES), lambda m: (0, m, 0, 0, 0, 0)
         ),
         out_shape=jax.ShapeDtypeStruct(
-            (blocks, members, fields, tiles, rows, LANES), jnp.float32
+            (blocks, members, fields, tiles, out_rows, LANES), jnp.float32
         ),
         compiler_params=params(),
-        name="forecast",
-    )(ensemble, up, down, depth)
-
-
-def pick_kernel(base_ref, lane_ref, place_ref, height_ref, out_ref):
+        name=name,
+    )(*pieces, depth)
+
+
+def list_kernel(shape, start_ref, x_ref, y_ref, inner_ref, outer_ref, count_ref):
+    members, tiles, rows = shape
+    x_start = start_ref[0]
+    col_block = tiles * LANES
+    inner_rows = rows - 2 * HALO
+    outer_rows = 2 * HALO
+
+    def one(o, counts):
+        n_inner, n_outer = counts
+        x = x_ref[o] - x_start
+        y = y_ref[o]
+        block = y // col_block
+        tile = (y % col_block) // LANES
+        lane = y % LANES
+        is_inner = (x >= HALO) & (x < rows - HALO)
+        is_outer = (x >= 0) & (x < rows) & jnp.logical_not(is_inner)
+        stack = block * members * tiles + tile
+        outer_x = jnp.where(x < HALO, x, x - inner_rows)
+        inner_ref[0, n_inner] = o
+        inner_ref[1, n_inner] = stack * inner_rows + x - HALO
+        inner_ref[2, n_inner] = lane
+        outer_ref[0, n_outer] = o
+        outer_ref[1, n_outer] = stack * outer_rows + outer_x
+        outer_ref[2, n_outer] = lane
+        return n_inner + is_inner.astype(jnp.int32), n_outer + is_outer.astype(jnp.int32)
+
+    zero = jnp.int32(0)
+    n_inner, n_outer = lax.fori_loop(0, x_ref.shape[0], one, (zero, zero))
+    count_ref[0] = n_inner
+    count_ref[1] = n_outer
+
+
+def list_observations(shape, start, flat_x, flat_y):
+    count = flat_x.shape[0]
+    return pl.pallas_call(
+        functools.partial(list_kernel, shape),
+        in_specs=smem(3),
+        out_specs=smem(3),
+        out_shape=[
+            jax.ShapeDtypeStruct((3, count), jnp.int32),
+            jax.ShapeDtypeStruct((3, count), jnp.int32),
+            jax.ShapeDtypeStruct((2,), jnp.int32),
+        ],
+        name="list",
+    )(start, flat_x, flat_y)
+
+
+def pick_kernel(which, list_ref, count_ref, height_ref, start_ref, out_ref):
     blocks, members, _, tiles, rows, _ = height_ref.shape
     flat = height_ref.reshape(blocks * members * tiles * rows, LANES)
     lanes = lax.broadcasted_iota(jnp.int32, (members, LANES), 1)
-    unroll = 16
-
-    def group(g, _):
-        def some(i, acc):
-            for j in range(unroll):
-                k = i * unroll + j
-                o = g * LANES + k
-                row = flat[pl.ds(base_ref[o], members, stride=tiles * rows), :]
-                row = pltpu.roll(row, lane_ref[o], 1)
-                acc = jnp.where(lanes == place_ref[o], row, acc)
-            return acc
-
-        acc = lax.fori_loop(
-            0, LANES // unroll, some, jnp.zeros((members, LANES), jnp.float32)
-        )
-        out_ref[:, pl.ds(pl.multiple_of(g * LANES, LANES), LANES)] = acc
+    out_ref[...] = start_ref[...]
+
+    def one(i, _):
+        o = list_ref[0, i]
+        place = o % LANES
+        row = flat[pl.ds(list_ref[1, i], members, stride=tiles * rows), :]
+        row = pltpu.roll(row, (place - list_ref[2, i]) % LANES, 1)
+        group = pl.ds(pl.multiple_of(o - place, LANES), LANES)
+        out_ref[:members, group] = jnp.where(lanes == place, row, out_ref[:members, group])
         return 0
 
-    lax.fori_loop(0, out_ref.shape[1] // LANES, group, 0)
-
-
-def pick_heights(sent, obs_x, obs_y, x_start):
+    lax.fori_loop(0, count_ref[which], one, 0)
+
+
+def pick_heights(which, lists, counts, sent, begin):
     blocks, members, fields, tiles, rows, _ = sent.shape
-    count = obs_x.shape[0]
-    col_block = tiles * LANES
-    local_x = obs_x - x_start
-    inside = (local_x >= 0) & (local_x < rows)
-    safe_x = jnp.where(inside, local_x, 0)
-    block = obs_y // col_block
-    tile = (obs_y % col_block) // LANES
-    base = (block * members * tiles + tile) * rows + safe_x
-    place = jnp.arange(count, dtype=jnp.int32) % LANES
-    shift = (place - obs_y % LANES) % LANES
-    place = jnp.where(inside, place, -1)
     return pl.pallas_call(
-        pick_kernel,
+        functools.partial(pick_kernel, which),
         grid=(1,),
-        in_specs=smem(3)
-        + [pl.BlockSpec((blocks, members, 1, tiles, rows, LANES), lambda i: (0,) * 6)],
-        out_specs=pl.BlockSpec((members, count), lambda i: (0, 0)),
-        out_shape=jax.ShapeDtypeStruct((members, count), jnp.float32),
+        in_specs=smem(2)
+        + [
+            pl.BlockSpec((blocks, members, 1, tiles, rows, LANES), lambda i: (0,) * 6),
+            pl.BlockSpec(begin.shape, lambda i: (0, 0)),
+        ],
+        out_specs=pl.BlockSpec(begin.shape, lambda i: (0, 0)),
+        out_shape=jax.ShapeDtypeStruct(begin.shape, jnp.float32),
         compiler_params=params(),
         name="pick",
-    )(base, shift, place, sent)
+    )(lists, counts, sent, begin)
 
 
 def pick_radius(cutoff, obs_x, obs_y, x_start, y_start):
@@ -323,6 +369,9 @@
 
 def update_kernel(
     sizes,
+    first_tile,
+    tile_stride,
+    continues,
     start_ref,
     count_ref,
     state_ref,
@@ -330,18 +379,17 @@
     lhs1_ref,
     lhs2_ref,
     place_ref,
-    out_ref,
-    members_ref,
-    rhs_ref,
-    back_ref,
+    *rest,
 ):
+    out_ref, members_ref, rhs_ref, back_ref = rest[1:] if continues else rest
     size_x, size_y = float(sizes[0]), float(sizes[1])
     members, fields, tiles, rows, _ = state_ref.shape
     batches = lhs1_ref.shape[0]
     cells = rows * LANES
     flat = state_ref.reshape(members * fields * tiles * rows, LANES)
     flat_back = back_ref.reshape(members * fields * rows, LANES)
-    row0 = (start_ref[0] + pl.program_id(0) * rows).astype(jnp.float32)
+    tile_id = first_tile + tile_stride * pl.program_id(0)
+    row0 = (start_ref[0] + tile_id * rows).astype(jnp.float32)
     lane = lax.broadcasted_iota(jnp.int32, (1, LANES), 1).astype(jnp.float32)
 
     def contribution(b, k, t):
@@ -398,29 +446,35 @@
         out_ref[:, :, :, t * LANES : (t + 1) * LANES] = back_ref[...]
 
 
-def update(start, counts, state, cutoff, lhs1, lhs2, place, sizes):
-    members, fields, tiles, rows, _ = state.shape
+def update(start, counts, state, cutoff, lhs1, lhs2, place, sizes, row_tiles, begun=None):
+    members, fields, tiles, _, _ = state.shape
+    rows = cutoff.shape[0]
     columns = tiles * LANES
     width = fields * ROW_TILE * LANES
+    first, stride = row_tiles[0], row_tiles[1] - row_tiles[0]
 
     def whole(array):
         return pl.BlockSpec(array.shape, lambda i: (0,) * array.ndim)
 
+    operands = [start, counts, state, cutoff, lhs1, lhs2, place]
+    in_specs = smem(2) + [
+        pl.BlockSpec((members, fields, tiles, ROW_TILE, LANES), lambda i: (0, 0, 0, i, 0)),
+        pl.BlockSpec((ROW_TILE, columns), lambda i: (first + stride * i, 0)),
+        whole(lhs1),
+        whole(lhs2),
+        whole(place),
+    ]
+    aliases = {}
+    if begun is not None:
+        aliases = {len(operands): 0}
+        operands.append(begun)
+        in_specs.append(pl.BlockSpec(memory_space=pl.ANY))
     return pl.pallas_call(
-        functools.partial(update_kernel, sizes),
-        grid=(rows // ROW_TILE,),
-        in_specs=smem(2)
-        + [
-            pl.BlockSpec(
-                (members, fields, tiles, ROW_TILE, LANES), lambda i: (0, 0, 0, i, 0)
-            ),
-            pl.BlockSpec((ROW_TILE, columns), lambda i: (i, 0)),
-            whole(lhs1),
-            whole(lhs2),
-            whole(place),
-        ],
+        functools.partial(update_kernel, sizes, first, stride, begun is not None),
+        grid=(len(row_tiles),),
+        in_specs=in_specs,
         out_specs=pl.BlockSpec(
-            (members, fields, ROW_TILE, columns), lambda i: (0, 0, i, 0)
+            (members, fields, ROW_TILE, columns), lambda i: (0, 0, first + stride * i, 0)
         ),
         out_shape=jax.ShapeDtypeStruct((members, fields, rows, columns), jnp.float32),
         scratch_shapes=[
@@ -428,9 +482,10 @@
             pltpu.VMEM((3 * members, width), jnp.bfloat16),
             pltpu.VMEM((members, fields, ROW_TILE, LANES), jnp.float32),
         ],
+        input_output_aliases=aliases,
         compiler_params=params(),
         name="update",
-    )(start, counts, state, cutoff, lhs1, lhs2, place)
+    )(*operands)
 
 
 def row_halos(block, axis):
@@ -459,23 +514,44 @@
 
     up, down = row_halos(ensemble, "sub")
     depth_up, depth_down = row_halos(sea_depth, "sub")
+    radius_part = pick_radius(cutoff, flat_x, flat_y, x_start, y_start)
+    begin = jnp.pad(radius_part[None, :], ((members, -(members + 1) % 8), (0, 0)))
+    tiles = col_block // LANES
+    inner_list, outer_list, list_counts = list_observations(
+        (members, tiles, rows), start, flat_x, flat_y
+    )
+
+    sent_inner = forecast(
+        inner_kernel, "inner", rows - 2 * HALO, sea_depth, blocks, ensemble
+    )
+    received_inner = lax.all_to_all(
+        sent_inner, "mem", split_axis=0, concat_axis=0, tiled=True
+    )
+    part = pick_heights(0, inner_list, list_counts, sent_inner, begin)
+
     depth = jnp.concatenate([depth_up, sea_depth, depth_down], 0)
-    sent = forecast(ensemble, up, down, depth, blocks)
-
-    radius_part = pick_radius(cutoff, flat_x, flat_y, x_start, y_start)
-    heights_part = pick_heights(sent, flat_x, flat_y, x_start)
-    part = jnp.concatenate([heights_part, radius_part[None, :]], 0)
-    part = jnp.pad(part, ((0, -part.shape[0] % 8), (0, 0)))
+    sent_outer = forecast(outer_kernel, "outer", 2 * HALO, depth, blocks, ensemble, up, down)
+    part = pick_heights(1, outer_list, list_counts, sent_outer, part)
     every = gather_over(sum_over(part, "sub")[None], "mem")
+    every, sent_outer = lax.optimization_barrier((every, sent_outer))
+    received_outer = lax.all_to_all(
+        sent_outer, "mem", split_axis=0, concat_axis=0, tiled=True
+    )
     heights = every[:, :members].reshape(blocks * members, -1)
     radius_sq = jnp.sum(every[:, members], 0)[None, :]
-
-    received = lax.all_to_all(sent, "mem", split_axis=0, concat_axis=0, tiled=True)
-    state = received.reshape((blocks * members,) + received.shape[2:])
     lhs1, lhs2, place, counts = chain(
         start, heights, radius_sq, obs_x, obs_y, obs_value, obs_var, cutoff, sizes
     )
-    return update(start, counts, state, cutoff, lhs1, lhs2, place, sizes)
+
+    def analyse(received, row_tiles, begun=None):
+        state = received.reshape((blocks * members,) + received.shape[2:])
+        return update(
+            start, counts, state, cutoff, lhs1, lhs2, place, sizes, row_tiles, begun
+        )
+
+    row_tiles = list(range(rows // ROW_TILE))
+    done = analyse(received_inner, row_tiles[1:-1])
+    return analyse(received_outer, [row_tiles[0], row_tiles[-1]], done)
 
 
 def solution(mesh):

time: 167 us -> 163 us (0.976)
  waiting for transfers between devices: 76.2 us -> 16.8 us
  Pallas kernels: 58.2 us -> 108 us
  starting transfers between devices: 19.1 us -> 26.8 us
    pallas_call x3 -> x7, Pallas kernels: 41.2 us -> 91.2 us  [the longest x1 30.4 us: list_observations(): pl.pallas_call(functools.partial(list_kernel, shape), in_specs=smem(3), o...]
    ppermute x5, waiting for transfers between devices: 57.8 us -> 13.3 us  [exchange(): return lax.ppermute(value, axis, [(i, i ^ distance) for i in range(size)])]
    ppermute x2, waiting for transfers between devices: 18.5 us -> 0.01 us  [row_halos(): lax.ppermute(last, axis, onward)]
    all_to_all x1 -> x2, starting transfers between devices: 5.94 us -> 13 us  [the longest x1 7.38 us: local(): lax.all_to_all(sent_inner, 'mem', split_axis=0, concat_axis=0, tiled=True)]
    all_to_all x1 -> x2, waiting for transfers between devices: 0.01 us -> 3.52 us  [the longest x1 3.51 us: local(): lax.all_to_all(sent_outer, 'mem', split_axis=0, concat_axis=0, tiled=True)]
    ppermute x5, starting transfers between devices: 8.86 us -> 11.6 us  [exchange(): return lax.ppermute(value, axis, [(i, i ^ distance) for i in range(size)])]
    ppermute x2, starting transfers between devices: 3.53 us -> 1.75 us  [row_halos(): lax.ppermute(leading, axis, backward)]
    unnamed x28 -> x36, local copies, waits for them, and re-layouts: 6.24 us -> 6.83 us
  transfers between devices with their start and end apart: 10 -> 11, of which waited for: 6 -> 6; matrix products, arithmetic and copies ran while one was open for 3% -> 3% of each run, Pallas kernels for 15% -> 55%
where the time goes in v2:
time: 163 us
  Pallas kernels  108 us (66%)
  starting transfers between devices  26.8 us (16%)
  waiting for transfers between devices  16.8 us (10%)
  local copies, waits for them, and re-layouts  8.92 us (5%)
  other arithmetic  1.65 us (1%)
    pallas_call x1, Pallas kernels, list_observations(): pl.pallas_call(functools.partial(list_kernel, shape), in_specs=smem(3), o...  30.4 us
    pallas_call x2, Pallas kernels, update(): pl.pallas_call(functools.partial(update_kernel, sizes, first, stride, beg...  23.7 us
    pallas_call x2, Pallas kernels, pick_heights(): pl.pallas_call(functools.partial(pick_kernel, which), grid=(1,), in_specs...  19.4 us
    pallas_call x2, Pallas kernels, forecast(): pl.pallas_call(kernel, grid=(members,), in_specs=[pl.BlockSpec((1,) + pie...  17.7 us
    pallas_call x1, Pallas kernels, chain(): pl.pallas_call(functools.partial(chain_kernel, sizes), in_specs=smem() +...  17 us
    ppermute x5, waiting for transfers between devices, exchange(): return lax.ppermute(value, axis, [(i, i ^ distance) for i in range(size)])  13.3 us
    ppermute x5, starting transfers between devices, exchange(): return lax.ppermute(value, axis, [(i, i ^ distance) for i in range(size)])  11.6 us
    all_to_all x1, starting transfers between devices, local(): lax.all_to_all(sent_inner, 'mem', split_axis=0, concat_axis=0, tiled=True)  7.38 us
  transfers between devices with their start and end apart: 11, of which 6 were waited for; matrix products, arithmetic and copies ran while one was open for 3% of the time, Pallas kernels for 55%

profile of v2, /device:TPU:0, one launch (start us, length us, event | category | flops | bytes accessed | tf_op | source)
XLA Modules:
  0.0 163.4 jit_solution(5375454250071136397)
XLA Ops:
  0.0 0.0 copy-start
  0.0 1.9 %copy-done = f32[4,3,32,2048]{3,2,1,0:T(8,128)S(1)} copy-done((f32[4,3,32,2048]{3,2,1,0:T(8,128)S(1)}, f32[4,3,32,2048]{3,2,1,0:T(8,128)}, u32[]{:S(2)}) %copy-start) | copy-done | bytes 3145752
  1.9 0.0 copy-start.4
  1.9 0.9 copy-done.4
  2.8 0.0 copy-start.5
  2.8 0.0 copy-start.1
  2.8 6.8 %inner.1.height_ref = f32[8,4,3,2,16,128]{5,4,3,2,1,0:T(8,128)S(1)} custom-call(f32[4,3,32,2048]{3,2,1,0:T(8,128)S(1)} %copy-done, f32[32,2048]{1,0:T(8,128)S(1)} %copy-done.4), custom_call_target="tpu_custom_call" | custom-call | tf_op jit(solution)/shard_map/inner/pallas_call | solution.py:88
  9.6 0.0 copy-start.2
  9.6 1.1 copy-done.2
  10.7 0.0 copy-start.15
  10.8 0.0 copy-start.6
  10.8 7.4 %all-to-all-start.1 = ((f32[8,4,3,2,16,128]{5,4,3,2,1,0:T(8,128)}), f32[8,4,3,2,16,128]{5,4,3,2,1,0:T(8,128)}, u32[]{:S(2)}, u32[]{:S(2)}) async-start(f32[8,4,3,2,16,128]{5,4,3,2,1,0:T(8,128)} %copy-done.2), calls=%async_computation.1 | async-start | bytes 3145728 | tf_op jit(solution)/shard_map/all_to_all | solution.py:527
  18.1 0.0 copy-done.5
  18.1 0.6 fusion.6
  18.8 0.0 collective-permute-start.2
  18.8 1.7 %collective-permute-start.3 = (f32[8,2048]{1,0:T(8,128)}, f32[8,2048]{1,0:T(8,128)}, u32[]{:S(2)}, u32[]{:S(2)}) collective-permute-start(f32[8,2048]{1,0:T(8,128)} %get-tuple-element.26), channel_id=1, source_target_pairs={{1,0},{2,1},{3,2},{0,3},{5,4},{6,5},{7,6},{4,7},{9,8},{10,9},{11,1... | collective-permute-start | bytes 196616 | tf_op jit(solution)/shard_map/ppermute | solution.py:498
  20.5 0.0 copy-done.1
  20.5 1.2 fusion.5
  21.8 0.0 collective-permute-start.1
  21.8 0.5 collective-permute-start
  22.3 0.0 copy-done.15
  22.3 0.0 copy-start.13
  22.4 0.0 copy-start.14
  22.4 0.0 copy-done.6
  22.4 0.8 fusion
  23.2 0.7 pad_add_fusion.2.start_ref
  23.9 0.0 copy-done.13
  23.9 0.0 copy-done.14
  23.9 30.4 %list.1 = (s32[3,1024]{1,0:T(4,128)}, s32[3,1024]{1,0:T(4,128)}, s32[2]{0:T(128)}) custom-call(s32[2]{0:T(128)} %pad_add_fusion.2.start_ref, s32[1024]{0:T(1024)} %bitcast.27, s32[1024]{0:T(1024)} %bitcast.29), custom_call_target="tpu_custom_call" | custom-call | tf_op jit(solution)/shard_map/list/pallas_call | solution.py:140
  54.3 0.0 copy-start.3
  54.3 1.4 copy-done.3
  55.7 0.7 copy-done.8
  56.4 0.7 copy-done.12
  57.1 10.0 %pick.2.start_ref = f32[8,1024]{1,0:T(8,128)S(1)} custom-call(s32[3,1024]{1,0:T(4,128)S(1)} %copy-done.8, s32[2]{0:T(128)S(1)} %copy-done.12, f32[8,4,3,2,16,128]{5,4,3,2,1,0:T(8,128)S(1)} %copy-done.3, f32[8,1024]{1,0:T(8,128)S(1)} %pad.4.start_ref), custom_call_target="tpu_custom_call" | custom-call | tf_op jit(solution)/shard_map/pick/pallas_call | solution.py:173
  67.1 0.0 collective-permute-done.2
  67.1 0.0 collective-permute-done.3
  67.1 0.9 pad_maximum_fusion.depth_ref
  68.0 0.0 copy-start.7
  68.0 0.0 collective-permute-done.1.down_ref
  68.0 0.0 collective-permute-done.up_ref
  68.0 10.9 %outer.1.height_ref = f32[8,4,3,2,16,128]{5,4,3,2,1,0:T(8,128)} custom-call(f32[4,3,32,2048]{3,2,1,0:T(8,128)} %ens_ref.3, f32[4,3,8,2048]{3,2,1,0:T(8,128)S(1)} %collective-permute-done.up_ref, f32[4,3,8,2048]{3,2,1,0:T(8,128)S(1)} %collective-permute-done.1.down_ref, f32[48,2048]{1,0:T(8,128)S(1)} %pad_maximum_fusion.depth_ref), custom_call_target="tpu_custom_call" | custom-call | tf_op jit(solution)/shard_map/outer/pallas_call | solution.py:88
  79.0 0.0 copy-done.7
  79.0 0.0 copy-start.11
  79.0 9.3 %pick.3 = f32[8,1024]{1,0:T(8,128)S(1)} custom-call(s32[3,1024]{1,0:T(4,128)S(1)} %copy-done.7, s32[2]{0:T(128)S(1)} %copy-done.12, f32[8,4,3,2,16,128]{5,4,3,2,1,0:T(8,128)} %outer.1.height_ref, f32[8,1024]{1,0:T(8,128)S(1)} %pick.2.start_ref), custom_call_target="tpu_custom_call" | custom-call | tf_op jit(solution)/shard_map/pick/pallas_call | solution.py:173
  88.3 4.1 %collective-permute-start.4 = (f32[8,1024]{1,0:T(8,128)S(1)}, f32[8,1024]{1,0:T(8,128)S(1)}, u32[]{:S(2)}, u32[]{:S(2)}) collective-permute-start(f32[8,1024]{1,0:T(8,128)S(1)} %pick.3), channel_id=1, source_target_pairs={{0,1},{1,0},{2,3},{3,2},{4,5},{5,4},{6,7},{7,6},{8,9},{9,8},{10,11... | collective-permute-start | bytes 98312 | tf_op jit(solution)/shard_map/ppermute | solution.py:199
  92.4 0.9 collective-permute-done.4
  93.3 0.0 collective-permute-start.5
  93.3 3.9 %collective-permute-done.5 = f32[8,1024]{1,0:T(8,128)S(1)} collective-permute-done((f32[8,1024]{1,0:T(8,128)S(1)}, f32[8,1024]{1,0:T(8,128)S(1)}, u32[]{:S(2)}, u32[]{:S(2)}) %collective-permute-start.5) | collective-permute-done | bytes 32800 | tf_op jit(solution)/shard_map/ppermute | solution.py:199
  97.2 2.0 %collective-permute-start.6 = (f32[1,8,1024]{2,1,0:T(8,128)S(1)}, f32[1,8,1024]{2,1,0:T(8,128)S(1)}, u32[]{:S(2)}, u32[]{:S(2)}) collective-permute-start(f32[1,8,1024]{2,1,0:T(8,128)S(1)} %add_bitcast_fusion), channel_id=1, source_target_pairs={{0,4},{4,0},{8,12},{12,8},{16,20},{20,16},{24,28},{28,24},{1,5},{5... | collective-permute-start | bytes 98312 | tf_op jit(solution)/shard_map/ppermute | solution.py:199
  99.2 1.9 %collective-permute-done.6 = f32[1,8,1024]{2,1,0:T(8,128)S(1)} collective-permute-done((f32[1,8,1024]{2,1,0:T(8,128)S(1)}, f32[1,8,1024]{2,1,0:T(8,128)S(1)}, u32[]{:S(2)}, u32[]{:S(2)}) %collective-permute-start.6) | collective-permute-done | bytes 32800 | tf_op jit(solution)/shard_map/ppermute | solution.py:199
  101.1 2.1 %collective-permute-start.7 = (f32[2,8,1024]{2,1,0:T(8,128)S(1)}, f32[2,8,1024]{2,1,0:T(8,128)S(1)}, u32[]{:S(2)}, u32[]{:S(2)}) collective-permute-start(f32[2,8,1024]{2,1,0:T(8,128)S(1)} %maximum_select_fusion.2), channel_id=1, source_target_pairs={{0,8},{4,12},{8,0},{12,4},{16,24},{20,28},{24,16},{28,20},{1,9},{5... | collective-permute-start | bytes 196616 | tf_op jit(solution)/shard_map/ppermute | solution.py:199
  103.2 2.2 %collective-permute-done.7 = f32[2,8,1024]{2,1,0:T(8,128)S(1)} collective-permute-done((f32[2,8,1024]{2,1,0:T(8,128)S(1)}, f32[2,8,1024]{2,1,0:T(8,128)S(1)}, u32[]{:S(2)}, u32[]{:S(2)}) %collective-permute-start.7) | collective-permute-done | bytes 65568 | tf_op jit(solution)/shard_map/ppermute | solution.py:199
  105.4 3.4 %collective-permute-start.8 = (f32[4,8,1024]{2,1,0:T(8,128)S(1)}, f32[4,8,1024]{2,1,0:T(8,128)S(1)}, u32[]{:S(2)}, u32[]{:S(2)}) collective-permute-start(f32[4,8,1024]{2,1,0:T(8,128)S(1)} %maximum_select_fusion.1), channel_id=1, source_target_pairs={{0,16},{4,20},{8,24},{12,28},{16,0},{20,4},{24,8},{28,12},{1,17},{... | collective-permute-start | bytes 393224 | tf_op jit(solution)/shard_map/ppermute | solution.py:199
  108.9 4.4 %collective-permute-done.8 = f32[4,8,1024]{2,1,0:T(8,128)S(1)} collective-permute-done((f32[4,8,1024]{2,1,0:T(8,128)S(1)}, f32[4,8,1024]{2,1,0:T(8,128)S(1)}, u32[]{:S(2)}, u32[]{:S(2)}) %collective-permute-start.8) | collective-permute-done | bytes 131104 | tf_op jit(solution)/shard_map/ppermute | solution.py:199
  113.2 0.0 all-to-all-done.1
  113.2 5.6 %all-to-all-start = ((f32[8,4,3,2,16,128]{5,4,3,2,1,0:T(8,128)}), f32[8,4,3,2,16,128]{5,4,3,2,1,0:T(8,128)S(1)}, u32[]{:S(2)}, u32[]{:S(2)}) async-start(f32[8,4,3,2,16,128]{5,4,3,2,1,0:T(8,128)} %outer.1.height_ref), calls=%async_computation | async-start | bytes 3145728 | tf_op jit(solution)/shard_map/all_to_all | solution.py:537
  118.9 0.1 copy.26
  119.1 0.0 copy-done.9
  119.2 0.0 copy-done.10
  119.2 0.0 copy-done.11
  119.2 17.0 %chain.1 = (bf16[4,256,96]{2,1,0:T(8,128)(2,1)S(1)}, bf16[4,4,32,192]{3,2,1,0:T(8,128)(2,1)S(1)}, f32[4,256,256]{2,1,0:T(8,128)S(1)}, s32[4]{0:T(128)S(1)}) custom-call(s32[2]{0:T(128)S(1)} %copy-done.9, f32[32,1024]{1,0:T(8,128)S(1)} %reshape.31.heights_ref, f32[1,1024]{1,0:T(1,128)S(1)} %bitcast.21, s32[2,1024]{1,0:T(2,128)S(1)} %pad_add_fusion.row_ref, ...), custom_call_target="tpu_custom_call" | custom-call | tf_op jit(solution)/shard_map/chain/pallas_call | solution.py:353
  136.2 12.2 %update.2.rest_0_ = f32[32,3,32,256]{3,2,1,0:T(8,128)} custom-call(s32[2]{0:T(128)S(1)} %copy-done.9, s32[4]{0:T(128)S(1)} %get-tuple-element.18.count_ref, f32[32,3,2,16,128]{4,3,2,1,0:T(8,128)} %bitcast.7.state_ref, s32[32,256]{1,0:T(8,128)S(1)} %copy-done.6, bf16[4,256,96]{2,1,0:T(8,128)(2,1)S(1)} %get-tuple-element.20.lhs1_ref, ...), custom_call_target="tpu_custom_call" | custom-call | tf_op jit(solution)/shard_map/update/pallas_call | solution.py:472
  148.5 3.5 %all-to-all-done = f32[8,4,3,2,16,128]{5,4,3,2,1,0:T(8,128)S(1)} async-done(((f32[8,4,3,2,16,128]{5,4,3,2,1,0:T(8,128)}), f32[8,4,3,2,16,128]{5,4,3,2,1,0:T(8,128)S(1)}, u32[]{:S(2)}, u32[]{:S(2)}) %all-to-all-start) | async-done | bytes 1572896 | tf_op jit(solution)/shard_map/all_to_all | solution.py:537
  152.0 11.5 %update.3 = f32[32,3,32,256]{3,2,1,0:T(8,128)} custom-call(s32[2]{0:T(128)S(1)} %copy-done.9, s32[4]{0:T(128)S(1)} %get-tuple-element.18.count_ref, f32[32,3,2,16,128]{4,3,2,1,0:T(8,128)S(1)} %bitcast.19, s32[32,256]{1,0:T(8,128)S(1)} %copy-done.6, bf16[4,256,96]{2,1,0:T(8,128)(2,1)S(1)} %get-tuple-element.20.lhs1_ref, ...), custom_call_target="tpu_custom_call", output_to_operand_aliasing={{}: (7, {})} | custom-call | tf_op jit(solution)/shard_map/update/pallas_call | solution.py:472
  (21 shorter events, 0.2 us)
Async XLA Ops:
  0.0 1.9 %copy-start = (f32[4,3,32,2048]{3,2,1,0:T(8,128)S(1)}, f32[4,3,32,2048]{3,2,1,0:T(8,128)}, u32[]{:S(2)}) copy-start(f32[4,3,32,2048]{3,2,1,0:T(8,128)} %ens_ref.3) | copy-start | bytes 9437188
  1.9 0.9 copy-start.4
  2.8 15.3 %copy-start.5 = (f32[32,2048]{1,0:T(8,128)S(1)}, f32[32,2048]{1,0:T(8,128)}, u32[]{:S(2)}) copy-start(f32[32,2048]{1,0:T(8,128)} %depth_ref.1) | copy-start | bytes 786436
  2.8 17.7 %copy-start.1 = (f32[4,3,32,2048]{3,2,1,0:T(8,128)S(1)}, f32[4,3,32,2048]{3,2,1,0:T(8,128)}, u32[]{:S(2)}) copy-start(f32[4,3,32,2048]{3,2,1,0:T(8,128)} %ens_ref.3) | copy-start | bytes 9437188
  9.6 1.1 copy-start.2
  10.7 11.6 %copy-start.15 = (s32[4,256]{1,0:T(4,128)S(1)}, s32[4,256]{1,0:T(4,128)}, u32[]{:S(2)}) copy-start(s32[4,256]{1,0:T(4,128)} %param.9) | copy-start | bytes 12292
  10.8 11.6 %copy-start.6 = (s32[32,256]{1,0:T(8,128)S(1)}, s32[32,256]{1,0:T(8,128)}, u32[]{:S(2)}) copy-start(s32[32,256]{1,0:T(8,128)} %cutoff_ref.5) | copy-start | bytes 98308
  10.8 102.5 %all-to-all-start.1 = ((f32[8,4,3,2,16,128]{5,4,3,2,1,0:T(8,128)}), f32[8,4,3,2,16,128]{5,4,3,2,1,0:T(8,128)}, u32[]{:S(2)}, u32[]{:S(2)}) async-start(f32[8,4,3,2,16,128]{5,4,3,2,1,0:T(8,128)} %copy-done.2), calls=%async_computation.1 | async-start | bytes 3145728 | tf_op jit(solution)/shard_map/all_to_all | solution.py:527
  18.8 48.3 %collective-permute-start.2 = (f32[8,2048]{1,0:T(8,128)}, f32[8,2048]{1,0:T(8,128)S(1)}, u32[]{:S(2)}, u32[]{:S(2)}) collective-permute-start(f32[8,2048]{1,0:T(8,128)} %get-tuple-element.25), channel_id=1, source_target_pairs={{0,1},{1,2},{2,3},{3,0},{4,5},{5,6},{6,7},{7,4},{8,9},{9,10},{10,1... | collective-permute-start | bytes 196616 | tf_op jit(solution)/shard_map/ppermute | solution.py:498
  18.8 48.3 %collective-permute-start.3 = (f32[8,2048]{1,0:T(8,128)}, f32[8,2048]{1,0:T(8,128)}, u32[]{:S(2)}, u32[]{:S(2)}) collective-permute-start(f32[8,2048]{1,0:T(8,128)} %get-tuple-element.26), channel_id=1, source_target_pairs={{1,0},{2,1},{3,2},{0,3},{5,4},{6,5},{7,6},{4,7},{9,8},{10,9},{11,1... | collective-permute-start | bytes 196616 | tf_op jit(solution)/shard_map/ppermute | solution.py:498
  21.8 46.2 %collective-permute-start.1 = (f32[4,3,8,2048]{3,2,1,0:T(8,128)}, f32[4,3,8,2048]{3,2,1,0:T(8,128)S(1)}, u32[]{:S(2)}, u32[]{:S(2)}) collective-permute-start(f32[4,3,8,2048]{3,2,1,0:T(8,128)} %get-tuple-element.23), channel_id=1, source_target_pairs={{1,0},{2,1},{3,2},{0,3},{5,4},{6,5},{7,6},{4,7},{9,8},{10,9},{11,1... | collective-permute-start | bytes 2359304 | tf_op jit(solution)/shard_map/ppermute | solution.py:498
  21.8 46.2 %collective-permute-start = (f32[4,3,8,2048]{3,2,1,0:T(8,128)}, f32[4,3,8,2048]{3,2,1,0:T(8,128)S(1)}, u32[]{:S(2)}, u32[]{:S(2)}) collective-permute-start(f32[4,3,8,2048]{3,2,1,0:T(8,128)} %get-tuple-element.24), channel_id=1, source_target_pairs={{0,1},{1,2},{2,3},{3,0},{4,5},{5,6},{6,7},{7,4},{8,9},{9,10},{10,1... | collective-permute-start | bytes 2359304 | tf_op jit(solution)/shard_map/ppermute | solution.py:498
  22.3 1.5 copy-start.13
  22.4 1.5 copy-start.14
  54.3 1.4 copy-start.3
  55.7 0.7 copy-start.8
  56.4 0.7 copy-start.12
  68.0 10.9 %copy-start.7 = (s32[3,1024]{1,0:T(4,128)S(1)}, s32[3,1024]{1,0:T(4,128)}, u32[]{:S(2)}) copy-start(s32[3,1024]{1,0:T(4,128)} %get-tuple-element.14.list_ref) | copy-start | bytes 36868
  79.0 40.2 %copy-start.9 = (s32[2]{0:T(128)S(1)}, s32[2]{0:T(128)}, u32[]{:S(2)}) copy-start(s32[2]{0:T(128)} %pad_add_fusion.2.start_ref) | copy-start | bytes 28
  79.0 40.2 %copy-start.10 = (f32[4,256]{1,0:T(4,128)S(1)}, f32[4,256]{1,0:T(4,128)}, u32[]{:S(2)}) copy-start(f32[4,256]{1,0:T(4,128)} %value_ref.1) | copy-start | bytes 12292
  79.0 40.2 %copy-start.11 = (f32[4,256]{1,0:T(4,128)S(1)}, f32[4,256]{1,0:T(4,128)}, u32[]{:S(2)}) copy-start(f32[4,256]{1,0:T(4,128)} %variance_ref.1) | copy-start | bytes 12292
  88.3 4.9 %collective-permute-start.4 = (f32[8,1024]{1,0:T(8,128)S(1)}, f32[8,1024]{1,0:T(8,128)S(1)}, u32[]{:S(2)}, u32[]{:S(2)}) collective-permute-start(f32[8,1024]{1,0:T(8,128)S(1)} %pick.3), channel_id=1, source_target_pairs={{0,1},{1,0},{2,3},{3,2},{4,5},{5,4},{6,7},{7,6},{8,9},{9,8},{10,11... | collective-permute-start | bytes 98312 | tf_op jit(solution)/shard_map/ppermute | solution.py:199
  93.3 3.9 %collective-permute-start.5 = (f32[8,1024]{1,0:T(8,128)S(1)}, f32[8,1024]{1,0:T(8,128)S(1)}, u32[]{:S(2)}, u32[]{:S(2)}) collective-permute-start(f32[8,1024]{1,0:T(8,128)S(1)} %add.16), channel_id=1, source_target_pairs={{0,2},{1,3},{2,0},{3,1},{4,6},{5,7},{6,4},{7,5},{8,10},{9,11},{10,... | collective-permute-start | bytes 98312 | tf_op jit(solution)/shard_map/ppermute | solution.py:199
  97.2 3.9 %collective-permute-start.6 = (f32[1,8,1024]{2,1,0:T(8,128)S(1)}, f32[1,8,1024]{2,1,0:T(8,128)S(1)}, u32[]{:S(2)}, u32[]{:S(2)}) collective-permute-start(f32[1,8,1024]{2,1,0:T(8,128)S(1)} %add_bitcast_fusion), channel_id=1, source_target_pairs={{0,4},{4,0},{8,12},{12,8},{16,20},{20,16},{24,28},{28,24},{1,5},{5... | collective-permute-start | bytes 98312 | tf_op jit(solution)/shard_map/ppermute | solution.py:199
  101.1 4.3 %collective-permute-start.7 = (f32[2,8,1024]{2,1,0:T(8,128)S(1)}, f32[2,8,1024]{2,1,0:T(8,128)S(1)}, u32[]{:S(2)}, u32[]{:S(2)}) collective-permute-start(f32[2,8,1024]{2,1,0:T(8,128)S(1)} %maximum_select_fusion.2), channel_id=1, source_target_pairs={{0,8},{4,12},{8,0},{12,4},{16,24},{20,28},{24,16},{28,20},{1,9},{5... | collective-permute-start | bytes 196616 | tf_op jit(solution)/shard_map/ppermute | solution.py:199
  105.4 7.8 %collective-permute-start.8 = (f32[4,8,1024]{2,1,0:T(8,128)S(1)}, f32[4,8,1024]{2,1,0:T(8,128)S(1)}, u32[]{:S(2)}, u32[]{:S(2)}) collective-permute-start(f32[4,8,1024]{2,1,0:T(8,128)S(1)} %maximum_select_fusion.1), channel_id=1, source_target_pairs={{0,16},{4,20},{8,24},{12,28},{16,0},{20,4},{24,8},{28,12},{1,17},{... | collective-permute-start | bytes 393224 | tf_op jit(solution)/shard_map/ppermute | solution.py:199
  113.2 38.7 %all-to-all-start = ((f32[8,4,3,2,16,128]{5,4,3,2,1,0:T(8,128)}), f32[8,4,3,2,16,128]{5,4,3,2,1,0:T(8,128)S(1)}, u32[]{:S(2)}, u32[]{:S(2)}) async-start(f32[8,4,3,2,16,128]{5,4,3,2,1,0:T(8,128)} %outer.1.height_ref), calls=%async_computation | async-start | bytes 3145728 | tf_op jit(solution)/shard_map/all_to_all | solution.py:537

commit v3 on v1

--- a/solution.py
+++ b/solution.py
@@ -45,11 +45,8 @@
     return pltpu.roll(field, length - 1, axis) - pltpu.roll(field, 1, axis)
 
 
-def forecast_kernel(ens_ref, up_ref, down_ref, depth_ref, out_ref):
-    height, east, north = [
-        jnp.concatenate([up_ref[0, f], ens_ref[0, f], down_ref[0, f]], 0) for f in range(3)
-    ]
-    depth = depth_ref[...]
+def forecast_steps(window, depth):
+    height, east, north = window
     half = 0.5 * step_size
     turn = step_size * coriolis
     for _ in range(STEPS):
@@ -57,86 +54,162 @@
         north_new = north - turn * east - half * centred(height, 1)
         height = height - half * (centred(depth * east_new, 0) + centred(depth * north_new, 1))
         east, north = east_new, north_new
-    rows = ens_ref.shape[2]
-    blocks, _, _, tiles = out_ref.shape[:4]
-    for f, field in enumerate((height, east, north)):
+    return height, east, north
+
+
+def send_rows(out_ref, fields, first_row):
+    blocks, _, _, tiles, rows, _ = out_ref.shape
+    for f, field in enumerate(fields):
         for d in range(blocks):
             for t in range(tiles):
                 first = (d * tiles + t) * LANES
-                out_ref[d, 0, f, t] = field[HALO : HALO + rows, first : first + LANES]
-
-
-def forecast(ensemble, up, down, depth, blocks):
+                out_ref[d, 0, f, t] = field[
+                    first_row : first_row + rows, first : first + LANES
+                ]
+
+
+def near_kernel(parity_ref, ens_ref, halo_ref, depth_ref, depth_halo_ref, out_ref):
+    odd = parity_ref[0] == 1
+
+    def window(block, halo):
+        return jnp.where(
+            odd, jnp.concatenate([halo, block], 0), jnp.concatenate([block, halo], 0)
+        )
+
+    fields = [window(ens_ref[0, f], halo_ref[f]) for f in range(3)]
+    done = forecast_steps(fields, window(depth_ref[...], depth_halo_ref[0]))
+    send_rows(out_ref, done, HALO)
+
+
+def far_kernel(parity_ref, ens_ref, halo_ref, depth_ref, depth_halo_ref, out_ref):
+    odd = parity_ref[0] == 1
+    rows = depth_ref.shape[0]
+
+    def window(block, halo):
+        return jnp.where(
+            odd,
+            jnp.concatenate([block[rows - 2 * HALO :], halo], 0),
+            jnp.concatenate([halo, block[: 2 * HALO]], 0),
+        )
+
+    fields = [window(ens_ref[0, f], halo_ref[f]) for f in range(3)]
+    done = forecast_steps(fields, window(depth_ref[...], depth_halo_ref[0]))
+    send_rows(out_ref, done, HALO)
+
+
+def forecast(kernel, name, out_rows, parity, ensemble, halo, depth, blocks):
     members, fields, rows, columns = ensemble.shape
     tiles = columns // blocks // LANES
     return pl.pallas_call(
-        forecast_kernel,
+        kernel,
         grid=(members,),
-        in_specs=[
+        in_specs=smem()
+        + [
             pl.BlockSpec((1, fields, rows, columns), lambda m: (m, 0, 0, 0)),
-            pl.BlockSpec((1, fields, HALO, columns), lambda m: (m, 0, 0, 0)),
-            pl.BlockSpec((1, fields, HALO, columns), lambda m: (m, 0, 0, 0)),
-            pl.BlockSpec((rows + 2 * HALO, columns), lambda m: (0, 0)),
+            pl.BlockSpec((fields, HALO, columns), lambda m: (m, 0, 0)),
+            pl.BlockSpec((rows, columns), lambda m: (0, 0)),
+            pl.BlockSpec((1, HALO, columns), lambda m: (members * fields, 0, 0)),
         ],
         out_specs=pl.BlockSpec(
-            (blocks, 1, fields, tiles, rows, LANES), lambda m: (0, m, 0, 0, 0, 0)
+            (blocks, 1, fields, tiles, out_rows, LANES), lambda m: (0, m, 0, 0, 0, 0)
         ),
         out_shape=jax.ShapeDtypeStruct(
-            (blocks, members, fields, tiles, rows, LANES), jnp.float32
+            (blocks, members, fields, tiles, out_rows, LANES), jnp.float32
         ),
         compiler_params=params(),
-        name="forecast",
-    )(ensemble, up, down, depth)
-
-
-def pick_kernel(base_ref, lane_ref, place_ref, height_ref, out_ref):
+        name=name,
+    )(parity, ensemble, halo, depth, halo)
+
+
+def pick(row_ref, col_ref, height_ref):
     blocks, members, _, tiles, rows, _ = height_ref.shape
-    flat = height_ref.reshape(blocks * members * tiles * rows, LANES)
-    lanes = lax.broadcasted_iota(jnp.int32, (members, LANES), 1)
-    unroll = 16
-
-    def group(g, _):
-        def some(i, acc):
-            for j in range(unroll):
-                k = i * unroll + j
-                o = g * LANES + k
-                row = flat[pl.ds(base_ref[o], members, stride=tiles * rows), :]
-                row = pltpu.roll(row, lane_ref[o], 1)
-                acc = jnp.where(lanes == place_ref[o], row, acc)
-            return acc
-
-        acc = lax.fori_loop(
-            0, LANES // unroll, some, jnp.zeros((members, LANES), jnp.float32)
-        )
-        out_ref[:, pl.ds(pl.multiple_of(g * LANES, LANES), LANES)] = acc
-        return 0
-
-    lax.fori_loop(0, out_ref.shape[1] // LANES, group, 0)
-
-
-def pick_heights(sent, obs_x, obs_y, x_start):
-    blocks, members, fields, tiles, rows, _ = sent.shape
-    count = obs_x.shape[0]
-    col_block = tiles * LANES
-    local_x = obs_x - x_start
-    inside = (local_x >= 0) & (local_x < rows)
-    safe_x = jnp.where(inside, local_x, 0)
-    block = obs_y // col_block
-    tile = (obs_y % col_block) // LANES
-    base = (block * members * tiles + tile) * rows + safe_x
-    place = jnp.arange(count, dtype=jnp.int32) % LANES
-    shift = (place - obs_y % LANES) % LANES
-    place = jnp.where(inside, place, -1)
+    heights = jnp.concatenate(
+        [
+            height_ref[d, :, 0, t].reshape(members * rows, LANES)
+            for d in range(blocks)
+            for t in range(tiles)
+        ],
+        1,
+    )
+    high, rest = heights.astype(jnp.bfloat16), heights
+    pieces = [high]
+    for _ in range(2):
+        rest = rest - pieces[-1].astype(jnp.float32)
+        pieces.append(rest.astype(jnp.bfloat16))
+    count = col_ref.shape[1]
+    column = lax.broadcasted_iota(jnp.int32, (heights.shape[1], count), 0)
+    in_column = (column == col_ref[...]).astype(jnp.float32).astype(jnp.bfloat16)
+    found = jnp.dot(
+        jnp.concatenate(pieces, 0), in_column, preferred_element_type=jnp.float32
+    )
+    size = members * rows
+    found = (found[:size] + found[size : 2 * size]) + found[2 * size :]
+    found = found.reshape(members, rows, count)
+    row = lax.broadcasted_iota(jnp.int32, (1, rows, count), 1)
+    return jnp.sum(jnp.where(row == row_ref[...][None], found, 0.0), 1)
+
+
+def pick_near_kernel(row_ref, col_ref, height_ref, out_ref):
+    out_ref[...] = pick(row_ref, col_ref, height_ref)
+
+
+def pick_far_kernel(row_ref, col_ref, height_ref, near_ref, radius_ref, out_ref):
+    heights = pick(row_ref, col_ref, height_ref) + near_ref[...]
+    members, count = heights.shape
+    pieces = out_ref.shape[0]
+    groups = count // pieces // LANES
+    out_ref[...] = jnp.zeros_like(out_ref)
+    for j in range(pieces):
+        for g in range(groups):
+            part = slice((j * groups + g) * LANES, (j * groups + g + 1) * LANES)
+            for m in range(members):
+                row = m * groups + g
+                out_ref[j, row : row + 1, :] = heights[m : m + 1, part]
+            row = members * groups + g
+            out_ref[j, row : row + 1, :] = radius_ref[:, part]
+
+
+def height_spec(sent):
+    blocks, members, _, tiles, rows, _ = sent.shape
+    return pl.BlockSpec((blocks, members, 1, tiles, rows, LANES), lambda i: (0,) * 6)
+
+
+def whole_spec(shape):
+    return pl.BlockSpec(shape, lambda i: (0,) * len(shape))
+
+
+def pick_near(row, col, sent):
+    shape = (sent.shape[1], col.shape[1])
     return pl.pallas_call(
-        pick_kernel,
+        pick_near_kernel,
         grid=(1,),
-        in_specs=smem(3)
-        + [pl.BlockSpec((blocks, members, 1, tiles, rows, LANES), lambda i: (0,) * 6)],
-        out_specs=pl.BlockSpec((members, count), lambda i: (0, 0)),
-        out_shape=jax.ShapeDtypeStruct((members, count), jnp.float32),
+        in_specs=[whole_spec(row.shape), whole_spec(col.shape), height_spec(sent)],
+        out_specs=whole_spec(shape),
+        out_shape=jax.ShapeDtypeStruct(shape, jnp.float32),
         compiler_params=params(),
-        name="pick",
-    )(base, shift, place, sent)
+        name="pick_near",
+    )(row, col, sent)
+
+
+def pick_far(row, col, sent, near, radius, pieces):
+    members, count = near.shape
+    used = (members + 1) * (count // pieces // LANES)
+    shape = (pieces, used + -used % 8, LANES)
+    return pl.pallas_call(
+        pick_far_kernel,
+        grid=(1,),
+        in_specs=[
+            whole_spec(row.shape),
+            whole_spec(col.shape),
+            height_spec(sent),
+            whole_spec(near.shape),
+            whole_spec(radius.shape),
+        ],
+        out_specs=whole_spec(shape),
+        out_shape=jax.ShapeDtypeStruct(shape, jnp.float32),
+        compiler_params=params(),
+        name="pick_far",
+    )(row, col, sent, near, radius)
 
 
 def pick_radius(cutoff, obs_x, obs_y, x_start, y_start):
@@ -162,14 +235,9 @@
 
 
 def gather_over(value, axis):
-    here = lax.axis_index(axis)
     distance = 1
     while distance < lax.axis_size(axis):
-        other = exchange(value, axis, distance)
-        lower = (here & distance) == 0
-        value = jnp.where(
-            lower, jnp.concatenate([value, other], 0), jnp.concatenate([other, value], 0)
-        )
+        value = jnp.concatenate([value, exchange(value, axis, distance)], 0)
         distance *= 2
     return value
 
@@ -181,10 +249,10 @@
 
 
 def chain_kernel(
+    members,
     sizes,
     start_ref,
-    heights_ref,
-    radius_ref,
+    every_ref,
     row_ref,
     col_ref,
     value_ref,
@@ -196,15 +264,32 @@
     count_ref,
 ):
     size_x, size_y = sizes
-    members = heights_ref.shape[0]
+    pieces, sources, _, _ = every_ref.shape
     batches, count = value_ref.shape
+    groups = batches * count // pieces // LANES
+    local_members = members // sources
     rows, columns = cutoff_ref.shape
     x_start = start_ref[0]
     y_start = start_ref[1]
     reach = jnp.max(cutoff_ref[...])
     reach_sq = reach * reach
 
-    heights = heights_ref[...]
+    heights, radius_sq = [], []
+    for j in range(pieces):
+        piece = jnp.bitwise_xor(start_ref[2], j)
+        for g in range(groups):
+            found, radius = [], 0.0
+            for source in range(sources):
+                one = every_ref.at[piece, jnp.bitwise_xor(start_ref[3], source)]
+                found += [
+                    one[m * groups + g : m * groups + g + 1, :] for m in range(local_members)
+                ]
+                last = local_members * groups + g
+                radius = radius + one[last : last + 1, :]
+            heights.append(jnp.concatenate(found, 0))
+            radius_sq.append(radius)
+    heights = jnp.concatenate(heights, 1)
+    radius_sq = jnp.concatenate(radius_sq, 1)
     before = (
         lax.broadcasted_iota(jnp.int32, (count, count), 0)
         <= lax.broadcasted_iota(jnp.int32, (count, count), 1)
@@ -291,7 +376,7 @@
             dist_sq = apart_sq(col_ref[:, b : b + 1], row_ref[0:1, later], size_x) + apart_sq(
                 col_ref[:, batches + b : batches + b + 1], row_ref[1:2, later], size_y
             )
-            ratio = dist_sq.astype(jnp.float32) / radius_ref[:, later]
+            ratio = dist_sq.astype(jnp.float32) / radius_sq[:, later]
             gain = cross * jnp.square(jnp.maximum(1.0 - ratio, 0.0))
             ahead = ahead + jnp.dot(
                 mix, gain, precision=highest, preferred_element_type=jnp.float32
@@ -299,14 +384,13 @@
             heights = jnp.concatenate([heights[:, : (b + 1) * count], ahead], 1)
 
 
-def chain(start, heights, radius_sq, obs_x, obs_y, values, variance, cutoff, sizes):
-    members = heights.shape[0]
+def chain(members, start, every, obs_x, obs_y, values, variance, cutoff, sizes):
     batches, count = values.shape
     row_form = jnp.stack([obs_x.reshape(-1), obs_y.reshape(-1)], 0)
     col_form = jnp.concatenate([obs_x, obs_y], 0).T
     return pl.pallas_call(
-        functools.partial(chain_kernel, sizes),
-        in_specs=smem() + vmem(7),
+        functools.partial(chain_kernel, members, sizes),
+        in_specs=smem() + vmem(6),
         out_specs=vmem(3) + smem(),
         out_shape=[
             jax.ShapeDtypeStruct((batches, count, 3 * members), jnp.bfloat16),
@@ -318,11 +402,13 @@
         ],
         compiler_params=params(),
         name="chain",
-    )(start, heights, radius_sq, row_form, col_form, values, variance, cutoff)
+    )(start, every, row_form, col_form, values, variance, cutoff)
 
 
 def update_kernel(
     sizes,
+    continues,
+    tile_ref,
     start_ref,
     count_ref,
     state_ref,
@@ -330,18 +416,16 @@
     lhs1_ref,
     lhs2_ref,
     place_ref,
-    out_ref,
-    members_ref,
-    rhs_ref,
-    back_ref,
+    *rest,
 ):
+    out_ref, members_ref, rhs_ref, back_ref = rest[1:] if continues else rest
     size_x, size_y = float(sizes[0]), float(sizes[1])
     members, fields, tiles, rows, _ = state_ref.shape
     batches = lhs1_ref.shape[0]
     cells = rows * LANES
     flat = state_ref.reshape(members * fields * tiles * rows, LANES)
     flat_back = back_ref.reshape(members * fields * rows, LANES)
-    row0 = (start_ref[0] + pl.program_id(0) * rows).astype(jnp.float32)
+    row0 = (start_ref[0] + tile_ref[pl.program_id(0)] * rows).astype(jnp.float32)
     lane = lax.broadcasted_iota(jnp.int32, (1, LANES), 1).astype(jnp.float32)
 
     def contribution(b, k, t):
@@ -398,84 +482,124 @@
         out_ref[:, :, :, t * LANES : (t + 1) * LANES] = back_ref[...]
 
 
-def update(start, counts, state, cutoff, lhs1, lhs2, place, sizes):
-    members, fields, tiles, rows, _ = state.shape
+def update(row_tiles, start, counts, state, cutoff, lhs1, lhs2, place, sizes, begun=None):
+    members, fields, tiles, _, _ = state.shape
+    rows = cutoff.shape[0]
     columns = tiles * LANES
     width = fields * ROW_TILE * LANES
 
     def whole(array):
-        return pl.BlockSpec(array.shape, lambda i: (0,) * array.ndim)
-
+        return pl.BlockSpec(array.shape, lambda i, tile: (0,) * array.ndim)
+
+    operands = [row_tiles, start, counts, state, cutoff, lhs1, lhs2, place]
+    in_specs = smem(2) + [
+        pl.BlockSpec(
+            (members, fields, tiles, ROW_TILE, LANES), lambda i, tile: (0, 0, 0, i, 0)
+        ),
+        pl.BlockSpec((ROW_TILE, columns), lambda i, tile: (tile[i], 0)),
+        whole(lhs1),
+        whole(lhs2),
+        whole(place),
+    ]
+    aliases = {}
+    if begun is not None:
+        aliases = {len(operands): 0}
+        operands.append(begun)
+        in_specs.append(pl.BlockSpec(memory_space=pl.ANY))
     return pl.pallas_call(
-        functools.partial(update_kernel, sizes),
-        grid=(rows // ROW_TILE,),
-        in_specs=smem(2)
-        + [
-            pl.BlockSpec(
-                (members, fields, tiles, ROW_TILE, LANES), lambda i: (0, 0, 0, i, 0)
+        functools.partial(update_kernel, sizes, begun is not None),
+        grid_spec=pltpu.PrefetchScalarGridSpec(
+            num_scalar_prefetch=1,
+            grid=row_tiles.shape,
+            in_specs=in_specs,
+            out_specs=pl.BlockSpec(
+                (members, fields, ROW_TILE, columns), lambda i, tile: (0, 0, tile[i], 0)
             ),
-            pl.BlockSpec((ROW_TILE, columns), lambda i: (i, 0)),
-            whole(lhs1),
-            whole(lhs2),
-            whole(place),
-        ],
-        out_specs=pl.BlockSpec(
-            (members, fields, ROW_TILE, columns), lambda i: (0, 0, i, 0)
+            scratch_shapes=[
+                pltpu.VMEM((members, width), jnp.float32),
+                pltpu.VMEM((3 * members, width), jnp.bfloat16),
+                pltpu.VMEM((members, fields, ROW_TILE, LANES), jnp.float32),
+            ],
         ),
         out_shape=jax.ShapeDtypeStruct((members, fields, rows, columns), jnp.float32),
-        scratch_shapes=[
-            pltpu.VMEM((members, width), jnp.float32),
-            pltpu.VMEM((3 * members, width), jnp.bfloat16),
-            pltpu.VMEM((members, fields, ROW_TILE, LANES), jnp.float32),
-        ],
+        input_output_aliases=aliases,
         compiler_params=params(),
         name="update",
-    )(start, counts, state, cutoff, lhs1, lhs2, place)
-
-
-def row_halos(block, axis):
+    )(*operands)
+
+
+def row_halos(ensemble, depth, axis):
     size = lax.axis_size(axis)
-    onward = [(i, (i + 1) % size) for i in range(size)]
-    backward = [(j, i) for i, j in onward]
-    rows = block.shape[-2]
-    last = lax.slice_in_dim(block, rows - HALO, rows, axis=block.ndim - 2)
-    leading = lax.slice_in_dim(block, 0, HALO, axis=block.ndim - 2)
-    return lax.ppermute(last, axis, onward), lax.ppermute(leading, axis, backward)
+    odd = lax.axis_index(axis) % 2 == 1
+    columns = depth.shape[1]
+
+    def edge(start):
+        return jnp.concatenate(
+            [
+                ensemble[:, :, start : start + HALO].reshape(-1, HALO, columns),
+                depth[None, start : start + HALO],
+            ],
+            0,
+        )
+
+    first, last = edge(0), edge(depth.shape[0] - HALO)
+    far = [(i, (i + (1 if i % 2 else -1)) % size) for i in range(size)]
+    return (
+        exchange(jnp.where(odd, first, last), axis, 1),
+        lax.ppermute(jnp.where(odd, last, first), axis, far),
+    )
 
 
 def local(ensemble, sea_depth, cutoff, obs_index, obs_value, obs_var):
     blocks = lax.axis_size("mem")
-    members, fields, rows, size_y = ensemble.shape
+    subs = lax.axis_size("sub")
+    local_members, fields, rows, size_y = ensemble.shape
+    members = local_members * blocks
     col_block = size_y // blocks
-    size_x = rows * lax.axis_size("sub")
+    size_x = rows * subs
     sizes = (size_x, size_y)
-    x_start = lax.axis_index("sub") * rows
-    y_start = lax.axis_index("mem") * col_block
-    start = jnp.stack([x_start, y_start]).astype(jnp.int32)
+    sub, mem = lax.axis_index("sub"), lax.axis_index("mem")
+    odd = sub % 2
+    x_start = sub * rows
+    y_start = mem * col_block
+    start = jnp.stack([x_start, y_start, sub, mem]).astype(jnp.int32)
+    parity = odd.astype(jnp.int32)[None]
     obs_x = obs_index // size_y
     obs_y = obs_index % size_y
-    flat_x = obs_x.reshape(-1)
-    flat_y = obs_y.reshape(-1)
-
-    up, down = row_halos(ensemble, "sub")
-    depth_up, depth_down = row_halos(sea_depth, "sub")
-    depth = jnp.concatenate([depth_up, sea_depth, depth_down], 0)
-    sent = forecast(ensemble, up, down, depth, blocks)
-
-    radius_part = pick_radius(cutoff, flat_x, flat_y, x_start, y_start)
-    heights_part = pick_heights(sent, flat_x, flat_y, x_start)
-    part = jnp.concatenate([heights_part, radius_part[None, :]], 0)
-    part = jnp.pad(part, ((0, -part.shape[0] % 8), (0, 0)))
-    every = gather_over(sum_over(part, "sub")[None], "mem")
-    heights = every[:, :members].reshape(blocks * members, -1)
-    radius_sq = jnp.sum(every[:, members], 0)[None, :]
-
-    received = lax.all_to_all(sent, "mem", split_axis=0, concat_axis=0, tiled=True)
-    state = received.reshape((blocks * members,) + received.shape[2:])
+    flat_x = obs_x.reshape(1, -1)
+    flat_y = obs_y.reshape(1, -1)
+
+    near_halo, far_halo = row_halos(ensemble, sea_depth, "sub")
+    radius_part = pick_radius(cutoff, flat_x[0], flat_y[0], x_start, y_start)[None]
+    near_first = jnp.where(odd == 1, 0, HALO)
+    far_first = jnp.where(odd == 1, rows - HALO, 0)
+
+    sent_near = forecast(
+        near_kernel, "near", rows - HALO, parity, ensemble, near_halo, sea_depth, blocks
+    )
+    received_near = lax.all_to_all(sent_near, "mem", split_axis=0, concat_axis=0, tiled=True)
+    near_heights = pick_near(flat_x - x_start - near_first, flat_y, sent_near)
+
+    sent_far = forecast(far_kernel, "far", HALO, parity, ensemble, far_halo, sea_depth, blocks)
+    part = pick_far(
+        flat_x - x_start - far_first, flat_y, sent_far, near_heights, radius_part, subs
+    )
+    piece = lax.dynamic_index_in_dim(sum_over(part, "sub"), sub, 0, keepdims=True)
+    every = gather_over(gather_over(piece, "mem")[None], "sub")
     lhs1, lhs2, place, counts = chain(
-        start, heights, radius_sq, obs_x, obs_y, obs_value, obs_var, cutoff, sizes
+        members, start, every, obs_x, obs_y, obs_value, obs_var, cutoff, sizes
     )
-    return update(start, counts, state, cutoff, lhs1, lhs2, place, sizes)
+    received_far = lax.all_to_all(sent_far, "mem", split_axis=0, concat_axis=0, tiled=True)
+
+    def analyse(received, row_tiles, begun=None):
+        state = received.reshape((members,) + received.shape[2:])
+        return update(
+            row_tiles, start, counts, state, cutoff, lhs1, lhs2, place, sizes, begun
+        )
+
+    near_tiles = near_first // ROW_TILE + jnp.arange(rows // ROW_TILE - 1, dtype=jnp.int32)
+    far_tiles = (far_first // ROW_TILE).astype(jnp.int32)[None]
+    return analyse(received_far, far_tiles, analyse(received_near, near_tiles))
 
 
 def solution(mesh):

time: 167 us -> 152 us (0.910)
  waiting for transfers between devices: 76.2 us -> 63 us
  local copies, waits for them, and re-layouts: 9.49 us -> 3.51 us
  starting transfers between devices: 19.1 us -> 22.2 us
  Pallas kernels: 58.2 us -> 60.9 us
    ppermute x5 -> x8, waiting for transfers between devices: 57.8 us -> 16.8 us  [exchange(): return lax.ppermute(value, axis, [(i, i ^ distance) for i in range(size)])]
    all_to_all x1 -> x2, waiting for transfers between devices: 0.01 us -> 25.8 us  [the longest x1 25.8 us: local(): lax.all_to_all(sent_near, 'mem', split_axis=0, concat_axis=0, tiled=True)]
    all_to_all x1 -> x2, starting transfers between devices: 5.94 us -> 11.3 us  [the longest x1 7.44 us: local(): lax.all_to_all(sent_near, 'mem', split_axis=0, concat_axis=0, tiled=True)]
    unnamed x28 -> x20, local copies, waits for them, and re-layouts: 6.24 us -> 0.95 us
    ppermute x4 -> x1, starting transfers between devices: 4.32 us -> 0.98 us  [row_halos(): lax.ppermute(jnp.where(odd, last, first), axis, far)]
    pallas_call x4 -> x7, Pallas kernels: 58.2 us -> 60.9 us  [the longest x2 24.2 us: update(): pl.pallas_call(functools.partial(update_kernel, sizes, begun is not None)...]
    ppermute x4 -> x1, waiting for transfers between devices: 18.5 us -> 20.5 us  [row_halos(): lax.ppermute(jnp.where(odd, last, first), axis, far)]
    ppermute x5 -> x8, starting transfers between devices: 8.86 us -> 9.93 us  [exchange(): return lax.ppermute(value, axis, [(i, i ^ distance) for i in range(size)])]
  transfers between devices with their start and end apart: 10 -> 11, of which waited for: 6 -> 10; matrix products, arithmetic and copies ran while one was open for 3% -> 1% of each run, Pallas kernels for 15% -> 29%
where the time goes in v3:
time: 152 us
  waiting for transfers between devices  63 us (41%)
  Pallas kernels  60.9 us (40%)
  starting transfers between devices  22.2 us (15%)
  local copies, waits for them, and re-layouts  3.51 us (2%)
    all_to_all x1, waiting for transfers between devices, local(): lax.all_to_all(sent_near, 'mem', split_axis=0, concat_axis=0, tiled=True)  25.8 us
    pallas_call x2, Pallas kernels, update(): pl.pallas_call(functools.partial(update_kernel, sizes, begun is not None)...  24.2 us
    ppermute x1, waiting for transfers between devices, row_halos(): lax.ppermute(jnp.where(odd, last, first), axis, far)  20.5 us
    pallas_call x1, Pallas kernels, chain(): pl.pallas_call(functools.partial(chain_kernel, members, sizes), in_specs=...  17.1 us
    ppermute x8, waiting for transfers between devices, exchange(): return lax.ppermute(value, axis, [(i, i ^ distance) for i in range(size)])  16.8 us
    pallas_call x2, Pallas kernels, forecast(): pl.pallas_call(kernel, grid=(members,), in_specs=smem() + [pl.BlockSpec((...  16.1 us
    ppermute x8, starting transfers between devices, exchange(): return lax.ppermute(value, axis, [(i, i ^ distance) for i in range(size)])  9.93 us
    all_to_all x1, starting transfers between devices, local(): lax.all_to_all(sent_near, 'mem', split_axis=0, concat_axis=0, tiled=True)  7.44 us
  transfers between devices with their start and end apart: 11, of which 10 were waited for; matrix products, arithmetic and copies ran while one was open for 1% of the time, Pallas kernels for 29%

profile of v3, /device:TPU:0, one launch (start us, length us, event | category | flops | bytes accessed | tf_op | source)
XLA Modules:
  0.0 151.9 jit_solution(15555704038370483341)
XLA Ops:
  0.0 0.9 slice_bitcast_fusion.1
  0.9 0.0 copy-start.3
  0.9 1.6 %fusion.7 = (f32[4,3,8,2048]{3,2,1,0:T(8,128)S(1)}, f32[4,3,8,2048]{3,2,1,0:T(8,128)S(1)}) fusion(f32[4,3,32,2048]{3,2,1,0:T(8,128)} %ens_ref.3), kind=kLoop, calls=%fused_computation.35 | loop fusion | bytes 3145728 | tf_op jit(solution)/shard_map/slice | solution.py:539
  2.5 1.1 fusion.1
  3.5 0.5 collective-permute-start.1
  4.0 2.0 %collective-permute-done.1.halo_ref.depth_halo_ref = f32[13,8,2048]{2,1,0:T(8,128)S(1)} collective-permute-done((f32[13,8,2048]{2,1,0:T(8,128)S(1)}, f32[13,8,2048]{2,1,0:T(8,128)S(1)}, u32[]{:S(2)}, u32[]{:S(2)}) %collective-permute-start.1) | collective-permute-done | bytes 852000 | tf_op jit(solution)/shard_map/ppermute | solution.py:226
  6.0 0.0 copy-done.3
  6.0 10.0 %near.1.height_ref = f32[8,4,3,2,24,128]{5,4,3,2,1,0:T(8,128)} custom-call(s32[1]{0:T(128)} %bitcast.5.parity_ref, f32[4,3,32,2048]{3,2,1,0:T(8,128)} %ens_ref.3, f32[13,8,2048]{2,1,0:T(8,128)S(1)} %collective-permute-done.1.halo_ref.depth_halo_ref, f32[32,2048]{1,0:T(8,128)S(1)} %copy-done.3, f32[13,8,2048]{2,1,0:T(8,128)S(1)} %collective-permute-done.1.halo_ref.depth_halo_ref), custom_call_target="tpu_custom_call" | custom-call | tf_op jit(solution)/shard_map/near/pallas_call | solution.py:103
  16.0 0.0 copy-start.7
  16.0 0.0 copy-start
  16.0 7.4 %all-to-all-start.1 = ((f32[8,4,3,2,24,128]{5,4,3,2,1,0:T(8,128)}), f32[8,4,3,2,24,128]{5,4,3,2,1,0:T(8,128)}, u32[]{:S(2)}, u32[]{:S(2)}) async-start(f32[8,4,3,2,24,128]{5,4,3,2,1,0:T(8,128)} %near.1.height_ref), calls=%async_computation.1 | async-start | bytes 4718592 | tf_op jit(solution)/shard_map/all_to_all | solution.py:580
  23.5 1.0 collective-permute-start
  24.4 0.0 copy-done.7
  24.5 0.0 copy-start.4
  24.5 20.5 %collective-permute-done.halo_ref.depth_halo_ref = f32[13,8,2048]{2,1,0:T(8,128)} collective-permute-done((f32[13,8,2048]{2,1,0:T(8,128)}, f32[13,8,2048]{2,1,0:T(8,128)}, u32[]{:S(2)}, u32[]{:S(2)}) %collective-permute-start) | collective-permute-done | bytes 852000 | tf_op jit(solution)/shard_map/ppermute | solution.py:549
  44.9 0.0 copy-done
  44.9 6.1 %far.1.height_ref = f32[8,4,3,2,8,128]{5,4,3,2,1,0:T(8,128)S(1)} custom-call(s32[1]{0:T(128)} %bitcast.5.parity_ref, f32[4,3,32,2048]{3,2,1,0:T(8,128)S(1)} %copy-done, f32[13,8,2048]{2,1,0:T(8,128)} %collective-permute-done.halo_ref.depth_halo_ref, f32[32,2048]{1,0:T(8,128)S(1)} %copy-done.3, f32[13,8,2048]{2,1,0:T(8,128)} %collective-permute-done.halo_ref.depth_halo_ref), custom_call_target="tpu_custom_call" | custom-call | tf_op jit(solution)/shard_map/far/pallas_call | solution.py:103
  51.1 0.0 copy-start.1
  51.1 0.9 copy-done.1
  52.0 25.8 %all-to-all-done.1 = f32[8,4,3,2,24,128]{5,4,3,2,1,0:T(8,128)} async-done(((f32[8,4,3,2,24,128]{5,4,3,2,1,0:T(8,128)}), f32[8,4,3,2,24,128]{5,4,3,2,1,0:T(8,128)}, u32[]{:S(2)}, u32[]{:S(2)}) %all-to-all-start.1) | async-done | bytes 2359328 | tf_op jit(solution)/shard_map/all_to_all | solution.py:580
  77.7 0.0 copy-start.2
  77.7 3.9 %all-to-all-start = ((f32[8,4,3,2,8,128]{5,4,3,2,1,0:T(8,128)}), f32[8,4,3,2,8,128]{5,4,3,2,1,0:T(8,128)S(1)}, u32[]{:S(2)}, u32[]{:S(2)}) async-start(f32[8,4,3,2,8,128]{5,4,3,2,1,0:T(8,128)} %copy-done.1), calls=%async_computation | async-start | bytes 1572864 | tf_op jit(solution)/shard_map/all_to_all | solution.py:592
  81.6 0.0 copy-start.5
  81.6 0.0 copy-start.6
  81.7 0.0 copy-done.4
  81.7 0.8 fusion
  82.5 2.6 %pick_near.1.near_ref = f32[4,1024]{1,0:T(4,128)S(1)} custom-call(s32[1,1024]{1,0:T(1,128)S(1)} %get-tuple-element.23.row_ref, s32[1,1024]{1,0:T(1,128)S(1)} %bitcast.32, f32[8,4,3,2,24,128]{5,4,3,2,1,0:T(8,128)} %near.1.height_ref), custom_call_target="tpu_custom_call" | custom-call | tf_op jit(solution)/shard_map/pick_near/pallas_call | solution.py:183
  85.1 0.0 copy-done.2
  85.1 0.9 pick_far.1
  86.0 0.1 collective-permute-start.2
  86.1 1.2 collective-permute-done.2
  87.3 1.5 collective-permute-start.3
  88.8 2.4 %collective-permute-done.3 = f32[4,16,128]{2,1,0:T(8,128)S(1)} collective-permute-done((f32[4,16,128]{2,1,0:T(8,128)S(1)}, f32[4,16,128]{2,1,0:T(8,128)S(1)}, u32[]{:S(2)}, u32[]{:S(2)}) %collective-permute-start.3) | collective-permute-done | bytes 32800 | tf_op jit(solution)/shard_map/ppermute | solution.py:226
  91.2 1.9 %collective-permute-start.4 = (f32[1,16,128]{2,1,0:T(8,128)S(1)}, f32[1,16,128]{2,1,0:T(8,128)S(1)}, u32[]{:S(2)}, u32[]{:S(2)}) collective-permute-start(f32[1,16,128]{2,1,0:T(8,128)S(1)} %dynamic-slice_add_fusion), channel_id=1, source_target_pairs={{0,4},{4,0},{8,12},{12,8},{16,20},{20,16},{24,28},{28,24},{1,5},{5... | collective-permute-start | bytes 24584 | tf_op jit(solution)/shard_map/ppermute | solution.py:226
  93.1 1.8 %collective-permute-done.4 = f32[1,16,128]{2,1,0:T(8,128)S(1)} collective-permute-done((f32[1,16,128]{2,1,0:T(8,128)S(1)}, f32[1,16,128]{2,1,0:T(8,128)S(1)}, u32[]{:S(2)}, u32[]{:S(2)}) %collective-permute-start.4) | collective-permute-done | bytes 8224 | tf_op jit(solution)/shard_map/ppermute | solution.py:226
  95.0 1.8 %collective-permute-start.5 = (f32[2,16,128]{2,1,0:T(8,128)S(1)}, f32[2,16,128]{2,1,0:T(8,128)S(1)}, u32[]{:S(2)}, u32[]{:S(2)}) collective-permute-start(f32[2,16,128]{2,1,0:T(8,128)S(1)} %pad_maximum_fusion.5), channel_id=1, source_target_pairs={{0,8},{4,12},{8,0},{12,4},{16,24},{20,28},{24,16},{28,20},{1,9},{5... | collective-permute-start | bytes 49160 | tf_op jit(solution)/shard_map/ppermute | solution.py:226
  96.8 2.1 %collective-permute-done.5 = f32[2,16,128]{2,1,0:T(8,128)S(1)} collective-permute-done((f32[2,16,128]{2,1,0:T(8,128)S(1)}, f32[2,16,128]{2,1,0:T(8,128)S(1)}, u32[]{:S(2)}, u32[]{:S(2)}) %collective-permute-start.5) | collective-permute-done | bytes 16416 | tf_op jit(solution)/shard_map/ppermute | solution.py:226
  98.9 2.6 %collective-permute-start.6 = (f32[4,16,128]{2,1,0:T(8,128)S(1)}, f32[4,16,128]{2,1,0:T(8,128)S(1)}, u32[]{:S(2)}, u32[]{:S(2)}) collective-permute-start(f32[4,16,128]{2,1,0:T(8,128)S(1)} %pad_maximum_fusion.4), channel_id=1, source_target_pairs={{0,16},{4,20},{8,24},{12,28},{16,0},{20,4},{24,8},{28,12},{1,17},{... | collective-permute-start | bytes 98312 | tf_op jit(solution)/shard_map/ppermute | solution.py:226
  101.4 2.2 %collective-permute-done.6 = f32[4,16,128]{2,1,0:T(8,128)S(1)} collective-permute-done((f32[4,16,128]{2,1,0:T(8,128)S(1)}, f32[4,16,128]{2,1,0:T(8,128)S(1)}, u32[]{:S(2)}, u32[]{:S(2)}) %collective-permute-start.6) | collective-permute-done | bytes 32800 | tf_op jit(solution)/shard_map/ppermute | solution.py:226
  103.7 0.0 collective-permute-start.7
  103.7 1.2 collective-permute-done.7
  104.9 1.6 %collective-permute-start.8 = (f32[2,8,16,128]{3,2,1,0:T(8,128)S(1)}, f32[2,8,16,128]{3,2,1,0:T(8,128)S(1)}, u32[]{:S(2)}, u32[]{:S(2)}) collective-permute-start(f32[2,8,16,128]{3,2,1,0:T(8,128)S(1)} %pad_maximum_fusion.3), channel_id=1, source_target_pairs={{0,2},{1,3},{2,0},{3,1},{4,6},{5,7},{6,4},{7,5},{8,10},{9,11},{10,... | collective-permute-start | bytes 393224 | tf_op jit(solution)/shard_map/ppermute | solution.py:226
  106.5 0.1 pad_add_fusion.2.start_ref
  106.6 0.1 copy.26
  106.8 3.8 %collective-permute-done.8 = f32[2,8,16,128]{3,2,1,0:T(8,128)S(1)} collective-permute-done((f32[2,8,16,128]{3,2,1,0:T(8,128)S(1)}, f32[2,8,16,128]{3,2,1,0:T(8,128)S(1)}, u32[]{:S(2)}, u32[]{:S(2)}) %collective-permute-start.8) | collective-permute-done | bytes 131104 | tf_op jit(solution)/shard_map/ppermute | solution.py:226
  110.6 0.0 copy-done.5
  110.6 0.0 copy-done.6
  110.6 17.1 %chain.1 = (bf16[4,256,96]{2,1,0:T(8,128)(2,1)S(1)}, bf16[4,4,32,192]{3,2,1,0:T(8,128)(2,1)S(1)}, f32[4,256,256]{2,1,0:T(8,128)S(1)}, s32[4]{0:T(128)S(1)}) custom-call(s32[4]{0:T(128)S(1)} %pad_add_fusion.2.start_ref, f32[4,8,16,128]{3,2,1,0:T(8,128)S(1)} %pad_maximum_fusion.2.every_ref, s32[2,1024]{1,0:T(2,128)S(1)} %pad_add_fusion.row_ref, ...), custom_call_target="tpu_custom_call" | custom-call | tf_op jit(solution)/shard_map/chain/pallas_call | solution.py:391
  127.7 17.8 %update.2.rest_0_ = f32[32,3,32,256]{3,2,1,0:T(8,128)} custom-call(s32[3]{0:T(128)S(1)} %iota_add_fusion.tile_ref, s32[4]{0:T(128)S(1)} %pad_add_fusion.2.start_ref, s32[4]{0:T(128)S(1)} %get-tuple-element.9.count_ref, f32[32,3,2,24,128]{4,3,2,1,0:T(8,128)} %bitcast.14.state_ref, s32[32,256]{1,0:T(8,128)S(1)} %copy-done.4, ...), custom_call_target="tpu_custom_call" | custom-call | tf_op jit(solution)/shard_map/update/pallas_call | solution.py:509
  145.4 0.0 all-to-all-done
  145.4 6.4 %update.3 = f32[32,3,32,256]{3,2,1,0:T(8,128)} custom-call(s32[1]{0:T(128)} %bitcast.tile_ref, s32[4]{0:T(128)S(1)} %pad_add_fusion.2.start_ref, s32[4]{0:T(128)S(1)} %get-tuple-element.9.count_ref, f32[32,3,2,8,128]{4,3,2,1,0:T(8,128)S(1)} %bitcast.30, s32[32,256]{1,0:T(8,128)S(1)} %copy-done.4, ...), custom_call_target="tpu_custom_call", output_to_operand_aliasing={{}: (8, {})} | custom-call | tf_op jit(solution)/shard_map/update/pallas_call | solution.py:509
  (16 shorter events, 0.1 us)
Async XLA Ops:
  0.9 5.1 %copy-start.3 = (f32[32,2048]{1,0:T(8,128)S(1)}, f32[32,2048]{1,0:T(8,128)}, u32[]{:S(2)}) copy-start(f32[32,2048]{1,0:T(8,128)} %depth_ref.3) | copy-start | bytes 786436
  3.5 2.5 %collective-permute-start.1 = (f32[13,8,2048]{2,1,0:T(8,128)S(1)}, f32[13,8,2048]{2,1,0:T(8,128)S(1)}, u32[]{:S(2)}, u32[]{:S(2)}) collective-permute-start(f32[13,8,2048]{2,1,0:T(8,128)S(1)} %get-tuple-element.19), channel_id=1, source_target_pairs={{0,1},{1,0},{2,3},{3,2},{4,5},{5,4},{6,7},{7,6},{8,9},{9,8},{10,11... | collective-permute-start | bytes 2555912 | tf_op jit(solution)/shard_map/ppermute | solution.py:226
  16.0 8.4 %copy-start.7 = (s32[4,256]{1,0:T(4,128)S(1)}, s32[4,256]{1,0:T(4,128)}, u32[]{:S(2)}) copy-start(s32[4,256]{1,0:T(4,128)} %param.9) | copy-start | bytes 12292
  16.0 28.9 %copy-start = (f32[4,3,32,2048]{3,2,1,0:T(8,128)S(1)}, f32[4,3,32,2048]{3,2,1,0:T(8,128)}, u32[]{:S(2)}) copy-start(f32[4,3,32,2048]{3,2,1,0:T(8,128)} %ens_ref.3) | copy-start | bytes 9437188
  16.0 61.7 %all-to-all-start.1 = ((f32[8,4,3,2,24,128]{5,4,3,2,1,0:T(8,128)}), f32[8,4,3,2,24,128]{5,4,3,2,1,0:T(8,128)}, u32[]{:S(2)}, u32[]{:S(2)}) async-start(f32[8,4,3,2,24,128]{5,4,3,2,1,0:T(8,128)} %near.1.height_ref), calls=%async_computation.1 | async-start | bytes 4718592 | tf_op jit(solution)/shard_map/all_to_all | solution.py:580
  23.5 21.5 %collective-permute-start = (f32[13,8,2048]{2,1,0:T(8,128)}, f32[13,8,2048]{2,1,0:T(8,128)}, u32[]{:S(2)}, u32[]{:S(2)}) collective-permute-start(f32[13,8,2048]{2,1,0:T(8,128)} %get-tuple-element.20), channel_id=1, source_target_pairs={{0,3},{1,2},{2,1},{3,0},{4,7},{5,6},{6,5},{7,4},{8,11},{9,10},{10,... | collective-permute-start | bytes 2555912 | tf_op jit(solution)/shard_map/ppermute | solution.py:549
  24.5 57.2 %copy-start.4 = (s32[32,256]{1,0:T(8,128)S(1)}, s32[32,256]{1,0:T(8,128)}, u32[]{:S(2)}) copy-start(s32[32,256]{1,0:T(8,128)} %cutoff_ref.5) | copy-start | bytes 98308
  51.1 0.9 copy-start.1
  77.7 7.4 %copy-start.2 = (f32[8,4,3,2,8,128]{5,4,3,2,1,0:T(8,128)S(1)}, f32[8,4,3,2,8,128]{5,4,3,2,1,0:T(8,128)}, u32[]{:S(2)}) copy-start(f32[8,4,3,2,8,128]{5,4,3,2,1,0:T(8,128)} %copy-done.1) | copy-start | bytes 2359300
  77.7 67.7 %all-to-all-start = ((f32[8,4,3,2,8,128]{5,4,3,2,1,0:T(8,128)}), f32[8,4,3,2,8,128]{5,4,3,2,1,0:T(8,128)S(1)}, u32[]{:S(2)}, u32[]{:S(2)}) async-start(f32[8,4,3,2,8,128]{5,4,3,2,1,0:T(8,128)} %copy-done.1), calls=%async_computation | async-start | bytes 1572864 | tf_op jit(solution)/shard_map/all_to_all | solution.py:592
  81.6 29.0 %copy-start.5 = (f32[4,256]{1,0:T(4,128)S(1)}, f32[4,256]{1,0:T(4,128)}, u32[]{:S(2)}) copy-start(f32[4,256]{1,0:T(4,128)} %value_ref.1) | copy-start | bytes 12292
  81.6 29.0 %copy-start.6 = (f32[4,256]{1,0:T(4,128)S(1)}, f32[4,256]{1,0:T(4,128)}, u32[]{:S(2)}) copy-start(f32[4,256]{1,0:T(4,128)} %variance_ref.1) | copy-start | bytes 12292
  86.0 1.3 collective-permute-start.2
  87.3 3.9 %collective-permute-start.3 = (f32[4,16,128]{2,1,0:T(8,128)S(1)}, f32[4,16,128]{2,1,0:T(8,128)S(1)}, u32[]{:S(2)}, u32[]{:S(2)}) collective-permute-start(f32[4,16,128]{2,1,0:T(8,128)S(1)} %add.32), channel_id=1, source_target_pairs={{0,2},{1,3},{2,0},{3,1},{4,6},{5,7},{6,4},{7,5},{8,10},{9,11},{10,... | collective-permute-start | bytes 98312 | tf_op jit(solution)/shard_map/ppermute | solution.py:226
  91.2 3.7 %collective-permute-start.4 = (f32[1,16,128]{2,1,0:T(8,128)S(1)}, f32[1,16,128]{2,1,0:T(8,128)S(1)}, u32[]{:S(2)}, u32[]{:S(2)}) collective-permute-start(f32[1,16,128]{2,1,0:T(8,128)S(1)} %dynamic-slice_add_fusion), channel_id=1, source_target_pairs={{0,4},{4,0},{8,12},{12,8},{16,20},{20,16},{24,28},{28,24},{1,5},{5... | collective-permute-start | bytes 24584 | tf_op jit(solution)/shard_map/ppermute | solution.py:226
  95.0 3.9 %collective-permute-start.5 = (f32[2,16,128]{2,1,0:T(8,128)S(1)}, f32[2,16,128]{2,1,0:T(8,128)S(1)}, u32[]{:S(2)}, u32[]{:S(2)}) collective-permute-start(f32[2,16,128]{2,1,0:T(8,128)S(1)} %pad_maximum_fusion.5), channel_id=1, source_target_pairs={{0,8},{4,12},{8,0},{12,4},{16,24},{20,28},{24,16},{28,20},{1,9},{5... | collective-permute-start | bytes 49160 | tf_op jit(solution)/shard_map/ppermute | solution.py:226
  98.9 4.8 %collective-permute-start.6 = (f32[4,16,128]{2,1,0:T(8,128)S(1)}, f32[4,16,128]{2,1,0:T(8,128)S(1)}, u32[]{:S(2)}, u32[]{:S(2)}) collective-permute-start(f32[4,16,128]{2,1,0:T(8,128)S(1)} %pad_maximum_fusion.4), channel_id=1, source_target_pairs={{0,16},{4,20},{8,24},{12,28},{16,0},{20,4},{24,8},{28,12},{1,17},{... | collective-permute-start | bytes 98312 | tf_op jit(solution)/shard_map/ppermute | solution.py:226
  103.7 1.3 collective-permute-start.7
  104.9 5.6 %collective-permute-start.8 = (f32[2,8,16,128]{3,2,1,0:T(8,128)S(1)}, f32[2,8,16,128]{3,2,1,0:T(8,128)S(1)}, u32[]{:S(2)}, u32[]{:S(2)}) collective-permute-start(f32[2,8,16,128]{3,2,1,0:T(8,128)S(1)} %pad_maximum_fusion.3), channel_id=1, source_target_pairs={{0,2},{1,3},{2,0},{3,1},{4,6},{5,7},{6,4},{7,5},{8,10},{9,11},{10,... | collective-permute-start | bytes 393224 | tf_op jit(solution)/shard_map/ppermute | solution.py:226

commit v4 on v3

--- a/solution.py
+++ b/solution.py
@@ -13,6 +13,7 @@
 OBS_BLOCK = 64
 ROW_TILE = 8
 VMEM_LIMIT = 48 * 2**20
+CHAIN_COST = pl.CostEstimate(flops=26 * 10**9, bytes_accessed=85 * 10**6, transcendentals=0)
 
 step_size = 0.3
 coriolis = 0.2
@@ -248,6 +249,48 @@
     return gap * gap
 
 
+def eliminate_four(system, k, row_id):
+    width = system.shape[1]
+    row = [system[k + i : k + i + 1, :] for i in range(4)]
+    p = [
+        [jnp.broadcast_to(row[i][:, k + j : k + j + 1], (1, LANES)) for j in range(4)]
+        for i in range(4)
+    ]
+
+    def wide(value):
+        return jnp.concatenate([value] * (width // LANES), 1)
+
+    def inverse(a00, a01, a10, a11):
+        scale = 1.0 / (a00 * a11 - a01 * a10)
+        return a11 * scale, -a01 * scale, -a10 * scale, a00 * scale
+
+    i00, i01, i10, i11 = inverse(p[0][0], p[0][1], p[1][0], p[1][1])
+    y = [
+        [i00 * p[0][2 + j] + i01 * p[1][2 + j] for j in range(2)],
+        [i10 * p[0][2 + j] + i11 * p[1][2 + j] for j in range(2)],
+    ]
+    schur = [
+        [p[2 + i][2 + j] - p[2 + i][0] * y[0][j] - p[2 + i][1] * y[1][j] for j in range(2)]
+        for i in range(2)
+    ]
+    s00, s01, s10, s11 = inverse(schur[0][0], schur[0][1], schur[1][0], schur[1][1])
+    top0 = wide(i00) * row[0] + wide(i01) * row[1]
+    top1 = wide(i10) * row[0] + wide(i11) * row[1]
+    low0 = row[2] - wide(p[2][0]) * top0 - wide(p[2][1]) * top1
+    low1 = row[3] - wide(p[3][0]) * top0 - wide(p[3][1]) * top1
+    new2 = wide(s00) * low0 + wide(s01) * low1
+    new3 = wide(s10) * low0 + wide(s11) * low1
+    new0 = top0 - wide(y[0][0]) * new2 - wide(y[0][1]) * new3
+    new1 = top1 - wide(y[1][0]) * new2 - wide(y[1][1]) * new3
+    new = (new0, new1, new2, new3)
+    result = system
+    for i in range(4):
+        result = result - system[:, k + i : k + i + 1] * new[i]
+    for i in range(4):
+        result = jnp.where(row_id == k + i, new[i], result)
+    return result
+
+
 def chain_kernel(
     members,
     sizes,
@@ -316,11 +359,8 @@
         system = jnp.concatenate(
             [inner, proj, jnp.zeros((members, LANES - members - 1), jnp.float32), scaled], 1
         )
-        for k in range(members):
-            pivot_row = system[k : k + 1, :] / system[k : k + 1, k : k + 1]
-            system = jnp.where(
-                member_row == k, pivot_row, system - system[:, k : k + 1] * pivot_row
-            )
+        for k in range(0, members, 4):
+            system = eliminate_four(system, k, member_row)
         solved_proj = system[:, members : members + 1]
         solved_anom = system[:, LANES:]
         solved_innov = precision * (
@@ -401,6 +441,7 @@
             jax.ShapeDtypeStruct((batches,), jnp.int32),
         ],
         compiler_params=params(),
+        cost_estimate=CHAIN_COST,
         name="chain",
     )(start, every, row_form, col_form, values, variance, cutoff)
 
@@ -589,6 +630,7 @@
     lhs1, lhs2, place, counts = chain(
         members, start, every, obs_x, obs_y, obs_value, obs_var, cutoff, sizes
     )
+    lhs1, sent_far = lax.optimization_barrier((lhs1, sent_far))
     received_far = lax.all_to_all(sent_far, "mem", split_axis=0, concat_axis=0, tiled=True)
 
     def analyse(received, row_tiles, begun=None):

time: 152 us -> 127 us (0.84)
  waiting for transfers between devices: 63 us -> 41.3 us
  Pallas kernels: 60.9 us -> 55.9 us
  starting transfers between devices: 22.2 us -> 24.3 us
    all_to_all x1, waiting for transfers between devices: 25.8 us -> 0.01 us  [local(): lax.all_to_all(sent_near, 'mem', split_axis=0, concat_axis=0, tiled=True)]
    ppermute x8, waiting for transfers between devices: 16.8 us -> 39.3 us  [exchange(): return lax.ppermute(value, axis, [(i, i ^ distance) for i in range(size)])]
    ppermute x1, waiting for transfers between devices: 20.5 us -> 0.01 us  [row_halos(): lax.ppermute(jnp.where(odd, last, first), axis, far)]
    pallas_call x1, Pallas kernels: 17.1 us -> 10.7 us  [chain(): pl.pallas_call(functools.partial(chain_kernel, members, sizes), in_specs=...]
    all_to_all x1, waiting for transfers between devices: 0.01 us -> 2.02 us  [local(): lax.all_to_all(sent_far, 'mem', split_axis=0, concat_axis=0, tiled=True)]
    ppermute x1, starting transfers between devices: 0.98 us -> 2.63 us  [row_halos(): lax.ppermute(jnp.where(odd, last, first), axis, far)]
  transfers between devices with their start and end apart: 11 -> 11, of which waited for: 10 -> 8; matrix products, arithmetic and copies ran while one was open for 1% -> 1% of each run, Pallas kernels for 29% -> 39%
where the time goes in v4:
time: 127 us; the launch traced here: 126 us
  Pallas kernels  55.9 us (44%)
  waiting for transfers between devices  41.3 us (33%)
  starting transfers between devices  24.3 us (19%)
  local copies, waits for them, and re-layouts  2.61 us (2%)
    ppermute x8, waiting for transfers between devices, exchange(): return lax.ppermute(value, axis, [(i, i ^ distance) for i in range(size)])  39.3 us
    pallas_call x2, Pallas kernels, update(): pl.pallas_call(functools.partial(update_kernel, sizes, begun is not None)...  24 us
    pallas_call x2, Pallas kernels, forecast(): pl.pallas_call(kernel, grid=(members,), in_specs=smem() + [pl.BlockSpec((...  16.8 us
    ppermute x8, starting transfers between devices, exchange(): return lax.ppermute(value, axis, [(i, i ^ distance) for i in range(size)])  11.1 us
    pallas_call x1, Pallas kernels, chain(): pl.pallas_call(functools.partial(chain_kernel, members, sizes), in_specs=...  10.7 us
    all_to_all x1, starting transfers between devices, local(): lax.all_to_all(sent_near, 'mem', split_axis=0, concat_axis=0, tiled=True)  6.81 us
    all_to_all x1, starting transfers between devices, local(): lax.all_to_all(sent_far, 'mem', split_axis=0, concat_axis=0, tiled=True)  3.78 us
    ppermute x1, starting transfers between devices, row_halos(): lax.ppermute(jnp.where(odd, last, first), axis, far)  2.63 us
  transfers between devices with their start and end apart: 11, of which 8 were waited for; matrix products, arithmetic and copies ran while one was open for 1% of the time, Pallas kernels for 39%

profile of v4, /device:TPU:0, one launch (start us, length us, event | category | flops | bytes accessed | tf_op | source)
XLA Modules:
  0.0 126.5 jit_solution(9885875304541749759)
XLA Ops:
  0.0 0.9 slice_bitcast_fusion.1
  0.9 0.0 copy-start.1
  0.9 1.6 %fusion.7 = (f32[4,3,8,2048]{3,2,1,0:T(8,128)S(1)}, f32[4,3,8,2048]{3,2,1,0:T(8,128)S(1)}) fusion(f32[4,3,32,2048]{3,2,1,0:T(8,128)} %ens_ref.3), kind=kLoop, calls=%fused_computation.35 | loop fusion | bytes 3145728 | tf_op jit(solution)/shard_map/slice | solution.py:580
  2.5 1.1 fusion.1
  3.5 0.5 collective-permute-start.1
  4.0 2.6 %collective-permute-start = (f32[13,8,2048]{2,1,0:T(8,128)}, f32[13,8,2048]{2,1,0:T(8,128)}, u32[]{:S(2)}, u32[]{:S(2)}) collective-permute-start(f32[13,8,2048]{2,1,0:T(8,128)} %get-tuple-element.24), channel_id=1, source_target_pairs={{0,3},{1,2},{2,1},{3,0},{4,7},{5,6},{6,5},{7,4},{8,11},{9,10},{10,... | collective-permute-start | bytes 2555912 | tf_op jit(solution)/shard_map/ppermute | solution.py:590
  6.6 0.0 collective-permute-done.1.halo_ref.depth_halo_ref
  6.6 0.0 copy-done.1
  6.6 10.0 %near.1.height_ref = f32[8,4,3,2,24,128]{5,4,3,2,1,0:T(8,128)} custom-call(s32[1]{0:T(128)} %bitcast.5.parity_ref, f32[4,3,32,2048]{3,2,1,0:T(8,128)} %ens_ref.3, f32[13,8,2048]{2,1,0:T(8,128)S(1)} %collective-permute-done.1.halo_ref.depth_halo_ref, f32[32,2048]{1,0:T(8,128)S(1)} %copy-done.1, f32[13,8,2048]{2,1,0:T(8,128)S(1)} %collective-permute-done.1.halo_ref.depth_halo_ref), custom_call_target="tpu_custom_call" | custom-call | tf_op jit(solution)/shard_map/near/pallas_call | solution.py:104
  16.6 0.0 copy-start.5
  16.6 0.0 copy-start.2
  16.6 0.0 copy-start
  16.6 6.8 %all-to-all-start.1 = ((f32[8,4,3,2,24,128]{5,4,3,2,1,0:T(8,128)}), f32[8,4,3,2,24,128]{5,4,3,2,1,0:T(8,128)}, u32[]{:S(2)}, u32[]{:S(2)}) async-start(f32[8,4,3,2,24,128]{5,4,3,2,1,0:T(8,128)} %near.1.height_ref), calls=%async_computation.1 | async-start | bytes 4718592 | tf_op jit(solution)/shard_map/all_to_all | solution.py:621
  23.4 0.0 copy-done.5
  23.5 0.0 copy-done.2
  23.5 0.8 fusion
  24.4 2.6 %pick_near.1.near_ref = f32[4,1024]{1,0:T(4,128)S(1)} custom-call(s32[1,1024]{1,0:T(1,128)S(1)} %get-tuple-element.27.row_ref, s32[1,1024]{1,0:T(1,128)S(1)} %bitcast.32, f32[8,4,3,2,24,128]{5,4,3,2,1,0:T(8,128)} %near.1.height_ref), custom_call_target="tpu_custom_call" | custom-call | tf_op jit(solution)/shard_map/pick_near/pallas_call | solution.py:184
  27.0 0.0 copy-start.3
  27.0 0.0 copy-start.4
  27.0 0.0 collective-permute-done.halo_ref.depth_halo_ref
  27.0 0.0 copy-done
  27.0 6.8 %far.1.height_ref = f32[8,4,3,2,8,128]{5,4,3,2,1,0:T(8,128)} custom-call(s32[1]{0:T(128)} %bitcast.5.parity_ref, f32[4,3,32,2048]{3,2,1,0:T(8,128)S(1)} %copy-done, f32[13,8,2048]{2,1,0:T(8,128)} %collective-permute-done.halo_ref.depth_halo_ref, f32[32,2048]{1,0:T(8,128)S(1)} %copy-done.1, f32[13,8,2048]{2,1,0:T(8,128)} %collective-permute-done.halo_ref.depth_halo_ref), custom_call_target="tpu_custom_call" | custom-call | tf_op jit(solution)/shard_map/far/pallas_call | solution.py:104
  33.8 1.8 %pick_far.1 = f32[4,16,128]{2,1,0:T(8,128)S(1)} custom-call(s32[1,1024]{1,0:T(1,128)S(1)} %get-tuple-element.28.row_ref, s32[1,1024]{1,0:T(1,128)S(1)} %bitcast.33, f32[8,4,3,2,8,128]{5,4,3,2,1,0:T(8,128)} %far.1.height_ref, f32[4,1024]{1,0:T(4,128)S(1)} %pick_near.1.near_ref, f32[1,1024]{1,0:T(1,128)S(1)} %bitcast.35), custom_call_target="tpu_custom_call" | custom-call | tf_op jit(solution)/shard_map/pick_far/pallas_call | solution.py:199
  35.6 0.1 collective-permute-start.2
  35.7 1.2 collective-permute-done.2
  36.9 1.5 %collective-permute-start.3 = (f32[4,16,128]{2,1,0:T(8,128)S(1)}, f32[4,16,128]{2,1,0:T(8,128)S(1)}, u32[]{:S(2)}, u32[]{:S(2)}) collective-permute-start(f32[4,16,128]{2,1,0:T(8,128)S(1)} %add.32), channel_id=1, source_target_pairs={{0,2},{1,3},{2,0},{3,1},{4,6},{5,7},{6,4},{7,5},{8,10},{9,11},{10,... | collective-permute-start | bytes 98312 | tf_op jit(solution)/shard_map/ppermute | solution.py:227
  38.5 2.4 %collective-permute-done.3 = f32[4,16,128]{2,1,0:T(8,128)S(1)} collective-permute-done((f32[4,16,128]{2,1,0:T(8,128)S(1)}, f32[4,16,128]{2,1,0:T(8,128)S(1)}, u32[]{:S(2)}, u32[]{:S(2)}) %collective-permute-start.3) | collective-permute-done | bytes 32800 | tf_op jit(solution)/shard_map/ppermute | solution.py:227
  40.8 2.0 %collective-permute-start.4 = (f32[1,16,128]{2,1,0:T(8,128)S(1)}, f32[1,16,128]{2,1,0:T(8,128)S(1)}, u32[]{:S(2)}, u32[]{:S(2)}) collective-permute-start(f32[1,16,128]{2,1,0:T(8,128)S(1)} %dynamic-slice_add_fusion), channel_id=1, source_target_pairs={{0,4},{4,0},{8,12},{12,8},{16,20},{20,16},{24,28},{28,24},{1,5},{5... | collective-permute-start | bytes 24584 | tf_op jit(solution)/shard_map/ppermute | solution.py:227
  42.9 1.6 %collective-permute-done.4 = f32[1,16,128]{2,1,0:T(8,128)S(1)} collective-permute-done((f32[1,16,128]{2,1,0:T(8,128)S(1)}, f32[1,16,128]{2,1,0:T(8,128)S(1)}, u32[]{:S(2)}, u32[]{:S(2)}) %collective-permute-start.4) | collective-permute-done | bytes 8224 | tf_op jit(solution)/shard_map/ppermute | solution.py:227
  44.5 2.0 %collective-permute-start.5 = (f32[2,16,128]{2,1,0:T(8,128)S(1)}, f32[2,16,128]{2,1,0:T(8,128)S(1)}, u32[]{:S(2)}, u32[]{:S(2)}) collective-permute-start(f32[2,16,128]{2,1,0:T(8,128)S(1)} %pad_maximum_fusion.5), channel_id=1, source_target_pairs={{0,8},{4,12},{8,0},{12,4},{16,24},{20,28},{24,16},{28,20},{1,9},{5... | collective-permute-start | bytes 49160 | tf_op jit(solution)/shard_map/ppermute | solution.py:227
  46.5 16.9 %collective-permute-done.5 = f32[2,16,128]{2,1,0:T(8,128)S(1)} collective-permute-done((f32[2,16,128]{2,1,0:T(8,128)S(1)}, f32[2,16,128]{2,1,0:T(8,128)S(1)}, u32[]{:S(2)}, u32[]{:S(2)}) %collective-permute-start.5) | collective-permute-done | bytes 16416 | tf_op jit(solution)/shard_map/ppermute | solution.py:227
  63.4 3.4 %collective-permute-start.6 = (f32[4,16,128]{2,1,0:T(8,128)S(1)}, f32[4,16,128]{2,1,0:T(8,128)S(1)}, u32[]{:S(2)}, u32[]{:S(2)}) collective-permute-start(f32[4,16,128]{2,1,0:T(8,128)S(1)} %pad_maximum_fusion.4), channel_id=1, source_target_pairs={{0,16},{4,20},{8,24},{12,28},{16,0},{20,4},{24,8},{28,12},{1,17},{... | collective-permute-start | bytes 98312 | tf_op jit(solution)/shard_map/ppermute | solution.py:227
  66.9 12.1 %collective-permute-done.6 = f32[4,16,128]{2,1,0:T(8,128)S(1)} collective-permute-done((f32[4,16,128]{2,1,0:T(8,128)S(1)}, f32[4,16,128]{2,1,0:T(8,128)S(1)}, u32[]{:S(2)}, u32[]{:S(2)}) %collective-permute-start.6) | collective-permute-done | bytes 32800 | tf_op jit(solution)/shard_map/ppermute | solution.py:227
  79.0 0.0 collective-permute-start.7
  79.0 1.2 collective-permute-done.7
  80.3 1.6 %collective-permute-start.8 = (f32[2,8,16,128]{3,2,1,0:T(8,128)S(1)}, f32[2,8,16,128]{3,2,1,0:T(8,128)S(1)}, u32[]{:S(2)}, u32[]{:S(2)}) collective-permute-start(f32[2,8,16,128]{3,2,1,0:T(8,128)S(1)} %pad_maximum_fusion.3), channel_id=1, source_target_pairs={{0,2},{1,3},{2,0},{3,1},{4,6},{5,7},{6,4},{7,5},{8,10},{9,11},{10,... | collective-permute-start | bytes 393224 | tf_op jit(solution)/shard_map/ppermute | solution.py:227
  81.9 0.1 pad_add_fusion.2.start_ref
  81.9 0.1 copy.26
  82.1 3.8 %collective-permute-done.8 = f32[2,8,16,128]{3,2,1,0:T(8,128)S(1)} collective-permute-done((f32[2,8,16,128]{3,2,1,0:T(8,128)S(1)}, f32[2,8,16,128]{3,2,1,0:T(8,128)S(1)}, u32[]{:S(2)}, u32[]{:S(2)}) %collective-permute-start.8) | collective-permute-done | bytes 131104 | tf_op jit(solution)/shard_map/ppermute | solution.py:227
  85.9 0.0 copy-done.3
  85.9 0.0 copy-done.4
  85.9 10.7 %chain.1 = (bf16[4,256,96]{2,1,0:T(8,128)(2,1)S(1)}, bf16[4,4,32,192]{3,2,1,0:T(8,128)(2,1)S(1)}, f32[4,256,256]{2,1,0:T(8,128)S(1)}, s32[4]{0:T(128)S(1)}) custom-call(s32[4]{0:T(128)S(1)} %pad_add_fusion.2.start_ref, f32[4,8,16,128]{3,2,1,0:T(8,128)S(1)} %pad_maximum_fusion.2.every_ref, s32[2,1024]{1,0:T(2,128)S(1)} %pad_add_fusion.row_ref, ...), custom_call_target="tpu_custom_call" | custom-call | flops 25999998976 | bytes 85000000 | tf_op jit(solution)/shard_map/chain/pallas_call | solution.py:431
  96.7 0.0 all-to-all-done.1
  96.7 3.8 %all-to-all-start = ((f32[8,4,3,2,8,128]{5,4,3,2,1,0:T(8,128)}), f32[8,4,3,2,8,128]{5,4,3,2,1,0:T(8,128)S(1)}, u32[]{:S(2)}, u32[]{:S(2)}) async-start(f32[8,4,3,2,8,128]{5,4,3,2,1,0:T(8,128)} %far.1.height_ref), calls=%async_computation | async-start | bytes 1572864 | tf_op jit(solution)/shard_map/all_to_all | solution.py:634
  100.5 17.6 %update.2.rest_0_ = f32[32,3,32,256]{3,2,1,0:T(8,128)} custom-call(s32[3]{0:T(128)S(1)} %iota_add_fusion.tile_ref, s32[4]{0:T(128)S(1)} %pad_add_fusion.2.start_ref, s32[4]{0:T(128)S(1)} %get-tuple-element.11.count_ref, f32[32,3,2,24,128]{4,3,2,1,0:T(8,128)} %bitcast.14.state_ref, s32[32,256]{1,0:T(8,128)S(1)} %copy-done.2, ...), custom_call_target="tpu_custom_call" | custom-call | tf_op jit(solution)/shard_map/update/pallas_call | solution.py:550
  118.1 2.0 %all-to-all-done = f32[8,4,3,2,8,128]{5,4,3,2,1,0:T(8,128)S(1)} async-done(((f32[8,4,3,2,8,128]{5,4,3,2,1,0:T(8,128)}), f32[8,4,3,2,8,128]{5,4,3,2,1,0:T(8,128)S(1)}, u32[]{:S(2)}, u32[]{:S(2)}) %all-to-all-start) | async-done | bytes 786464 | tf_op jit(solution)/shard_map/all_to_all | solution.py:634
  120.1 6.4 %update.3 = f32[32,3,32,256]{3,2,1,0:T(8,128)} custom-call(s32[1]{0:T(128)} %bitcast.tile_ref, s32[4]{0:T(128)S(1)} %pad_add_fusion.2.start_ref, s32[4]{0:T(128)S(1)} %get-tuple-element.11.count_ref, f32[32,3,2,8,128]{4,3,2,1,0:T(8,128)S(1)} %bitcast.30, s32[32,256]{1,0:T(8,128)S(1)} %copy-done.2, ...), custom_call_target="tpu_custom_call", output_to_operand_aliasing={{}: (8, {})} | custom-call | tf_op jit(solution)/shard_map/update/pallas_call | solution.py:550
  (16 shorter events, 0.1 us)
Async XLA Ops:
  0.9 5.7 %copy-start.1 = (f32[32,2048]{1,0:T(8,128)S(1)}, f32[32,2048]{1,0:T(8,128)}, u32[]{:S(2)}) copy-start(f32[32,2048]{1,0:T(8,128)} %depth_ref.3) | copy-start | bytes 786436
  3.5 3.1 %collective-permute-start.1 = (f32[13,8,2048]{2,1,0:T(8,128)S(1)}, f32[13,8,2048]{2,1,0:T(8,128)S(1)}, u32[]{:S(2)}, u32[]{:S(2)}) collective-permute-start(f32[13,8,2048]{2,1,0:T(8,128)S(1)} %get-tuple-element.23), channel_id=1, source_target_pairs={{0,1},{1,0},{2,3},{3,2},{4,5},{5,4},{6,7},{7,6},{8,9},{9,8},{10,11... | collective-permute-start | bytes 2555912 | tf_op jit(solution)/shard_map/ppermute | solution.py:227
  4.0 23.0 %collective-permute-start = (f32[13,8,2048]{2,1,0:T(8,128)}, f32[13,8,2048]{2,1,0:T(8,128)}, u32[]{:S(2)}, u32[]{:S(2)}) collective-permute-start(f32[13,8,2048]{2,1,0:T(8,128)} %get-tuple-element.24), channel_id=1, source_target_pairs={{0,3},{1,2},{2,1},{3,0},{4,7},{5,6},{6,5},{7,4},{8,11},{9,10},{10,... | collective-permute-start | bytes 2555912 | tf_op jit(solution)/shard_map/ppermute | solution.py:590
  16.6 6.8 %copy-start.5 = (s32[4,256]{1,0:T(4,128)S(1)}, s32[4,256]{1,0:T(4,128)}, u32[]{:S(2)}) copy-start(s32[4,256]{1,0:T(4,128)} %param.9) | copy-start | bytes 12292
  16.6 6.9 %copy-start.2 = (s32[32,256]{1,0:T(8,128)S(1)}, s32[32,256]{1,0:T(8,128)}, u32[]{:S(2)}) copy-start(s32[32,256]{1,0:T(8,128)} %cutoff_ref.5) | copy-start | bytes 98308
  16.6 10.4 %copy-start = (f32[4,3,32,2048]{3,2,1,0:T(8,128)S(1)}, f32[4,3,32,2048]{3,2,1,0:T(8,128)}, u32[]{:S(2)}) copy-start(f32[4,3,32,2048]{3,2,1,0:T(8,128)} %ens_ref.3) | copy-start | bytes 9437188
  16.6 80.1 %all-to-all-start.1 = ((f32[8,4,3,2,24,128]{5,4,3,2,1,0:T(8,128)}), f32[8,4,3,2,24,128]{5,4,3,2,1,0:T(8,128)}, u32[]{:S(2)}, u32[]{:S(2)}) async-start(f32[8,4,3,2,24,128]{5,4,3,2,1,0:T(8,128)} %near.1.height_ref), calls=%async_computation.1 | async-start | bytes 4718592 | tf_op jit(solution)/shard_map/all_to_all | solution.py:621
  27.0 58.9 %copy-start.3 = (f32[4,256]{1,0:T(4,128)S(1)}, f32[4,256]{1,0:T(4,128)}, u32[]{:S(2)}) copy-start(f32[4,256]{1,0:T(4,128)} %value_ref.1) | copy-start | bytes 12292
  27.0 58.9 %copy-start.4 = (f32[4,256]{1,0:T(4,128)S(1)}, f32[4,256]{1,0:T(4,128)}, u32[]{:S(2)}) copy-start(f32[4,256]{1,0:T(4,128)} %variance_ref.1) | copy-start | bytes 12292
  35.6 1.3 %collective-permute-start.2 = (f32[4,16,128]{2,1,0:T(8,128)S(1)}, f32[4,16,128]{2,1,0:T(8,128)S(1)}, u32[]{:S(2)}, u32[]{:S(2)}) collective-permute-start(f32[4,16,128]{2,1,0:T(8,128)S(1)} %pick_far.1), channel_id=1, source_target_pairs={{0,1},{1,0},{2,3},{3,2},{4,5},{5,4},{6,7},{7,6},{8,9},{9,8},{10,11... | collective-permute-start | bytes 98312 | tf_op jit(solution)/shard_map/ppermute | solution.py:227
  36.9 3.9 %collective-permute-start.3 = (f32[4,16,128]{2,1,0:T(8,128)S(1)}, f32[4,16,128]{2,1,0:T(8,128)S(1)}, u32[]{:S(2)}, u32[]{:S(2)}) collective-permute-start(f32[4,16,128]{2,1,0:T(8,128)S(1)} %add.32), channel_id=1, source_target_pairs={{0,2},{1,3},{2,0},{3,1},{4,6},{5,7},{6,4},{7,5},{8,10},{9,11},{10,... | collective-permute-start | bytes 98312 | tf_op jit(solution)/shard_map/ppermute | solution.py:227
  40.8 3.7 %collective-permute-start.4 = (f32[1,16,128]{2,1,0:T(8,128)S(1)}, f32[1,16,128]{2,1,0:T(8,128)S(1)}, u32[]{:S(2)}, u32[]{:S(2)}) collective-permute-start(f32[1,16,128]{2,1,0:T(8,128)S(1)} %dynamic-slice_add_fusion), channel_id=1, source_target_pairs={{0,4},{4,0},{8,12},{12,8},{16,20},{20,16},{24,28},{28,24},{1,5},{5... | collective-permute-start | bytes 24584 | tf_op jit(solution)/shard_map/ppermute | solution.py:227
  44.5 18.9 %collective-permute-start.5 = (f32[2,16,128]{2,1,0:T(8,128)S(1)}, f32[2,16,128]{2,1,0:T(8,128)S(1)}, u32[]{:S(2)}, u32[]{:S(2)}) collective-permute-start(f32[2,16,128]{2,1,0:T(8,128)S(1)} %pad_maximum_fusion.5), channel_id=1, source_target_pairs={{0,8},{4,12},{8,0},{12,4},{16,24},{20,28},{24,16},{28,20},{1,9},{5... | collective-permute-start | bytes 49160 | tf_op jit(solution)/shard_map/ppermute | solution.py:227
  63.4 15.6 %collective-permute-start.6 = (f32[4,16,128]{2,1,0:T(8,128)S(1)}, f32[4,16,128]{2,1,0:T(8,128)S(1)}, u32[]{:S(2)}, u32[]{:S(2)}) collective-permute-start(f32[4,16,128]{2,1,0:T(8,128)S(1)} %pad_maximum_fusion.4), channel_id=1, source_target_pairs={{0,16},{4,20},{8,24},{12,28},{16,0},{20,4},{24,8},{28,12},{1,17},{... | collective-permute-start | bytes 98312 | tf_op jit(solution)/shard_map/ppermute | solution.py:227
  79.0 1.3 collective-permute-start.7
  80.3 5.6 %collective-permute-start.8 = (f32[2,8,16,128]{3,2,1,0:T(8,128)S(1)}, f32[2,8,16,128]{3,2,1,0:T(8,128)S(1)}, u32[]{:S(2)}, u32[]{:S(2)}) collective-permute-start(f32[2,8,16,128]{3,2,1,0:T(8,128)S(1)} %pad_maximum_fusion.3), channel_id=1, source_target_pairs={{0,2},{1,3},{2,0},{3,1},{4,6},{5,7},{6,4},{7,5},{8,10},{9,11},{10,... | collective-permute-start | bytes 393224 | tf_op jit(solution)/shard_map/ppermute | solution.py:227
  96.7 23.4 %all-to-all-start = ((f32[8,4,3,2,8,128]{5,4,3,2,1,0:T(8,128)}), f32[8,4,3,2,8,128]{5,4,3,2,1,0:T(8,128)S(1)}, u32[]{:S(2)}, u32[]{:S(2)}) async-start(f32[8,4,3,2,8,128]{5,4,3,2,1,0:T(8,128)} %far.1.height_ref), calls=%async_computation | async-start | bytes 1572864 | tf_op jit(solution)/shard_map/all_to_all | solution.py:634

commit v5 on v4

v5 whole, which is shorter than its diff:
```python
import functools

import jax
import jax.numpy as jnp
from jax import lax
from jax.experimental import pallas as pl
from jax.experimental.pallas import tpu as pltpu
from jax.sharding import PartitionSpec as P

STEPS = 4
HALO = 2 * STEPS
LANES = 128
OBS_BLOCK = 48
ROW_TILE = 8
VMEM_LIMIT = 48 * 2**20
OUTER_COST = pl.CostEstimate(flops=23 * 10**9, bytes_accessed=74 * 10**6, transcendentals=0)
CHAIN_COST = pl.CostEstimate(flops=26 * 10**9, bytes_accessed=85 * 10**6, transcendentals=0)

step_size = 0.3
coriolis = 0.2
highest = lax.Precision.HIGHEST

NT = (((1,), (1,)), ((), ()))
TN = (((0,), (0,)), ((), ()))


def params():
    return pltpu.CompilerParams(vmem_limit_bytes=VMEM_LIMIT)


def vmem(count=1):
    return [pl.BlockSpec(memory_space=pltpu.VMEM)] * count


def smem(count=1):
    return [pl.BlockSpec(memory_space=pltpu.SMEM)] * count


def split_bf16(value):
    high = value.astype(jnp.bfloat16)
    low = (value - high.astype(jnp.float32)).astype(jnp.bfloat16)
    return high, low


def row_centred(field):
    return pltpu.roll(field, field.shape[0] - 1, 0) - pltpu.roll(field, 1, 0)


def column_centred(tile_of, tiles):
    onward, back = [None] * tiles, [None] * tiles

    def at(t):
        for n in ((t - 1) % tiles, t, (t + 1) % tiles):
            if onward[n] is None:
                tile = tile_of(n)
                onward[n] = pltpu.roll(tile, LANES - 1, 1)
                back[n] = pltpu.roll(tile, 1, 1)
        lane = lax.broadcasted_iota(jnp.int32, onward[t].shape, 1)
        return jnp.where(
            lane == LANES - 1, onward[(t + 1) % tiles], onward[t]
        ) - jnp.where(lane == 0, back[(t - 1) % tiles], back[t])

    return at


def forecast_steps(height, east, north, half_depth):
    tiles = height.shape[0]
    half = 0.5 * step_size
    turn = step_size * coriolis
    for _ in range(STEPS):
        slope = column_centred(lambda t: half * height[t], tiles)
        for t in range(tiles):
            u, v = east[t], north[t]
            slope_y = slope(t)
            east[t] = u + turn * v - row_centred(half * height[t])
            north[t] = v - turn * u - slope_y
        inflow = column_centred(lambda t: half_depth[t] * north[t], tiles)
        for t in range(tiles):
            flow_y = inflow(t)
            height[t] = height[t] - (row_centred(half_depth[t] * east[t]) + flow_y)


def forecast_kernel(joins, kept, parity_ref, *refs):
    ens_ref, depth_ref, *halos, out_ref, height, east, north, half_depth = refs
    blocks, _, fields, out_tiles = out_ref.shape[:4]
    odd = parity_ref[0] == 1

    def window(block, near, far):
        if not joins:
            return block
        return jnp.concatenate([jnp.where(odd, near, far), block, jnp.where(odd, far, near)], 0)

    near_ref, far_ref, near_depth_ref, far_depth_ref = halos if joins else [None] * 4
    tiles = height.shape[0]

    def part(ref, index, t):
        return None if ref is None else ref[index][:, t * LANES : (t + 1) * LANES]

    @pl.when(pl.program_id(0) == 0)
    def _():
        for t in range(tiles):
            half_depth[t] = (0.5 * step_size) * window(
                depth_ref[:, t * LANES : (t + 1) * LANES],
                part(near_depth_ref, 0, t),
                part(far_depth_ref, 0, t),
            )

    state = (height, east, north)
    for f in range(fields):
        for t in range(tiles):
            state[f][t] = window(
                ens_ref[0, f, :, t * LANES : (t + 1) * LANES],
                part(near_ref, f, t),
                part(far_ref, f, t),
            )
    forecast_steps(*state, half_depth)
    for f in range(fields):
        for t in range(tiles):
            place = 0
            for first, count in kept:
                out_ref[t // out_tiles, 0, f, t % out_tiles, place : place + count] = state[f][
                    t, first : first + count
                ]
                place += count


def forecast(name, kept, parity, ensemble, depth, blocks, halos=()):
    members, fields, rows, columns = ensemble.shape
    tiles = columns // LANES
    window_rows = rows + (2 * HALO if halos else 0)
    out_shape = (blocks, members, fields, tiles // blocks, sum(n for _, n in kept), LANES)
    in_specs = smem() + [
        pl.BlockSpec((1, fields, rows, columns), lambda m: (m, 0, 0, 0)),
        pl.BlockSpec((rows, columns), lambda m: (0, 0)),
    ]
    operands = [parity, ensemble, depth]
    if halos:
        in_specs += [pl.BlockSpec((fields, HALO, columns), lambda m: (m, 0, 0))] * 2
        in_specs += [pl.BlockSpec((1, HALO, columns), lambda m: (members * fields, 0, 0))] * 2
        operands += [*halos, *halos]
    return pl.pallas_call(
        functools.partial(forecast_kernel, bool(halos), kept),
        grid=(members,),
        in_specs=in_specs,
        out_specs=pl.BlockSpec(
            (blocks, 1) + out_shape[2:], lambda m: (0, m, 0, 0, 0, 0)
        ),
        out_shape=jax.ShapeDtypeStruct(out_shape, jnp.float32),
        scratch_shapes=[pltpu.VMEM((tiles, window_rows, LANES), jnp.float32)] * 4,
        compiler_params=params(),
        cost_estimate=OUTER_COST if halos else None,
        name=name,
    )(*operands)


def pick(row_ref, col_ref, height_ref):
    blocks, members, _, tiles, rows, _ = height_ref.shape
    heights = jnp.concatenate(
        [
            height_ref[d, :, 0, t].reshape(members * rows, LANES)
            for d in range(blocks)
            for t in range(tiles)
        ],
        1,
    )
    high, rest = heights.astype(jnp.bfloat16), heights
    pieces = [high]
    for _ in range(2):
        rest = rest - pieces[-1].astype(jnp.float32)
        pieces.append(rest.astype(jnp.bfloat16))
    count = col_ref.shape[1]
    column = lax.broadcasted_iota(jnp.int32, (heights.shape[1], count), 0)
    in_column = (column == col_ref[...]).astype(jnp.float32).astype(jnp.bfloat16)
    found = jnp.dot(
        jnp.concatenate(pieces, 0), in_column, preferred_element_type=jnp.float32
    )
    size = members * rows
    found = (found[:size] + found[size : 2 * size]) + found[2 * size :]
    found = found.reshape(members, rows, count)
    row = lax.broadcasted_iota(jnp.int32, (1, rows, count), 1)
    return jnp.sum(jnp.where(row == row_ref[...][None], found, 0.0), 1)


def pick_inner_kernel(row_ref, col_ref, height_ref, out_ref):
    out_ref[...] = pick(row_ref, col_ref, height_ref)


def pick_outer_kernel(row_ref, col_ref, height_ref, inner_ref, radius_ref, out_ref):
    heights = pick(row_ref, col_ref, height_ref) + inner_ref[...]
    members, count = heights.shape
    pieces = out_ref.shape[0]
    groups = count // pieces // LANES
    out_ref[...] = jnp.zeros_like(out_ref)
    for j in range(pieces):
        for g in range(groups):
            part = slice((j * groups + g) * LANES, (j * groups + g + 1) * LANES)
            for m in range(members):
                row = g * members + m
                out_ref[j, row : row + 1, :] = heights[m : m + 1, part]
            row = members * groups + g
            out_ref[j, row : row + 1, :] = radius_ref[:, part]


def height_spec(sent):
    blocks, members, _, tiles, rows, _ = sent.shape
    return pl.BlockSpec((blocks, members, 1, tiles, rows, LANES), lambda i: (0,) * 6)


def whole_spec(shape):
    return pl.BlockSpec(shape, lambda i: (0,) * len(shape))


def pick_inner(row, col, sent):
    shape = (sent.shape[1], col.shape[1])
    return pl.pallas_call(
        pick_inner_kernel,
        grid=(1,),
        in_specs=[whole_spec(row.shape), whole_spec(col.shape), height_spec(sent)],
        out_specs=whole_spec(shape),
        out_shape=jax.ShapeDtypeStruct(shape, jnp.float32),
        compiler_params=params(),
        name="pick_inner",
    )(row, col, sent)


def pick_outer(row, col, sent, inner, radius, pieces):
    members, count = inner.shape
    used = (members + 1) * (count // pieces // LANES)
    shape = (pieces, used + -used % 8, LANES)
    return pl.pallas_call(
        pick_outer_kernel,
        grid=(1,),
        in_specs=[
            whole_spec(row.shape),
            whole_spec(col.shape),
            height_spec(sent),
            whole_spec(inner.shape),
            whole_spec(radius.shape),
        ],
        out_specs=whole_spec(shape),
        out_shape=jax.ShapeDtypeStruct(shape, jnp.float32),
        compiler_params=params(),
        name="pick_outer",
    )(row, col, sent, inner, radius)


def pick_radius(cutoff, obs_x, obs_y, x_start, y_start):
    rows, columns = cutoff.shape
    radius_sq = jnp.square(cutoff.astype(jnp.float32))
    row_is = (obs_x[:, None] - x_start == jnp.arange(rows)[None, :]).astype(jnp.float32)
    col_is = obs_y[:, None] - y_start == jnp.arange(columns)[None, :]
    by_row = jnp.dot(row_is, radius_sq, precision=highest)
    return jnp.sum(jnp.where(col_is, by_row, 0.0), 1)


def exchange(value, axis, distance):
    size = lax.axis_size(axis)
    return lax.ppermute(value, axis, [(i, i ^ distance) for i in range(size)])


def sum_over(value, axis):
    distance = 1
    while distance < lax.axis_size(axis):
        value = value + exchange(value, axis, distance)
        distance *= 2
    return value


def gather_over(value, axis, first=1, width=None):
    width = lax.axis_size(axis) if width is None else width
    return jnp.concatenate(
        [value] + [exchange(value, axis, r * first) for r in range(1, width)], 0
    )


def apart_sq(a, b, size):
    gap = jnp.abs(a - b)
    gap = jnp.minimum(gap, size - gap)
    return gap * gap


def eliminate_four(system, k, row_id):
    width = system.shape[1]
    row = [system[k + i : k + i + 1, :] for i in range(4)]
    p = [
        [jnp.broadcast_to(row[i][:, k + j : k + j + 1], (1, LANES)) for j in range(4)]
        for i in range(4)
    ]

    def wide(value):
        return jnp.concatenate([value] * (width // LANES), 1)

    def inverse(a00, a01, a10, a11):
        scale = 1.0 / (a00 * a11 - a01 * a10)
        return a11 * scale, -a01 * scale, -a10 * scale, a00 * scale

    i00, i01, i10, i11 = inverse(p[0][0], p[0][1], p[1][0], p[1][1])
    y = [
        [i00 * p[0][2 + j] + i01 * p[1][2 + j] for j in range(2)],
        [i10 * p[0][2 + j] + i11 * p[1][2 + j] for j in range(2)],
    ]
    schur = [
        [p[2 + i][2 + j] - p[2 + i][0] * y[0][j] - p[2 + i][1] * y[1][j] for j in range(2)]
        for i in range(2)
    ]
    s00, s01, s10, s11 = inverse(schur[0][0], schur[0][1], schur[1][0], schur[1][1])
    top0 = wide(i00) * row[0] + wide(i01) * row[1]
    top1 = wide(i10) * row[0] + wide(i11) * row[1]
    low0 = row[2] - wide(p[2][0]) * top0 - wide(p[2][1]) * top1
    low1 = row[3] - wide(p[3][0]) * top0 - wide(p[3][1]) * top1
    new2 = wide(s00) * low0 + wide(s01) * low1
    new3 = wide(s10) * low0 + wide(s11) * low1
    new0 = top0 - wide(y[0][0]) * new2 - wide(y[0][1]) * new3
    new1 = top1 - wide(y[1][0]) * new2 - wide(y[1][1]) * new3
    new = (new0, new1, new2, new3)
    result = system
    for i in range(4):
        result = result - system[:, k + i : k + i + 1] * new[i]
    for i in range(4):
        result = jnp.where(row_id == k + i, new[i], result)
    return result


def chain_kernel(
    members,
    sizes,
    start_ref,
    every_ref,
    row_ref,
    col_ref,
    value_ref,
    variance_ref,
    cutoff_ref,
    lhs1_ref,
    lhs2_ref,
    place_ref,
    count_ref,
    local_ref,
    anom_ref,
    mix_ref,
    rank_ref,
):
    size_x, size_y = sizes
    pieces, sources, _, _ = every_ref.shape
    batches, count = value_ref.shape
    groups = batches * count // pieces // LANES
    local_members = members // sources
    rows, columns = cutoff_ref.shape
    tiles = columns // LANES
    x_start = start_ref[0]
    y_start = start_ref[1]
    reach = jnp.max(cutoff_ref[...])
    reach_sq = reach * reach

    heights, radius_sq = [], []
    for j in range(pieces):
        piece = jnp.bitwise_xor(start_ref[2], j)
        for g in range(groups):
            found, radius = [], 0.0
            for source in range(sources):
                one = every_ref.at[piece, jnp.bitwise_xor(start_ref[3], source)]
                found.append(one[g * local_members : (g + 1) * local_members, :])
                last = local_members * groups + g
                radius = radius + one[last : last + 1, :]
            heights.append(jnp.concatenate(found, 0))
            radius_sq.append(radius)
    heights = jnp.concatenate(heights, 1)
    inverse_sq = 1.0 / jnp.concatenate(radius_sq, 1)
    before = (
        lax.broadcasted_iota(jnp.int32, (count, count), 0)
        <= lax.broadcasted_iota(jnp.int32, (count, count), 1)
    ).astype(jnp.bfloat16)
    slot = lax.broadcasted_iota(jnp.int32, (OBS_BLOCK, count), 0)
    twice = lax.broadcasted_iota(jnp.int32, (members, 3 * OBS_BLOCK), 1) < 2 * OBS_BLOCK
    member_row = lax.broadcasted_iota(jnp.int32, (members, LANES + count), 0)
    eye = (
        lax.broadcasted_iota(jnp.int32, (members, members), 0)
        == lax.broadcasted_iota(jnp.int32, (members, members), 1)
    ).astype(jnp.float32)

    def rank_reaching(b, t):
        obs_x = row_ref[0:1, b * count : (b + 1) * count]
        obs_y = row_ref[1:2, b * count : (b + 1) * count]
        off_x = jnp.where(obs_x >= x_start, obs_x - x_start, obs_x - x_start + size_x)
        gap_x = jnp.where(off_x < rows, 0, jnp.minimum(off_x - (rows - 1), size_x - off_x))
        off_y = obs_y - (y_start + t * LANES)
        off_y = jnp.where(off_y >= 0, off_y, off_y + size_y)
        gap_y = jnp.where(off_y < LANES, 0, jnp.minimum(off_y - (LANES - 1), size_y - off_y))
        reaches = gap_x * gap_x + gap_y * gap_y < reach_sq
        flags = jnp.broadcast_to(reaches.astype(jnp.float32), (8, count))
        ranks = jnp.dot(
            flags.astype(jnp.bfloat16), before, preferred_element_type=jnp.float32
        )
        rank_ref[b, t] = jnp.where(reaches, ranks.astype(jnp.int32) - 1, -1)
        count_ref[b, t] = jnp.sum(flags[0:1, :]).astype(jnp.int32)

    def gather(b, t, k):
        chosen = (slot == rank_ref[b, t, 0:1, :] - k * OBS_BLOCK).astype(jnp.float32)
        thrice = jnp.concatenate([chosen] * 3, 0).astype(jnp.bfloat16)
        chosen = chosen.astype(jnp.bfloat16)

        def product(x, y):
            return lax.dot_general(x, y, NT, preferred_element_type=jnp.float32)

        lhs1_ref[b, t, k] = product(chosen, anom_ref[b]).astype(jnp.bfloat16)
        lhs2_ref[b, t, k] = jnp.where(
            twice, product(mix_ref[b, 0], thrice), product(mix_ref[b, 1], thrice)
        ).astype(jnp.bfloat16)
        cells = row_ref[:, b * count : (b + 1) * count]
        place_ref[b, t, k] = product(
            chosen,
            jnp.concatenate([cells // 256, cells % 256], 0)
            .astype(jnp.float32)
            .astype(jnp.bfloat16),
        )

    def localize(b, first, size):
        later = slice((b + 1) * count, batches * count)
        part = slice(first, first + size)
        dist_sq = apart_sq(col_ref[part, b : b + 1], row_ref[0:1, later], size_x) + apart_sq(
            col_ref[part, batches + b : batches + b + 1], row_ref[1:2, later], size_y
        )
        ratio = dist_sq.astype(jnp.float32) * inverse_sq[:, later]
        local_ref[part, later] = jnp.square(jnp.maximum(1.0 - ratio, 0.0))

    for b in range(batches):
        here = slice(b * count, (b + 1) * count)
        prior = heights[:, here]
        mean = jnp.mean(prior, 0, keepdims=True)
        anom = prior - mean
        precision = 1.0 / variance_ref[b : b + 1, :]
        innov = value_ref[b : b + 1, :] - mean
        scaled = anom * precision
        inner = eye + lax.dot_general(
            scaled, anom, NT, precision=highest, preferred_element_type=jnp.float32
        ) / (members - 1)
        proj = jnp.sum(scaled * innov, 1, keepdims=True)
        system = jnp.concatenate(
            [inner, proj, jnp.zeros((members, LANES - members - 1), jnp.float32), scaled], 1
        )
        aside = [functools.partial(rank_reaching, b, t) for t in range(tiles)]
        if b > 0:
            aside += [functools.partial(gather, b - 1, t, 0) for t in range(tiles)]
        if b + 1 < batches:
            aside += [functools.partial(localize, b, first, 32) for first in range(0, count, 32)]
        steps = members // 4
        for step in range(steps):
            system = eliminate_four(system, 4 * step, member_row)
            for one in aside[step::steps]:
                one()
        solved_proj = system[:, members : members + 1]
        solved_anom = system[:, LANES:]
        solved_innov = precision * (
            innov - jnp.sum(anom * solved_proj, 0, keepdims=True) / (members - 1)
        )
        mix = (solved_innov - 0.5 * solved_anom) / (members - 1)
        high, low = split_bf16(anom)
        anom_ref[b] = jnp.concatenate([high, high, low], 0)
        mix_high, mix_low = split_bf16(mix)
        mix_ref[b, 0] = mix_high
        mix_ref[b, 1] = mix_low

        if b + 1 < batches:
            later = slice((b + 1) * count, batches * count)
            ahead = heights[:, later]
            ahead_anom = ahead - jnp.mean(ahead, 0, keepdims=True)
            cross = lax.dot_general(
                anom, ahead_anom, TN, precision=highest, preferred_element_type=jnp.float32
            )
            high, low = split_bf16(cross * local_ref[:, later])
            both = jnp.dot(
                jnp.concatenate([mix_high, mix_low], 0), high, preferred_element_type=jnp.float32
            )
            rest = jnp.dot(mix_high, low, preferred_element_type=jnp.float32)
            ahead = ahead + (both[:members] + (both[members:] + rest))
            heights = jnp.concatenate([heights[:, : (b + 1) * count], ahead], 1)

    for t in range(tiles):
        gather(batches - 1, t, 0)
    counts = [[count_ref[b, t] for t in range(tiles)] for b in range(batches)]
    most = functools.reduce(jnp.maximum, sum(counts, []))

    @pl.when(most > OBS_BLOCK)
    def _():
        for b in range(batches):
            for t in range(tiles):

                def more(k, _, b=b, t=t):
                    gather(b, t, k)
                    return 0

                blocks = (counts[b][t] + (OBS_BLOCK - 1)) // OBS_BLOCK
                lax.fori_loop(1, blocks, more, 0)


def chain(members, start, every, obs_x, obs_y, values, variance, cutoff, sizes):
    batches, count = values.shape
    row_form = jnp.stack([obs_x.reshape(-1), obs_y.reshape(-1)], 0)
    col_form = jnp.concatenate([obs_x, obs_y], 0).T
    tiles = cutoff.shape[1] // LANES
    slots = (batches, tiles, -(-count // OBS_BLOCK))
    return pl.pallas_call(
        functools.partial(chain_kernel, members, sizes),
        in_specs=smem() + vmem(6),
        out_specs=vmem(3) + smem(),
        out_shape=[
            jax.ShapeDtypeStruct(slots + (OBS_BLOCK, 3 * members), jnp.bfloat16),
            jax.ShapeDtypeStruct(slots + (members, 3 * OBS_BLOCK), jnp.bfloat16),
            jax.ShapeDtypeStruct(slots + (OBS_BLOCK, 4), jnp.float32),
            jax.ShapeDtypeStruct(slots[:2], jnp.int32),
        ],
        scratch_shapes=[
            pltpu.VMEM((count, batches * count), jnp.float32),
            pltpu.VMEM((batches, 3 * members, count), jnp.bfloat16),
            pltpu.VMEM((batches, 2, members, count), jnp.bfloat16),
            pltpu.VMEM((batches, tiles, 8, count), jnp.int32),
        ],
        compiler_params=params(),
        cost_estimate=CHAIN_COST,
        name="chain",
    )(start, every, row_form, col_form, values, variance, cutoff)


def update_kernel(
    sizes,
    continues,
    tile_ref,
    start_ref,
    count_ref,
    state_ref,
    cutoff_ref,
    lhs1_ref,
    lhs2_ref,
    place_ref,
    *rest,
):
    out_ref, members_ref, rhs_ref = rest[1:] if continues else rest
    size_x, size_y = float(sizes[0]), float(sizes[1])
    members, fields, _, rows, _ = state_ref.shape
    batches = lhs1_ref.shape[0]
    cells = rows * LANES
    t = pl.program_id(1)
    flat = state_ref.reshape(members * fields * rows, LANES)
    flat_out = out_ref.reshape(members * fields * rows, LANES)
    row0 = (start_ref[0] + tile_ref[pl.program_id(0)] * rows).astype(jnp.float32)
    col0 = (start_ref[1] + t * LANES).astype(jnp.float32)
    lane = lax.broadcasted_iota(jnp.int32, (1, LANES), 1).astype(jnp.float32)
    radius = cutoff_ref[...].astype(jnp.float32)
    radius_sq = radius * radius
    inverse = 1.0 / radius_sq

    def localized(b, k):
        place = place_ref[b, 0, k]
        obs_x = jnp.broadcast_to(place[:, 0:1] * 256.0 + place[:, 2:3], (OBS_BLOCK, LANES))
        obs_y = jnp.broadcast_to(place[:, 1:2] * 256.0 + place[:, 3:4], (OBS_BLOCK, LANES))
        dist_y = apart_sq(obs_y, lane + col0, size_y)
        dist_x = apart_sq(obs_x, lane + row0, size_x)
        weights = []
        for r in range(rows):
            ratio = (dist_y + dist_x[:, r : r + 1]) * inverse[r : r + 1, :]
            weights.append(jnp.square(jnp.maximum(1.0 - ratio, 0.0)))
        return jnp.concatenate(weights, 1)

    def contribution(b, k, weights, rhs):
        cross = jnp.dot(lhs1_ref[b, 0, k], rhs, preferred_element_type=jnp.float32)
        high, low = split_bf16(cross * weights)
        return jnp.dot(
            lhs2_ref[b, 0, k],
            jnp.concatenate([high, low, high], 0),
            preferred_element_type=jnp.float32,
        )

    def split_anom(state):
        high, low = split_bf16(state - jnp.mean(state, 0, keepdims=True))
        return jnp.concatenate([high, low, high], 0)

    def load(f):
        return jnp.concatenate(
            [
                flat[pl.ds(f * rows + r, members, stride=fields * rows), :]
                for r in range(rows)
            ],
            1,
        )

    def store(f, state):
        for r in range(rows):
            flat_out[pl.ds(f * rows + r, members, stride=fields * rows), :] = state[
                :, r * LANES : (r + 1) * LANES
            ]

    most = count_ref[0, t]
    for b in range(1, batches):
        most = jnp.maximum(most, count_ref[b, t])

    @pl.when(most <= OBS_BLOCK)
    def _():
        states = [load(f) for f in range(fields)]
        for b in range(batches):
            weights = localized(b, 0)
            rhs = [split_anom(x) for x in states]
            cross = [jnp.dot(lhs1_ref[b, 0, 0], x, preferred_element_type=jnp.float32) for x in rhs]
            gain = []
            for c in cross:
                high, low = split_bf16(c * weights)
                gain.append(jnp.concatenate([high, low, high], 0))
            moved = [jnp.dot(lhs2_ref[b, 0, 0], g, preferred_element_type=jnp.float32) for g in gain]
            states = [x + y for x, y in zip(states, moved)]
        for f in range(fields):
            store(f, states[f])

    @pl.when(most > OBS_BLOCK)
    def _():
        for f in range(fields):
            members_ref[f] = load(f)
        for b in range(batches):
            for f in range(fields):
                rhs_ref[f] = split_anom(members_ref[f])

            def block(k, _, b=b):
                weights = localized(b, k)
                for f in range(fields):
                    members_ref[f] += contribution(b, k, weights, rhs_ref[f])
                return 0

            blocks = (count_ref[b, t] + (OBS_BLOCK - 1)) // OBS_BLOCK
            lax.fori_loop(0, blocks, block, 0)
        for f in range(fields):
            store(f, members_ref[f])


def update(row_tiles, start, counts, state, cutoff, lhs1, lhs2, place, sizes, begun=None):
    members, fields, tiles, _, _ = state.shape
    rows = cutoff.shape[0]
    columns = tiles * LANES
    cells = ROW_TILE * LANES

    def of_tile(array):
        shape = (array.shape[0], 1) + array.shape[2:]
        return pl.BlockSpec(shape, lambda i, t, tile: (0, t) + (0,) * (array.ndim - 2))

    operands = [row_tiles, start, counts, state, cutoff, lhs1, lhs2, place]
    in_specs = smem(2) + [
        pl.BlockSpec(
            (members, fields, 1, ROW_TILE, LANES), lambda i, t, tile: (0, 0, t, i, 0)
        ),
        pl.BlockSpec((ROW_TILE, LANES), lambda i, t, tile: (tile[i], t)),
        of_tile(lhs1),
        of_tile(lhs2),
        of_tile(place),
    ]
    aliases = {}
    if begun is not None:
        aliases = {len(operands): 0}
        operands.append(begun)
        in_specs.append(pl.BlockSpec(memory_space=pl.ANY))
    return pl.pallas_call(
        functools.partial(update_kernel, sizes, begun is not None),
        grid_spec=pltpu.PrefetchScalarGridSpec(
            num_scalar_prefetch=1,
            grid=row_tiles.shape + (tiles,),
            in_specs=in_specs,
            out_specs=pl.BlockSpec(
                (members, fields, ROW_TILE, LANES), lambda i, t, tile: (0, 0, tile[i], t)
            ),
            scratch_shapes=[
                pltpu.VMEM((fields, members, cells), jnp.float32),
                pltpu.VMEM((fields, 3 * members, cells), jnp.bfloat16),
            ],
        ),
        out_shape=jax.ShapeDtypeStruct((members, fields, rows, columns), jnp.float32),
        input_output_aliases=aliases,
        compiler_params=params(),
        name="update",
    )(*operands)


def row_halos(ensemble, depth, axis):
    size = lax.axis_size(axis)
    odd = lax.axis_index(axis) % 2 == 1
    columns = depth.shape[1]

    def edge(start):
        return jnp.concatenate(
            [
                ensemble[:, :, start : start + HALO].reshape(-1, HALO, columns),
                depth[None, start : start + HALO],
            ],
            0,
        )

    first, last = edge(0), edge(depth.shape[0] - HALO)
    far = [(i, (i + (1 if i % 2 else -1)) % size) for i in range(size)]
    return (
        exchange(jnp.where(odd, first, last), axis, 1),
        lax.ppermute(jnp.where(odd, last, first), axis, far),
    )


def local(ensemble, sea_depth, cutoff, obs_index, obs_value, obs_var):
    blocks = lax.axis_size("mem")
    subs = lax.axis_size("sub")
    local_members, fields, rows, size_y = ensemble.shape
    members = local_members * blocks
    col_block = size_y // blocks
    size_x = rows * subs
    sizes = (size_x, size_y)
    sub, mem = lax.axis_index("sub"), lax.axis_index("mem")
    odd = sub % 2
    x_start = sub * rows
    y_start = mem * col_block
    start = jnp.stack([x_start, y_start, sub, mem]).astype(jnp.int32)
    parity = odd.astype(jnp.int32)[None]
    obs_x = obs_index // size_y
    obs_y = obs_index % size_y
    flat_x = obs_x.reshape(1, -1)
    flat_y = obs_y.reshape(1, -1)

    halos = row_halos(ensemble, sea_depth, "sub")
    radius_part = pick_radius(cutoff, flat_x[0], flat_y[0], x_start, y_start)[None]

    inner_rows = rows - 2 * HALO
    sent_inner = forecast(
        "inner", [(HALO, inner_rows)], parity, ensemble, sea_depth, blocks
    )
    received_inner = lax.all_to_all(
        sent_inner, "mem", split_axis=0, concat_axis=0, tiled=True
    )
    row = flat_x - x_start
    inner_heights = pick_inner(row - HALO, flat_y, sent_inner)

    outer_row = jnp.where(
        row < HALO, row, jnp.where(row < rows - HALO, -1, row - inner_rows)
    )
    sent_outer = forecast(
        "outer", [(HALO, HALO), (rows, HALO)], parity, ensemble, sea_depth, blocks, halos
    )
    part = pick_outer(outer_row, flat_y, sent_outer, inner_heights, radius_part, subs)
    piece = lax.dynamic_index_in_dim(sum_over(part, "sub"), sub, 0, keepdims=True)
    low = max(blocks // 4, 1)
    every = gather_over(gather_over(piece, "mem", 1, low), "mem", low, blocks // low)
    every, sent_outer = lax.optimization_barrier((every, sent_outer))
    received_outer = lax.all_to_all(
        sent_outer, "mem", split_axis=0, concat_axis=0, tiled=True
    )
    every = gather_over(every[None], "sub")
    lhs1, lhs2, place, counts = chain(
        members, start, every, obs_x, obs_y, obs_value, obs_var, cutoff, sizes
    )

    def analyse(received, row_tiles, begun=None):
        state = received.reshape((members,) + received.shape[2:])
        row_tiles = jnp.array(row_tiles, jnp.int32)
        return update(
            row_tiles, start, counts, state, cutoff, lhs1, lhs2, place, sizes, begun
        )

    last = rows // ROW_TILE - 1
    return analyse(received_outer, [0, last], analyse(received_inner, list(range(1, last))))


def solution(mesh):
    return jax.shard_map(
        local,
        mesh=mesh,
        in_specs=(P("mem", None, "sub", None), P("sub", None), P("sub", "mem"), P(), P(), P()),
        out_specs=P(None, None, "sub", "mem"),
        check_vma=False,
    )
```

time: 127 us -> 113 us (0.89)
  waiting for transfers between devices: 41.3 us -> 27.6 us
  Pallas kernels: 55.9 us -> 49.4 us
  local copies, waits for them, and re-layouts: 2.61 us -> 8.78 us
    ppermute x8 -> x10, waiting for transfers between devices: 39.3 us -> 14.1 us  [exchange(): return lax.ppermute(value, axis, [(i, i ^ distance) for i in range(size)])]
    all_to_all x2, waiting for transfers between devices: 2.02 us -> 10.9 us  [the longest x1 10.9 us: local(): lax.all_to_all(sent_outer, 'mem', split_axis=0, concat_axis=0, tiled=True)]
    unnamed x16 -> x33, local copies, waits for them, and re-layouts: 0.05 us -> 6.26 us
    pallas_call x2, Pallas kernels: 24 us -> 18.4 us  [update(): pl.pallas_call(functools.partial(update_kernel, sizes, begun is not None)...]
    ppermute x1, waiting for transfers between devices: 0.01 us -> 2.62 us  [row_halos(): lax.ppermute(jnp.where(odd, last, first), axis, far)]
    pallas_call x1, Pallas kernels: 10.7 us -> 8.74 us  [chain(): pl.pallas_call(functools.partial(chain_kernel, members, sizes), in_specs=...]
    ppermute x8 -> x10, starting transfers between devices: 11.1 us -> 11.9 us  [exchange(): return lax.ppermute(value, axis, [(i, i ^ distance) for i in range(size)])]
  transfers between devices with their start and end apart: 11 -> 13, of which waited for: 8 -> 9; matrix products, arithmetic and copies ran while one was open for 1% -> 1% of each run, Pallas kernels for 39% -> 36%
where the time goes in v5:
time: 113 us; the launch traced here: 112 us
  Pallas kernels  49.4 us (44%)
  waiting for transfers between devices  27.6 us (24%)
  starting transfers between devices  24 us (21%)
  local copies, waits for them, and re-layouts  8.78 us (8%)
  other arithmetic  1.55 us (1%)
    pallas_call x2, Pallas kernels, update(): pl.pallas_call(functools.partial(update_kernel, sizes, begun is not None)...  18.4 us
    pallas_call x2, Pallas kernels, forecast(): pl.pallas_call(functools.partial(forecast_kernel, bool(halos), kept), gri...  18.1 us
    ppermute x10, waiting for transfers between devices, exchange(): return lax.ppermute(value, axis, [(i, i ^ distance) for i in range(size)])  14.1 us
    ppermute x10, starting transfers between devices, exchange(): return lax.ppermute(value, axis, [(i, i ^ distance) for i in range(size)])  11.9 us
    all_to_all x1, waiting for transfers between devices, local(): lax.all_to_all(sent_outer, 'mem', split_axis=0, concat_axis=0, tiled=True)  10.9 us
    pallas_call x1, Pallas kernels, chain(): pl.pallas_call(functools.partial(chain_kernel, members, sizes), in_specs=...  8.74 us
    unnamed x33, local copies, waits for them, and re-layouts  6.26 us
    all_to_all x1, starting transfers between devices, local(): lax.all_to_all(sent_inner, 'mem', split_axis=0, concat_axis=0, tiled=True)  5.94 us
  transfers between devices with their start and end apart: 13, of which 9 were waited for; matrix products, arithmetic and copies ran while one was open for 1% of the time, Pallas kernels for 36%

profile of v5, /device:TPU:0, one launch (start us, length us, event | category | flops | bytes accessed | tf_op | source)
XLA Modules:
  0.0 112.4 jit_solution(13409261082346847913)
XLA Ops:
  0.0 0.9 slice_bitcast_fusion.1
  0.9 1.5 %fusion.7 = (f32[4,3,8,2048]{3,2,1,0:T(8,128)S(1)}, f32[4,3,8,2048]{3,2,1,0:T(8,128)S(1)}) fusion(f32[4,3,32,2048]{3,2,1,0:T(8,128)} %refs_0_.3), kind=kLoop, calls=%fused_computation.38 | loop fusion | bytes 3145728 | tf_op jit(solution)/shard_map/slice | solution.py:686
  2.4 0.0 copy-start
  2.4 0.0 copy-start.7
  2.4 1.4 %fusion.1 = (f32[13,8,2048]{2,1,0:T(8,128)}, f32[13,8,2048]{2,1,0:T(8,128)}) fusion(f32[1,8,2048]{2,1,0:T(8,128)S(1)} %get-tuple-element.28, f32[12,8,2048]{2,1,0:T(8,128)S(1)} %bitcast.36, f32[1,8,2048]{2,1,0:T(8,128)S(1)} %get-tuple-element.27, f32[12,8,2048]{2,1,0:T(8,128)S(1)} %bitcast.35, pred[]{:T(512)S(6)} %eq.34), kind=kLoop, calls=%fused_computation.5 | loop fusion | flops 851968 | bytes 3407873 | tf_op jit(solution)/shard_map/jit(_where)/select_n | solution.py:696
  3.8 2.4 %collective-permute-start.1 = (f32[13,8,2048]{2,1,0:T(8,128)}, f32[13,8,2048]{2,1,0:T(8,128)}, u32[]{:S(2)}, u32[]{:S(2)}) collective-permute-start(f32[13,8,2048]{2,1,0:T(8,128)} %get-tuple-element.25), channel_id=1, source_target_pairs={{0,3},{1,2},{2,1},{3,0},{4,7},{5,6},{6,5},{7,4},{8,11},{9,10},{10,... | collective-permute-start | bytes 2555912 | tf_op jit(solution)/shard_map/ppermute | solution.py:696
  6.2 0.7 collective-permute-start
  6.9 0.0 copy-done
  6.9 0.0 copy-done.7
  6.9 7.3 %inner.1.height_ref = f32[8,4,3,2,16,128]{5,4,3,2,1,0:T(8,128)} custom-call(s32[1]{0:T(128)} %bitcast.4.parity_ref, f32[4,3,32,2048]{3,2,1,0:T(8,128)S(1)} %copy-done, f32[32,2048]{1,0:T(8,128)S(1)} %copy-done.7), custom_call_target="tpu_custom_call" | custom-call | tf_op jit(solution)/shard_map/inner/pallas_call | solution.py:141
  14.2 0.0 copy-start.12
  14.2 5.9 %all-to-all-start.1 = ((f32[8,4,3,2,16,128]{5,4,3,2,1,0:T(8,128)}), f32[8,4,3,2,16,128]{5,4,3,2,1,0:T(8,128)S(1)}, u32[]{:S(2)}, u32[]{:S(2)}) async-start(f32[8,4,3,2,16,128]{5,4,3,2,1,0:T(8,128)} %inner.1.height_ref), calls=%async_computation.1 | async-start | bytes 3145728 | tf_op jit(solution)/shard_map/all_to_all | solution.py:726
  20.2 0.0 copy-done.12
  20.3 2.1 %pick_inner.1.inner_ref = f32[4,1024]{1,0:T(4,128)S(1)} custom-call(s32[1,1024]{1,0:T(1,128)S(1)} %get-tuple-element.29.row_ref, s32[1,1024]{1,0:T(1,128)S(1)} %bitcast.31, f32[8,4,3,2,16,128]{5,4,3,2,1,0:T(8,128)} %inner.1.height_ref), custom_call_target="tpu_custom_call" | custom-call | tf_op jit(solution)/shard_map/pick_inner/pallas_call | solution.py:215
  22.4 0.0 copy-done.8
  22.4 0.8 fusion
  23.3 2.6 %collective-permute-done.1.refs_3_.refs_5_ = f32[13,8,2048]{2,1,0:T(8,128)} collective-permute-done((f32[13,8,2048]{2,1,0:T(8,128)}, f32[13,8,2048]{2,1,0:T(8,128)}, u32[]{:S(2)}, u32[]{:S(2)}) %collective-permute-start.1) | collective-permute-done | bytes 852000 | tf_op jit(solution)/shard_map/ppermute | solution.py:696
  25.9 0.0 collective-permute-done.refs_2_.refs_4_
  25.9 10.7 %outer.1.height_ref = f32[8,4,3,2,16,128]{5,4,3,2,1,0:T(8,128)} custom-call(s32[1]{0:T(128)} %bitcast.4.parity_ref, f32[4,3,32,2048]{3,2,1,0:T(8,128)} %refs_0_.3, f32[32,2048]{1,0:T(8,128)S(1)} %copy-done.7, f32[13,8,2048]{2,1,0:T(8,128)} %collective-permute-done.refs_2_.refs_4_, f32[13,8,2048]{2,1,0:T(8,128)} %collective-permute-done.1.refs_3_.refs_5_, ...), custom_call_target="tpu_custom_call" | custom-call | flops 23000000512 | bytes 74000000 | tf_op jit(solution)/shard_map/outer/pallas_call | solution.py:141
  36.6 2.1 %pick_outer.1 = f32[4,16,128]{2,1,0:T(8,128)S(1)} custom-call(s32[1,1024]{1,0:T(1,128)S(1)} %get-tuple-element.30.row_ref, s32[1,1024]{1,0:T(1,128)S(1)} %bitcast.32, f32[8,4,3,2,16,128]{5,4,3,2,1,0:T(8,128)} %outer.1.height_ref, f32[4,1024]{1,0:T(4,128)S(1)} %pick_inner.1.inner_ref, f32[1,1024]{1,0:T(1,128)S(1)} %bitcast.34), custom_call_target="tpu_custom_call" | custom-call | tf_op jit(solution)/shard_map/pick_outer/pallas_call | solution.py:230
  38.7 0.3 collective-permute-start.2
  39.0 1.0 collective-permute-done.2
  40.0 2.5 %collective-permute-start.3 = (f32[4,16,128]{2,1,0:T(8,128)S(1)}, f32[4,16,128]{2,1,0:T(8,128)S(1)}, u32[]{:S(2)}, u32[]{:S(2)}) collective-permute-start(f32[4,16,128]{2,1,0:T(8,128)S(1)} %add.42), channel_id=1, source_target_pairs={{0,2},{1,3},{2,0},{3,1},{4,6},{5,7},{6,4},{7,5},{8,10},{9,11},{10,... | collective-permute-start | bytes 98312 | tf_op jit(solution)/shard_map/ppermute | solution.py:258
  42.5 1.9 %collective-permute-done.3 = f32[4,16,128]{2,1,0:T(8,128)S(1)} collective-permute-done((f32[4,16,128]{2,1,0:T(8,128)S(1)}, f32[4,16,128]{2,1,0:T(8,128)S(1)}, u32[]{:S(2)}, u32[]{:S(2)}) %collective-permute-start.3) | collective-permute-done | bytes 32800 | tf_op jit(solution)/shard_map/ppermute | solution.py:258
  44.4 1.9 %collective-permute-start.4 = (f32[1,16,128]{2,1,0:T(8,128)S(1)}, f32[1,16,128]{2,1,0:T(8,128)S(1)}, u32[]{:S(2)}, u32[]{:S(2)}) collective-permute-start(f32[1,16,128]{2,1,0:T(8,128)S(1)} %get-tuple-element.18), channel_id=1, source_target_pairs={{0,4},{4,0},{8,12},{12,8},{16,20},{20,16},{24,28},{28,24},{1,5},{5... | collective-permute-start | bytes 24584 | tf_op jit(solution)/shard_map/ppermute | solution.py:258
  46.3 0.1 copy.28
  46.4 1.6 %collective-permute-done.4 = f32[1,16,128]{2,1,0:T(8,128)S(1)} collective-permute-done((f32[1,16,128]{2,1,0:T(8,128)S(1)}, f32[1,16,128]{2,1,0:T(8,128)S(1)}, u32[]{:S(2)}, u32[]{:S(2)}) %collective-permute-start.4) | collective-permute-done | bytes 8224 | tf_op jit(solution)/shard_map/ppermute | solution.py:258
  48.0 4.0 %collective-permute-start.7 = (f32[2,16,128]{2,1,0:T(8,128)S(1)}, f32[2,16,128]{2,1,0:T(8,128)S(1)}, u32[]{:S(2)}, u32[]{:S(2)}) collective-permute-start(f32[2,16,128]{2,1,0:T(8,128)S(1)} %pad_maximum_fusion.3), channel_id=1, source_target_pairs={{0,24},{4,28},{8,16},{12,20},{16,8},{20,12},{24,0},{28,4},{1,25},{... | collective-permute-start | bytes 49160 | tf_op jit(solution)/shard_map/ppermute | solution.py:258
  52.1 0.0 collective-permute-start.6
  52.1 0.6 collective-permute-start.5
  52.6 4.0 %collective-permute-done.5 = f32[2,16,128]{2,1,0:T(8,128)S(1)} collective-permute-done((f32[2,16,128]{2,1,0:T(8,128)S(1)}, f32[2,16,128]{2,1,0:T(8,128)S(1)}, u32[]{:S(2)}, u32[]{:S(2)}) %collective-permute-start.5) | collective-permute-done | bytes 16416 | tf_op jit(solution)/shard_map/ppermute | solution.py:258
  56.6 2.2 %collective-permute-done.6 = f32[2,16,128]{2,1,0:T(8,128)S(1)} collective-permute-done((f32[2,16,128]{2,1,0:T(8,128)S(1)}, f32[2,16,128]{2,1,0:T(8,128)S(1)}, u32[]{:S(2)}, u32[]{:S(2)}) %collective-permute-start.6) | collective-permute-done | bytes 16416 | tf_op jit(solution)/shard_map/ppermute | solution.py:258
  58.8 0.0 collective-permute-done.7
  58.8 0.0 copy-start.10
  58.8 0.0 copy-start.11
  58.8 0.0 all-to-all-done.1
  58.8 3.8 %all-to-all-start = ((f32[8,4,3,2,16,128]{5,4,3,2,1,0:T(8,128)}), f32[8,4,3,2,16,128]{5,4,3,2,1,0:T(8,128)S(1)}, u32[]{:S(2)}, u32[]{:S(2)}) async-start(f32[8,4,3,2,16,128]{5,4,3,2,1,0:T(8,128)} %outer.1.height_ref), calls=%async_computation | async-start | bytes 3145728 | tf_op jit(solution)/shard_map/all_to_all | solution.py:743
  62.6 0.1 collective-permute-start.10
  62.7 1.2 %collective-permute-start.9 = (f32[1,8,16,128]{3,2,1,0:T(8,128)S(1)}, f32[1,8,16,128]{3,2,1,0:T(8,128)S(1)}, u32[]{:S(2)}, u32[]{:S(2)}) collective-permute-start(f32[1,8,16,128]{3,2,1,0:T(8,128)S(1)} %bitcast.38), channel_id=1, source_target_pairs={{0,2},{1,3},{2,0},{3,1},{4,6},{5,7},{6,4},{7,5},{8,10},{9,11},{10,... | collective-permute-start | bytes 196616 | tf_op jit(solution)/shard_map/ppermute | solution.py:258
  64.0 0.6 collective-permute-start.8
  64.6 0.1 pad_add_fusion.2.start_ref
  64.6 2.5 %collective-permute-done.10 = f32[1,8,16,128]{3,2,1,0:T(8,128)S(1)} collective-permute-done((f32[1,8,16,128]{3,2,1,0:T(8,128)S(1)}, f32[1,8,16,128]{3,2,1,0:T(8,128)S(1)}, u32[]{:S(2)}, u32[]{:S(2)}) %collective-permute-start.10) | collective-permute-done | bytes 65568 | tf_op jit(solution)/shard_map/ppermute | solution.py:258
  67.1 1.0 collective-permute-done.9
  68.1 0.0 collective-permute-done.8
  68.1 0.0 copy-done.10
  68.1 0.0 copy-done.11
  68.2 0.0 copy-start.9
  68.2 8.7 %chain.1 = (bf16[4,2,6,48,96]{4,3,2,1,0:T(8,128)(2,1)S(1)}, bf16[4,2,6,32,144]{4,3,2,1,0:T(8,128)(2,1)S(1)}, f32[4,2,6,48,4]{4,3,2,1,0:T(8,128)S(1)}, s32[4,2]{1,0:T(4,128)S(1)}) custom-call(s32[4]{0:T(128)S(1)} %pad_add_fusion.2.start_ref, f32[4,8,16,128]{3,2,1,0:T(8,128)S(1)} %pad_maximum_fusion.2.every_ref, s32[2,1024]{1,0:T(2,128)S(1)} %pad_add_fusion.row_ref, ...), custom_call_target="tpu_custom_call" | custom-call | flops 25999998976 | bytes 85000000 | tf_op jit(solution)/shard_map/chain/pallas_call | solution.py:502
  76.9 0.0 copy-done.9
  76.9 9.2 %update.2.rest_0_ = f32[32,3,32,256]{3,2,1,0:T(8,128)} custom-call(s32[2]{0:T(128)S(1)} %copy-done.9, s32[4]{0:T(128)S(1)} %pad_add_fusion.2.start_ref, s32[4,2]{1,0:T(4,128)S(1)} %get-tuple-element.12.count_ref, f32[32,3,2,16,128]{4,3,2,1,0:T(8,128)S(1)} %bitcast.28, s32[32,256]{1,0:T(8,128)S(1)} %copy-done.8, ...), custom_call_target="tpu_custom_call" | custom-call | tf_op jit(solution)/shard_map/update/pallas_call | solution.py:657
  86.1 0.0 copy-start.1
  86.1 1.0 copy-done.1
  87.2 0.0 copy-start.3
  87.2 0.9 copy-done.3
  88.1 0.0 copy-start.5
  88.1 0.8 copy-done.5
  88.9 10.9 %all-to-all-done = f32[8,4,3,2,16,128]{5,4,3,2,1,0:T(8,128)S(1)} async-done(((f32[8,4,3,2,16,128]{5,4,3,2,1,0:T(8,128)}), f32[8,4,3,2,16,128]{5,4,3,2,1,0:T(8,128)S(1)}, u32[]{:S(2)}, u32[]{:S(2)}) %all-to-all-start) | async-done | bytes 1572896 | tf_op jit(solution)/shard_map/all_to_all | solution.py:743
  99.7 0.0 copy-start.2
  99.7 1.3 %copy-done.2 = f32[4,2,6,48,4]{4,3,2,1,0:T(8,128)S(1)} copy-done((f32[4,2,6,48,4]{4,3,2,1,0:T(8,128)S(1)}, f32[4,2,6,48,4]{4,3,2,1,0:T(8,128)}, u32[]{:S(2)}) %copy-start.2) | copy-done | bytes 36888
  101.0 0.0 copy-start.4
  101.0 1.1 %copy-done.4 = bf16[4,2,6,32,144]{4,3,2,1,0:T(8,128)(2,1)S(1)} copy-done((bf16[4,2,6,32,144]{4,3,2,1,0:T(8,128)(2,1)S(1)}, bf16[4,2,6,32,144]{4,3,2,1,0:T(8,128)(2,1)}, u32[]{:S(2)}) %copy-start.4) | copy-done | bytes 442392
  102.1 0.0 copy-start.6
  102.1 1.1 copy-done.6
  103.2 9.2 %update.3 = f32[32,3,32,256]{3,2,1,0:T(8,128)} custom-call(s32[2]{0:T(128)S(1)} %iota_multiply_fusion.tile_ref, s32[4]{0:T(128)S(1)} %pad_add_fusion.2.start_ref, s32[4,2]{1,0:T(4,128)S(1)} %get-tuple-element.12.count_ref, f32[32,3,2,16,128]{4,3,2,1,0:T(8,128)S(1)} %bitcast.29, s32[32,256]{1,0:T(8,128)S(1)} %copy-done.8, ...), custom_call_target="tpu_custom_call", output_to_operand_aliasing={{}: (8, {})} | custom-call | tf_op jit(solution)/shard_map/update/pallas_call | solution.py:657
  (18 shorter events, 0.1 us)
Async XLA Ops:
  2.4 4.5 %copy-start = (f32[4,3,32,2048]{3,2,1,0:T(8,128)S(1)}, f32[4,3,32,2048]{3,2,1,0:T(8,128)}, u32[]{:S(2)}) copy-start(f32[4,3,32,2048]{3,2,1,0:T(8,128)} %refs_0_.3) | copy-start | bytes 9437188
  2.4 4.5 %copy-start.7 = (f32[32,2048]{1,0:T(8,128)S(1)}, f32[32,2048]{1,0:T(8,128)}, u32[]{:S(2)}) copy-start(f32[32,2048]{1,0:T(8,128)} %refs_1_.3) | copy-start | bytes 786436
  3.8 22.0 %collective-permute-start.1 = (f32[13,8,2048]{2,1,0:T(8,128)}, f32[13,8,2048]{2,1,0:T(8,128)}, u32[]{:S(2)}, u32[]{:S(2)}) collective-permute-start(f32[13,8,2048]{2,1,0:T(8,128)} %get-tuple-element.25), channel_id=1, source_target_pairs={{0,3},{1,2},{2,1},{3,0},{4,7},{5,6},{6,5},{7,4},{8,11},{9,10},{10,... | collective-permute-start | bytes 2555912 | tf_op jit(solution)/shard_map/ppermute | solution.py:696
  6.2 19.6 %collective-permute-start = (f32[13,8,2048]{2,1,0:T(8,128)}, f32[13,8,2048]{2,1,0:T(8,128)}, u32[]{:S(2)}, u32[]{:S(2)}) collective-permute-start(f32[13,8,2048]{2,1,0:T(8,128)} %get-tuple-element.26), channel_id=1, source_target_pairs={{0,1},{1,0},{2,3},{3,2},{4,5},{5,4},{6,7},{7,6},{8,9},{9,8},{10,11... | collective-permute-start | bytes 2555912 | tf_op jit(solution)/shard_map/ppermute | solution.py:258
  14.2 6.0 %copy-start.12 = (s32[4,256]{1,0:T(4,128)S(1)}, s32[4,256]{1,0:T(4,128)}, u32[]{:S(2)}) copy-start(s32[4,256]{1,0:T(4,128)} %param.11) | copy-start | bytes 12292
  14.2 44.6 %all-to-all-start.1 = ((f32[8,4,3,2,16,128]{5,4,3,2,1,0:T(8,128)}), f32[8,4,3,2,16,128]{5,4,3,2,1,0:T(8,128)S(1)}, u32[]{:S(2)}, u32[]{:S(2)}) async-start(f32[8,4,3,2,16,128]{5,4,3,2,1,0:T(8,128)} %inner.1.height_ref), calls=%async_computation.1 | async-start | bytes 3145728 | tf_op jit(solution)/shard_map/all_to_all | solution.py:726
  20.2 2.2 %copy-start.8 = (s32[32,256]{1,0:T(8,128)S(1)}, s32[32,256]{1,0:T(8,128)}, u32[]{:S(2)}) copy-start(s32[32,256]{1,0:T(8,128)} %cutoff_ref.5) | copy-start | bytes 98308
  38.7 1.3 %collective-permute-start.2 = (f32[4,16,128]{2,1,0:T(8,128)S(1)}, f32[4,16,128]{2,1,0:T(8,128)S(1)}, u32[]{:S(2)}, u32[]{:S(2)}) collective-permute-start(f32[4,16,128]{2,1,0:T(8,128)S(1)} %pick_outer.1), channel_id=1, source_target_pairs={{0,1},{1,0},{2,3},{3,2},{4,5},{5,4},{6,7},{7,6},{8,9},{9,8},{10,11... | collective-permute-start | bytes 98312 | tf_op jit(solution)/shard_map/ppermute | solution.py:258
  40.0 4.4 %collective-permute-start.3 = (f32[4,16,128]{2,1,0:T(8,128)S(1)}, f32[4,16,128]{2,1,0:T(8,128)S(1)}, u32[]{:S(2)}, u32[]{:S(2)}) collective-permute-start(f32[4,16,128]{2,1,0:T(8,128)S(1)} %add.42), channel_id=1, source_target_pairs={{0,2},{1,3},{2,0},{3,1},{4,6},{5,7},{6,4},{7,5},{8,10},{9,11},{10,... | collective-permute-start | bytes 98312 | tf_op jit(solution)/shard_map/ppermute | solution.py:258
  44.4 3.7 %collective-permute-start.4 = (f32[1,16,128]{2,1,0:T(8,128)S(1)}, f32[1,16,128]{2,1,0:T(8,128)S(1)}, u32[]{:S(2)}, u32[]{:S(2)}) collective-permute-start(f32[1,16,128]{2,1,0:T(8,128)S(1)} %get-tuple-element.18), channel_id=1, source_target_pairs={{0,4},{4,0},{8,12},{12,8},{16,20},{20,16},{24,28},{28,24},{1,5},{5... | collective-permute-start | bytes 24584 | tf_op jit(solution)/shard_map/ppermute | solution.py:258
  48.0 10.8 %collective-permute-start.7 = (f32[2,16,128]{2,1,0:T(8,128)S(1)}, f32[2,16,128]{2,1,0:T(8,128)S(1)}, u32[]{:S(2)}, u32[]{:S(2)}) collective-permute-start(f32[2,16,128]{2,1,0:T(8,128)S(1)} %pad_maximum_fusion.3), channel_id=1, source_target_pairs={{0,24},{4,28},{8,16},{12,20},{16,8},{20,12},{24,0},{28,4},{1,25},{... | collective-permute-start | bytes 49160 | tf_op jit(solution)/shard_map/ppermute | solution.py:258
  52.1 6.7 %collective-permute-start.6 = (f32[2,16,128]{2,1,0:T(8,128)S(1)}, f32[2,16,128]{2,1,0:T(8,128)S(1)}, u32[]{:S(2)}, u32[]{:S(2)}) collective-permute-start(f32[2,16,128]{2,1,0:T(8,128)S(1)} %pad_maximum_fusion.3), channel_id=1, source_target_pairs={{0,16},{4,20},{8,24},{12,28},{16,0},{20,4},{24,8},{28,12},{1,17},{... | collective-permute-start | bytes 49160 | tf_op jit(solution)/shard_map/ppermute | solution.py:258
  52.1 4.5 %collective-permute-start.5 = (f32[2,16,128]{2,1,0:T(8,128)S(1)}, f32[2,16,128]{2,1,0:T(8,128)S(1)}, u32[]{:S(2)}, u32[]{:S(2)}) collective-permute-start(f32[2,16,128]{2,1,0:T(8,128)S(1)} %pad_maximum_fusion.3), channel_id=1, source_target_pairs={{0,8},{4,12},{8,0},{12,4},{16,24},{20,28},{24,16},{28,20},{1,9},{5... | collective-permute-start | bytes 49160 | tf_op jit(solution)/shard_map/ppermute | solution.py:258
  58.8 9.3 %copy-start.10 = (f32[4,256]{1,0:T(4,128)S(1)}, f32[4,256]{1,0:T(4,128)}, u32[]{:S(2)}) copy-start(f32[4,256]{1,0:T(4,128)} %value_ref.1) | copy-start | bytes 12292
  58.8 9.3 %copy-start.11 = (f32[4,256]{1,0:T(4,128)S(1)}, f32[4,256]{1,0:T(4,128)}, u32[]{:S(2)}) copy-start(f32[4,256]{1,0:T(4,128)} %variance_ref.1) | copy-start | bytes 12292
  58.8 40.9 %all-to-all-start = ((f32[8,4,3,2,16,128]{5,4,3,2,1,0:T(8,128)}), f32[8,4,3,2,16,128]{5,4,3,2,1,0:T(8,128)S(1)}, u32[]{:S(2)}, u32[]{:S(2)}) async-start(f32[8,4,3,2,16,128]{5,4,3,2,1,0:T(8,128)} %outer.1.height_ref), calls=%async_computation | async-start | bytes 3145728 | tf_op jit(solution)/shard_map/all_to_all | solution.py:743
  62.6 4.5 %collective-permute-start.10 = (f32[1,8,16,128]{3,2,1,0:T(8,128)S(1)}, f32[1,8,16,128]{3,2,1,0:T(8,128)S(1)}, u32[]{:S(2)}, u32[]{:S(2)}) collective-permute-start(f32[1,8,16,128]{3,2,1,0:T(8,128)S(1)} %bitcast.37), channel_id=1, source_target_pairs={{0,3},{1,2},{2,1},{3,0},{4,7},{5,6},{6,5},{7,4},{8,11},{9,10},{10,... | collective-permute-start | bytes 196616 | tf_op jit(solution)/shard_map/ppermute | solution.py:258
  62.7 5.4 %collective-permute-start.9 = (f32[1,8,16,128]{3,2,1,0:T(8,128)S(1)}, f32[1,8,16,128]{3,2,1,0:T(8,128)S(1)}, u32[]{:S(2)}, u32[]{:S(2)}) collective-permute-start(f32[1,8,16,128]{3,2,1,0:T(8,128)S(1)} %bitcast.38), channel_id=1, source_target_pairs={{0,2},{1,3},{2,0},{3,1},{4,6},{5,7},{6,4},{7,5},{8,10},{9,11},{10,... | collective-permute-start | bytes 196616 | tf_op jit(solution)/shard_map/ppermute | solution.py:258
  64.0 4.2 %collective-permute-start.8 = (f32[1,8,16,128]{3,2,1,0:T(8,128)S(1)}, f32[1,8,16,128]{3,2,1,0:T(8,128)S(1)}, u32[]{:S(2)}, u32[]{:S(2)}) collective-permute-start(f32[1,8,16,128]{3,2,1,0:T(8,128)S(1)} %bitcast.39), channel_id=1, source_target_pairs={{0,1},{1,0},{2,3},{3,2},{4,5},{5,4},{6,7},{7,6},{8,9},{9,8},{10,11... | collective-permute-start | bytes 196616 | tf_op jit(solution)/shard_map/ppermute | solution.py:258
  68.2 8.8 %copy-start.9 = (s32[2]{0:T(128)S(1)}, s32[2]{0:T(128)}, u32[]{:S(2)}) copy-start(s32[2]{0:T(128)} %constant.77.clone.tile_ref) | copy-start | bytes 28
  86.1 1.0 copy-start.1
  87.2 0.9 copy-start.3
  88.1 0.8 copy-start.5
  99.7 1.3 %copy-start.2 = (f32[4,2,6,48,4]{4,3,2,1,0:T(8,128)S(1)}, f32[4,2,6,48,4]{4,3,2,1,0:T(8,128)}, u32[]{:S(2)}) copy-start(f32[4,2,6,48,4]{4,3,2,1,0:T(8,128)} %copy-done.1) | copy-start | bytes 110596
  101.0 1.1 %copy-start.4 = (bf16[4,2,6,32,144]{4,3,2,1,0:T(8,128)(2,1)S(1)}, bf16[4,2,6,32,144]{4,3,2,1,0:T(8,128)(2,1)}, u32[]{:S(2)}) copy-start(bf16[4,2,6,32,144]{4,3,2,1,0:T(8,128)(2,1)} %copy-done.3) | copy-start | bytes 1327108
  102.1 1.1 copy-start.6

commit v6 on v5

--- a/solution.py
+++ b/solution.py
@@ -12,7 +12,6 @@
 LANES = 128
 OBS_BLOCK = 48
 ROW_TILE = 8
-VMEM_LIMIT = 48 * 2**20
 OUTER_COST = pl.CostEstimate(flops=23 * 10**9, bytes_accessed=74 * 10**6, transcendentals=0)
 CHAIN_COST = pl.CostEstimate(flops=26 * 10**9, bytes_accessed=85 * 10**6, transcendentals=0)
 
@@ -24,12 +23,16 @@
 TN = (((0,), (0,)), ((), ()))
 
 
-def params():
-    return pltpu.CompilerParams(vmem_limit_bytes=VMEM_LIMIT)
+def params(mebibytes):
+    return pltpu.CompilerParams(vmem_limit_bytes=mebibytes * 2**20)
 
 
 def vmem(count=1):
     return [pl.BlockSpec(memory_space=pltpu.VMEM)] * count
+
+
+def hbm(count=1):
+    return [pl.BlockSpec(memory_space=pltpu.HBM)] * count
 
 
 def smem(count=1):
@@ -80,84 +83,73 @@
             height[t] = height[t] - (row_centred(half_depth[t] * east[t]) + flow_y)
 
 
-def forecast_kernel(joins, kept, parity_ref, *refs):
+def forecast_kernel(joins, kept, *refs):
     ens_ref, depth_ref, *halos, out_ref, height, east, north, half_depth = refs
-    blocks, _, fields, out_tiles = out_ref.shape[:4]
-    odd = parity_ref[0] == 1
-
-    def window(block, near, far):
+    tiles = height.shape[0]
+    out_tiles = out_ref.shape[2]
+    fields = ens_ref.shape[1]
+
+    def window(block, above, below, t):
+        part = slice(t * LANES, (t + 1) * LANES)
         if not joins:
-            return block
-        return jnp.concatenate([jnp.where(odd, near, far), block, jnp.where(odd, far, near)], 0)
-
-    near_ref, far_ref, near_depth_ref, far_depth_ref = halos if joins else [None] * 4
-    tiles = height.shape[0]
-
-    def part(ref, index, t):
-        return None if ref is None else ref[index][:, t * LANES : (t + 1) * LANES]
+            return block[:, part]
+        return jnp.concatenate([above[:, part], block[:, part], below[:, part]], 0)
+
+    up_ref, down_ref, depth_up_ref, depth_down_ref = halos if joins else [None] * 4
 
     @pl.when(pl.program_id(0) == 0)
     def _():
         for t in range(tiles):
-            half_depth[t] = (0.5 * step_size) * window(
-                depth_ref[:, t * LANES : (t + 1) * LANES],
-                part(near_depth_ref, 0, t),
-                part(far_depth_ref, 0, t),
-            )
+            above, below = (depth_up_ref.at[0], depth_down_ref.at[0]) if joins else (None, None)
+            half_depth[t] = (0.5 * step_size) * window(depth_ref, above, below, t)
 
     state = (height, east, north)
     for f in range(fields):
+        above, below = (up_ref.at[f], down_ref.at[f]) if joins else (None, None)
         for t in range(tiles):
-            state[f][t] = window(
-                ens_ref[0, f, :, t * LANES : (t + 1) * LANES],
-                part(near_ref, f, t),
-                part(far_ref, f, t),
-            )
+            state[f][t] = window(ens_ref.at[0, f], above, below, t)
     forecast_steps(*state, half_depth)
     for f in range(fields):
         for t in range(tiles):
-            place = 0
-            for first, count in kept:
-                out_ref[t // out_tiles, 0, f, t % out_tiles, place : place + count] = state[f][
-                    t, first : first + count
+            for place, tile in enumerate(kept):
+                out_ref[t // out_tiles, place, t % out_tiles, 0, f] = state[f][
+                    t, tile * ROW_TILE : (tile + 1) * ROW_TILE
                 ]
-                place += count
-
-
-def forecast(name, kept, parity, ensemble, depth, blocks, halos=()):
+
+
+def forecast(name, kept, ensemble, depth, blocks, halos=()):
     members, fields, rows, columns = ensemble.shape
     tiles = columns // LANES
     window_rows = rows + (2 * HALO if halos else 0)
-    out_shape = (blocks, members, fields, tiles // blocks, sum(n for _, n in kept), LANES)
-    in_specs = smem() + [
+    out_shape = (blocks, len(kept), tiles // blocks, members, fields, ROW_TILE, LANES)
+    in_specs = [
         pl.BlockSpec((1, fields, rows, columns), lambda m: (m, 0, 0, 0)),
         pl.BlockSpec((rows, columns), lambda m: (0, 0)),
     ]
-    operands = [parity, ensemble, depth]
     if halos:
         in_specs += [pl.BlockSpec((fields, HALO, columns), lambda m: (m, 0, 0))] * 2
         in_specs += [pl.BlockSpec((1, HALO, columns), lambda m: (members * fields, 0, 0))] * 2
-        operands += [*halos, *halos]
     return pl.pallas_call(
         functools.partial(forecast_kernel, bool(halos), kept),
         grid=(members,),
         in_specs=in_specs,
         out_specs=pl.BlockSpec(
-            (blocks, 1) + out_shape[2:], lambda m: (0, m, 0, 0, 0, 0)
+            out_shape[:3] + (1,) + out_shape[4:], lambda m: (0, 0, 0, m, 0, 0, 0)
         ),
         out_shape=jax.ShapeDtypeStruct(out_shape, jnp.float32),
         scratch_shapes=[pltpu.VMEM((tiles, window_rows, LANES), jnp.float32)] * 4,
-        compiler_params=params(),
+        compiler_params=params(16),
         cost_estimate=OUTER_COST if halos else None,
         name=name,
-    )(*operands)
+    )(ensemble, depth, *halos)
 
 
 def pick(row_ref, col_ref, height_ref):
-    blocks, members, _, tiles, rows, _ = height_ref.shape
+    blocks, row_tiles, tiles, members, _, _, _ = height_ref.shape
+    rows = row_tiles * ROW_TILE
     heights = jnp.concatenate(
         [
-            height_ref[d, :, 0, t].reshape(members * rows, LANES)
+            height_ref[d, :, t, :, 0].reshape(rows * members, LANES)
             for d in range(blocks)
             for t in range(tiles)
         ],
@@ -176,9 +168,13 @@
     )
     size = members * rows
     found = (found[:size] + found[size : 2 * size]) + found[2 * size :]
-    found = found.reshape(members, rows, count)
-    row = lax.broadcasted_iota(jnp.int32, (1, rows, count), 1)
-    return jnp.sum(jnp.where(row == row_ref[...][None], found, 0.0), 1)
+    found = found.reshape(row_tiles, members, ROW_TILE, count)
+    row = lax.broadcasted_iota(jnp.int32, (1, ROW_TILE, count), 1)
+    result = 0.0
+    for i in range(row_tiles):
+        here = row + i * ROW_TILE == row_ref[...][None]
+        result = result + jnp.sum(jnp.where(here, found[i], 0.0), 1)
+    return result
 
 
 def pick_inner_kernel(row_ref, col_ref, height_ref, out_ref):
@@ -202,8 +198,8 @@
 
 
 def height_spec(sent):
-    blocks, members, _, tiles, rows, _ = sent.shape
-    return pl.BlockSpec((blocks, members, 1, tiles, rows, LANES), lambda i: (0,) * 6)
+    shape = sent.shape[:4] + (1,) + sent.shape[5:]
+    return pl.BlockSpec(shape, lambda i: (0,) * len(shape))
 
 
 def whole_spec(shape):
@@ -211,14 +207,14 @@
 
 
 def pick_inner(row, col, sent):
-    shape = (sent.shape[1], col.shape[1])
+    shape = (sent.shape[3], col.shape[1])
     return pl.pallas_call(
         pick_inner_kernel,
         grid=(1,),
         in_specs=[whole_spec(row.shape), whole_spec(col.shape), height_spec(sent)],
         out_specs=whole_spec(shape),
         out_shape=jax.ShapeDtypeStruct(shape, jnp.float32),
-        compiler_params=params(),
+        compiler_params=params(40),
         name="pick_inner",
     )(row, col, sent)
 
@@ -239,7 +235,7 @@
         ],
         out_specs=whole_spec(shape),
         out_shape=jax.ShapeDtypeStruct(shape, jnp.float32),
-        compiler_params=params(),
+        compiler_params=params(40),
         name="pick_outer",
     )(row, col, sent, inner, radius)
 
@@ -333,12 +329,16 @@
     cutoff_ref,
     lhs1_ref,
     lhs2_ref,
-    place_ref,
+    more1_ref,
+    more2_ref,
     count_ref,
     local_ref,
     anom_ref,
     mix_ref,
     rank_ref,
+    block1_ref,
+    block2_ref,
+    sem,
 ):
     size_x, size_y = sizes
     pieces, sources, _, _ = every_ref.shape
@@ -394,7 +394,7 @@
         rank_ref[b, t] = jnp.where(reaches, ranks.astype(jnp.int32) - 1, -1)
         count_ref[b, t] = jnp.sum(flags[0:1, :]).astype(jnp.int32)
 
-    def gather(b, t, k):
+    def gather(b, t, k, to1, to2):
         chosen = (slot == rank_ref[b, t, 0:1, :] - k * OBS_BLOCK).astype(jnp.float32)
         thrice = jnp.concatenate([chosen] * 3, 0).astype(jnp.bfloat16)
         chosen = chosen.astype(jnp.bfloat16)
@@ -402,17 +402,10 @@
         def product(x, y):
             return lax.dot_general(x, y, NT, preferred_element_type=jnp.float32)
 
-        lhs1_ref[b, t, k] = product(chosen, anom_ref[b]).astype(jnp.bfloat16)
-        lhs2_ref[b, t, k] = jnp.where(
+        to1[...] = product(chosen, anom_ref[b]).astype(jnp.bfloat16)
+        to2[...] = jnp.where(
             twice, product(mix_ref[b, 0], thrice), product(mix_ref[b, 1], thrice)
         ).astype(jnp.bfloat16)
-        cells = row_ref[:, b * count : (b + 1) * count]
-        place_ref[b, t, k] = product(
-            chosen,
-            jnp.concatenate([cells // 256, cells % 256], 0)
-            .astype(jnp.float32)
-            .astype(jnp.bfloat16),
-        )
 
     def localize(b, first, size):
         later = slice((b + 1) * count, batches * count)
@@ -440,7 +433,10 @@
         )
         aside = [functools.partial(rank_reaching, b, t) for t in range(tiles)]
         if b > 0:
-            aside += [functools.partial(gather, b - 1, t, 0) for t in range(tiles)]
+            aside += [
+                functools.partial(gather, b - 1, t, 0, lhs1_ref.at[b - 1, t], lhs2_ref.at[b - 1, t])
+                for t in range(tiles)
+            ]
         if b + 1 < batches:
             aside += [functools.partial(localize, b, first, 32) for first in range(0, count, 32)]
         steps = members // 4
@@ -455,7 +451,9 @@
         )
         mix = (solved_innov - 0.5 * solved_anom) / (members - 1)
         high, low = split_bf16(anom)
-        anom_ref[b] = jnp.concatenate([high, high, low], 0)
+        cells = row_ref[:, here]
+        cells = jnp.concatenate([cells // 256, cells % 256] * 4, 0).astype(jnp.float32)
+        anom_ref[b] = jnp.concatenate([high, high, low, cells.astype(jnp.bfloat16)], 0)
         mix_high, mix_low = split_bf16(mix)
         mix_ref[b, 0] = mix_high
         mix_ref[b, 1] = mix_low
@@ -476,7 +474,7 @@
             heights = jnp.concatenate([heights[:, : (b + 1) * count], ahead], 1)
 
     for t in range(tiles):
-        gather(batches - 1, t, 0)
+        gather(batches - 1, t, 0, lhs1_ref.at[batches - 1, t], lhs2_ref.at[batches - 1, t])
     counts = [[count_ref[b, t] for t in range(tiles)] for b in range(batches)]
     most = functools.reduce(jnp.maximum, sum(counts, []))
 
@@ -486,7 +484,13 @@
             for t in range(tiles):
 
                 def more(k, _, b=b, t=t):
-                    gather(b, t, k)
+                    gather(b, t, k, block1_ref, block2_ref)
+                    for i, (block, to) in enumerate(
+                        ((block1_ref, more1_ref), (block2_ref, more2_ref))
+                    ):
+                        copy = pltpu.make_async_copy(block, to.at[b, t, k - 1], sem.at[i])
+                        copy.start()
+                        copy.wait()
                     return 0
 
                 blocks = (counts[b][t] + (OBS_BLOCK - 1)) // OBS_BLOCK
@@ -498,24 +502,30 @@
     row_form = jnp.stack([obs_x.reshape(-1), obs_y.reshape(-1)], 0)
     col_form = jnp.concatenate([obs_x, obs_y], 0).T
     tiles = cutoff.shape[1] // LANES
-    slots = (batches, tiles, -(-count // OBS_BLOCK))
+    first = (batches, tiles)
+    more = first + (max(-(-count // OBS_BLOCK) - 1, 1),)
+    shape1 = (OBS_BLOCK, 3 * members + 16)
+    shape2 = (members, 3 * OBS_BLOCK)
     return pl.pallas_call(
         functools.partial(chain_kernel, members, sizes),
         in_specs=smem() + vmem(6),
-        out_specs=vmem(3) + smem(),
+        out_specs=vmem(2) + hbm(2) + smem(),
         out_shape=[
-            jax.ShapeDtypeStruct(slots + (OBS_BLOCK, 3 * members), jnp.bfloat16),
-            jax.ShapeDtypeStruct(slots + (members, 3 * OBS_BLOCK), jnp.bfloat16),
-            jax.ShapeDtypeStruct(slots + (OBS_BLOCK, 4), jnp.float32),
-            jax.ShapeDtypeStruct(slots[:2], jnp.int32),
-        ],
+            jax.ShapeDtypeStruct(lead + shape, jnp.bfloat16)
+            for lead in (first, more)
+            for shape in (shape1, shape2)
+        ]
+        + [jax.ShapeDtypeStruct(first, jnp.int32)],
         scratch_shapes=[
             pltpu.VMEM((count, batches * count), jnp.float32),
-            pltpu.VMEM((batches, 3 * members, count), jnp.bfloat16),
+            pltpu.VMEM((batches, 3 * members + 16, count), jnp.bfloat16),
             pltpu.VMEM((batches, 2, members, count), jnp.bfloat16),
             pltpu.VMEM((batches, tiles, 8, count), jnp.int32),
+            pltpu.VMEM(shape1, jnp.bfloat16),
+            pltpu.VMEM(shape2, jnp.bfloat16),
+            pltpu.SemaphoreType.DMA((2,)),
         ],
-        compiler_params=params(),
+        compiler_params=params(16),
         cost_estimate=CHAIN_COST,
         name="chain",
     )(start, every, row_form, col_form, values, variance, cutoff)
@@ -531,12 +541,14 @@
     cutoff_ref,
     lhs1_ref,
     lhs2_ref,
-    place_ref,
+    more1_ref,
+    more2_ref,
     *rest,
 ):
-    out_ref, members_ref, rhs_ref = rest[1:] if continues else rest
+    out_ref, members_ref, rhs_ref, block1_ref, block2_ref, sem = rest[1:] if continues else rest
     size_x, size_y = float(sizes[0]), float(sizes[1])
-    members, fields, _, rows, _ = state_ref.shape
+    sources, _, _, local_members, fields, rows, _ = state_ref.shape
+    members = sources * local_members
     batches = lhs1_ref.shape[0]
     cells = rows * LANES
     t = pl.program_id(1)
@@ -549,8 +561,8 @@
     radius_sq = radius * radius
     inverse = 1.0 / radius_sq
 
-    def localized(b, k):
-        place = place_ref[b, 0, k]
+    def localized(lhs1):
+        place = lhs1[:, 3 * members :].astype(jnp.float32)
         obs_x = jnp.broadcast_to(place[:, 0:1] * 256.0 + place[:, 2:3], (OBS_BLOCK, LANES))
         obs_y = jnp.broadcast_to(place[:, 1:2] * 256.0 + place[:, 3:4], (OBS_BLOCK, LANES))
         dist_y = apart_sq(obs_y, lane + col0, size_y)
@@ -561,13 +573,13 @@
             weights.append(jnp.square(jnp.maximum(1.0 - ratio, 0.0)))
         return jnp.concatenate(weights, 1)
 
-    def contribution(b, k, weights, rhs):
-        cross = jnp.dot(lhs1_ref[b, 0, k], rhs, preferred_element_type=jnp.float32)
+    def crossed(lhs1, rhs):
+        return jnp.dot(lhs1[:, : 3 * members], rhs, preferred_element_type=jnp.float32)
+
+    def moved(lhs2, cross, weights):
         high, low = split_bf16(cross * weights)
         return jnp.dot(
-            lhs2_ref[b, 0, k],
-            jnp.concatenate([high, low, high], 0),
-            preferred_element_type=jnp.float32,
+            lhs2, jnp.concatenate([high, low, high], 0), preferred_element_type=jnp.float32
         )
 
     def split_anom(state):
@@ -597,15 +609,11 @@
     def _():
         states = [load(f) for f in range(fields)]
         for b in range(batches):
-            weights = localized(b, 0)
-            rhs = [split_anom(x) for x in states]
-            cross = [jnp.dot(lhs1_ref[b, 0, 0], x, preferred_element_type=jnp.float32) for x in rhs]
-            gain = []
-            for c in cross:
-                high, low = split_bf16(c * weights)
-                gain.append(jnp.concatenate([high, low, high], 0))
-            moved = [jnp.dot(lhs2_ref[b, 0, 0], g, preferred_element_type=jnp.float32) for g in gain]
-            states = [x + y for x, y in zip(states, moved)]
+            lhs1 = lhs1_ref[b, 0]
+            weights = localized(lhs1)
+            cross = [crossed(lhs1, x) for x in [split_anom(state) for state in states]]
+            steps = [moved(lhs2_ref[b, 0], c, weights) for c in cross]
+            states = [state + step for state, step in zip(states, steps)]
         for f in range(fields):
             store(f, states[f])
 
@@ -617,20 +625,29 @@
             for f in range(fields):
                 rhs_ref[f] = split_anom(members_ref[f])
 
+            def add(lhs1, lhs2):
+                weights = localized(lhs1)
+                for f in range(fields):
+                    members_ref[f] += moved(lhs2, crossed(lhs1, rhs_ref[f]), weights)
+
             def block(k, _, b=b):
-                weights = localized(b, k)
-                for f in range(fields):
-                    members_ref[f] += contribution(b, k, weights, rhs_ref[f])
+                for i, (more, to) in enumerate(((more1_ref, block1_ref), (more2_ref, block2_ref))):
+                    copy = pltpu.make_async_copy(more.at[b, t, k - 1], to, sem.at[i])
+                    copy.start()
+                    copy.wait()
+                add(block1_ref[...], block2_ref[...])
                 return 0
 
+            add(lhs1_ref[b, 0], lhs2_ref[b, 0])
             blocks = (count_ref[b, t] + (OBS_BLOCK - 1)) // OBS_BLOCK
-            lax.fori_loop(0, blocks, block, 0)
+            lax.fori_loop(1, blocks, block, 0)
         for f in range(fields):
             store(f, members_ref[f])
 
 
-def update(row_tiles, start, counts, state, cutoff, lhs1, lhs2, place, sizes, begun=None):
-    members, fields, tiles, _, _ = state.shape
+def update(row_tiles, start, counts, state, cutoff, lhs, sizes, begun=None):
+    sources, _, tiles, local_members, fields, _, _ = state.shape
+    members = sources * local_members
     rows = cutoff.shape[0]
     columns = tiles * LANES
     cells = ROW_TILE * LANES
@@ -639,16 +656,16 @@
         shape = (array.shape[0], 1) + array.shape[2:]
         return pl.BlockSpec(shape, lambda i, t, tile: (0, t) + (0,) * (array.ndim - 2))
 
-    operands = [row_tiles, start, counts, state, cutoff, lhs1, lhs2, place]
+    operands = [row_tiles, start, counts, state, cutoff, *lhs]
     in_specs = smem(2) + [
         pl.BlockSpec(
-            (members, fields, 1, ROW_TILE, LANES), lambda i, t, tile: (0, 0, t, i, 0)
+            (sources, 1, 1, local_members, fields, ROW_TILE, LANES),
+            lambda i, t, tile: (0, i, t, 0, 0, 0, 0),
         ),
         pl.BlockSpec((ROW_TILE, LANES), lambda i, t, tile: (tile[i], t)),
-        of_tile(lhs1),
-        of_tile(lhs2),
-        of_tile(place),
-    ]
+        of_tile(lhs[0]),
+        of_tile(lhs[1]),
+    ] + hbm(2)
     aliases = {}
     if begun is not None:
         aliases = {len(operands): 0}
@@ -666,38 +683,55 @@
             scratch_shapes=[
                 pltpu.VMEM((fields, members, cells), jnp.float32),
                 pltpu.VMEM((fields, 3 * members, cells), jnp.bfloat16),
+                pltpu.VMEM(lhs[0].shape[2:], jnp.bfloat16),
+                pltpu.VMEM(lhs[1].shape[2:], jnp.bfloat16),
+                pltpu.SemaphoreType.DMA((2,)),
             ],
         ),
         out_shape=jax.ShapeDtypeStruct((members, fields, rows, columns), jnp.float32),
         input_output_aliases=aliases,
-        compiler_params=params(),
+        compiler_params=params(16),
         name="update",
     )(*operands)
 
 
+def edge_kernel(ens_ref, depth_ref, first_ref, last_ref, sem):
+    members, fields, rows, _ = ens_ref.shape
+    copies = []
+    for i, (out_ref, row) in enumerate(((first_ref, 0), (last_ref, rows - HALO))):
+        part = pl.ds(row, HALO)
+        for m in range(members):
+            to = out_ref.at[pl.ds(m * fields, fields)]
+            copies.append(pltpu.make_async_copy(ens_ref.at[m, :, part], to, sem.at[i, m]))
+        to = out_ref.at[members * fields]
+        copies.append(pltpu.make_async_copy(depth_ref.at[part], to, sem.at[i, members]))
+    for copy in copies:
+        copy.start()
+    for copy in copies:
+        copy.wait()
+
+
 def row_halos(ensemble, depth, axis):
     size = lax.axis_size(axis)
-    odd = lax.axis_index(axis) % 2 == 1
-    columns = depth.shape[1]
-
-    def edge(start):
-        return jnp.concatenate(
-            [
-                ensemble[:, :, start : start + HALO].reshape(-1, HALO, columns),
-                depth[None, start : start + HALO],
-            ],
-            0,
-        )
-
-    first, last = edge(0), edge(depth.shape[0] - HALO)
-    far = [(i, (i + (1 if i % 2 else -1)) % size) for i in range(size)]
-    return (
-        exchange(jnp.where(odd, first, last), axis, 1),
-        lax.ppermute(jnp.where(odd, last, first), axis, far),
-    )
+    onward = [(i, (i + 1) % size) for i in range(size)]
+    backward = [(j, i) for i, j in onward]
+    members, fields, _, columns = ensemble.shape
+    edge = jax.ShapeDtypeStruct((members * fields + 1, HALO, columns), jnp.float32)
+    first, last = pl.pallas_call(
+        edge_kernel,
+        in_specs=hbm(2),
+        out_specs=vmem(2),
+        out_shape=[edge, edge],
+        scratch_shapes=[pltpu.SemaphoreType.DMA((2, members + 1))],
+        compiler_params=params(16),
+        name="edges",
+    )(ensemble, depth)
+    return lax.ppermute(last, axis, onward), lax.ppermute(first, axis, backward)
 
 
 def local(ensemble, sea_depth, cutoff, obs_index, obs_value, obs_var):
+    ensemble = pltpu.with_memory_space_constraint(ensemble, pltpu.HBM)
+    sea_depth = pltpu.with_memory_space_constraint(sea_depth, pltpu.HBM)
     blocks = lax.axis_size("mem")
     subs = lax.axis_size("sub")
     local_members, fields, rows, size_y = ensemble.shape
@@ -706,23 +740,20 @@
     size_x = rows * subs
     sizes = (size_x, size_y)
     sub, mem = lax.axis_index("sub"), lax.axis_index("mem")
-    odd = sub % 2
     x_start = sub * rows
     y_start = mem * col_block
     start = jnp.stack([x_start, y_start, sub, mem]).astype(jnp.int32)
-    parity = odd.astype(jnp.int32)[None]
     obs_x = obs_index // size_y
     obs_y = obs_index % size_y
     flat_x = obs_x.reshape(1, -1)
     flat_y = obs_y.reshape(1, -1)
 
-    halos = row_halos(ensemble, sea_depth, "sub")
+    halos = row_halos(ensemble, sea_depth, "sub") * 2
     radius_part = pick_radius(cutoff, flat_x[0], flat_y[0], x_start, y_start)[None]
 
     inner_rows = rows - 2 * HALO
-    sent_inner = forecast(
-        "inner", [(HALO, inner_rows)], parity, ensemble, sea_depth, blocks
-    )
+    last = rows // ROW_TILE - 1
+    sent_inner = forecast("inner", range(1, last), ensemble, sea_depth, blocks)
     received_inner = lax.all_to_all(
         sent_inner, "mem", split_axis=0, concat_axis=0, tiled=True
     )
@@ -732,9 +763,7 @@
     outer_row = jnp.where(
         row < HALO, row, jnp.where(row < rows - HALO, -1, row - inner_rows)
     )
-    sent_outer = forecast(
-        "outer", [(HALO, HALO), (rows, HALO)], parity, ensemble, sea_depth, blocks, halos
-    )
+    sent_outer = forecast("outer", [1, last + 1], ensemble, sea_depth, blocks, halos)
     part = pick_outer(outer_row, flat_y, sent_outer, inner_heights, radius_part, subs)
     piece = lax.dynamic_index_in_dim(sum_over(part, "sub"), sub, 0, keepdims=True)
     low = max(blocks // 4, 1)
@@ -744,18 +773,16 @@
         sent_outer, "mem", split_axis=0, concat_axis=0, tiled=True
     )
     every = gather_over(every[None], "sub")
-    lhs1, lhs2, place, counts = chain(
+    *lhs, counts = chain(
         members, start, every, obs_x, obs_y, obs_value, obs_var, cutoff, sizes
     )
 
+    lhs[2:] = [pltpu.with_memory_space_constraint(more, pltpu.HBM) for more in lhs[2:]]
+
     def analyse(received, row_tiles, begun=None):
-        state = received.reshape((members,) + received.shape[2:])
         row_tiles = jnp.array(row_tiles, jnp.int32)
-        return update(
-            row_tiles, start, counts, state, cutoff, lhs1, lhs2, place, sizes, begun
-        )
-
-    last = rows // ROW_TILE - 1
+        return update(row_tiles, start, counts, received, cutoff, lhs, sizes, begun)
+
     return analyse(received_outer, [0, last], analyse(received_inner, list(range(1, last))))
 
 

time: 113 us -> 109 us (0.965)
  local copies, waits for them, and re-layouts: 8.78 us -> 3.16 us
  Pallas kernels: 49.4 us -> 52.6 us
    unnamed x33 -> x23, local copies, waits for them, and re-layouts: 6.26 us -> 3.03 us
    pallas_call x0 -> x1, Pallas kernels: none -> 2.47 us  [row_halos(): pl.pallas_call(edge_kernel, in_specs=hbm(2), out_specs=vmem(2), out_shape...]
    ppermute x1 -> x2, waiting for transfers between devices: 2.62 us -> 0.88 us  [the longest x1 0.88 us: row_halos(): lax.ppermute(first, axis, backward)]
    slice x1 -> x0, local copies, waits for them, and re-layouts: 1.51 us -> none  [edge(): ensemble[:, :, start:start + HALO].reshape(-1, HALO, columns)]
    ppermute x10 -> x9, waiting for transfers between devices: 14.1 us -> 15.5 us  [exchange(): return lax.ppermute(value, axis, [(i, i ^ distance) for i in range(size)])]
    select_n x1 -> x0, other arithmetic: 1.39 us -> none  [row_halos(): jnp.where(odd, last, first)]
    pallas_call x2, Pallas kernels: 18.1 us -> 19.3 us  [forecast(): pl.pallas_call(functools.partial(forecast_kernel, bool(halos), kept), gri...]
    ppermute x10 -> x9, starting transfers between devices: 11.9 us -> 11.3 us  [exchange(): return lax.ppermute(value, axis, [(i, i ^ distance) for i in range(size)])]
  transfers between devices with their start and end apart: 13 -> 13, of which waited for: 9 -> 9; matrix products, arithmetic and copies ran while one was open for 1% -> 1% of each run, Pallas kernels for 36% -> 38%
where the time goes in v6:
time: 109 us
  Pallas kernels  52.6 us (48%)
  waiting for transfers between devices  26.9 us (25%)
  starting transfers between devices  24.2 us (22%)
  local copies, waits for them, and re-layouts  3.16 us (3%)
    pallas_call x2, Pallas kernels, forecast(): pl.pallas_call(functools.partial(forecast_kernel, bool(halos), kept), gri...  19.3 us
    pallas_call x2, Pallas kernels, update(): pl.pallas_call(functools.partial(update_kernel, sizes, begun is not None)...  17.8 us
    ppermute x9, waiting for transfers between devices, exchange(): return lax.ppermute(value, axis, [(i, i ^ distance) for i in range(size)])  15.5 us
    ppermute x9, starting transfers between devices, exchange(): return lax.ppermute(value, axis, [(i, i ^ distance) for i in range(size)])  11.3 us
    all_to_all x1, waiting for transfers between devices, local(): lax.all_to_all(sent_outer, 'mem', split_axis=0, concat_axis=0, tiled=True)  10.5 us
    pallas_call x1, Pallas kernels, chain(): pl.pallas_call(functools.partial(chain_kernel, members, sizes), in_specs=...  8.73 us
    all_to_all x1, starting transfers between devices, local(): lax.all_to_all(sent_inner, 'mem', split_axis=0, concat_axis=0, tiled=True)  6.66 us
    all_to_all x1, starting transfers between devices, local(): lax.all_to_all(sent_outer, 'mem', split_axis=0, concat_axis=0, tiled=True)  3.77 us
  transfers between devices with their start and end apart: 13, of which 9 were waited for; matrix products, arithmetic and copies ran while one was open for 1% of the time, Pallas kernels for 38%

profile of v6, /device:TPU:0, one launch (start us, length us, event | category | flops | bytes accessed | tf_op | source)
XLA Modules:
  0.0 108.6 jit_solution(6414420202892380538)
XLA Ops:
  0.0 2.5 %edges.1 = (f32[13,8,2048]{2,1,0:T(8,128)S(1)}, f32[13,8,2048]{2,1,0:T(8,128)}) custom-call(f32[4,3,32,2048]{3,2,1,0:T(8,128)} %refs_0_.3, f32[32,2048]{1,0:T(8,128)} %refs_1_.3), custom_call_target="tpu_custom_call" | custom-call | tf_op jit(solution)/shard_map/edges/pallas_call | solution.py:720
  2.5 0.5 collective-permute-start
  3.0 2.0 %collective-permute-start.1 = (f32[13,8,2048]{2,1,0:T(8,128)S(1)}, f32[13,8,2048]{2,1,0:T(8,128)}, u32[]{:S(2)}, u32[]{:S(2)}) collective-permute-start(f32[13,8,2048]{2,1,0:T(8,128)S(1)} %get-tuple-element.15), channel_id=1, source_target_pairs={{1,0},{2,1},{3,2},{0,3},{5,4},{6,5},{7,6},{4,7},{9,8},{10,9},{11,1... | collective-permute-start | bytes 2555912 | tf_op jit(solution)/shard_map/ppermute | solution.py:729
  5.0 8.5 %inner.1.height_ref = f32[8,2,2,4,3,8,128]{6,5,4,3,2,1,0:T(8,128)} custom-call(f32[4,3,32,2048]{3,2,1,0:T(8,128)} %refs_0_.3, f32[32,2048]{1,0:T(8,128)} %refs_1_.3), custom_call_target="tpu_custom_call" | custom-call | tf_op jit(solution)/shard_map/inner/pallas_call | solution.py:132
  13.6 0.0 copy-start.7
  13.6 6.7 %all-to-all-start.1 = ((f32[8,2,2,4,3,8,128]{6,5,4,3,2,1,0:T(8,128)}), f32[8,2,2,4,3,8,128]{6,5,4,3,2,1,0:T(8,128)S(1)}, u32[]{:S(2)}, u32[]{:S(2)}) async-start(f32[8,2,2,4,3,8,128]{6,5,4,3,2,1,0:T(8,128)} %inner.1.height_ref), calls=%async_computation.1 | async-start | bytes 3145728 | tf_op jit(solution)/shard_map/all_to_all | solution.py:757
  20.2 0.0 copy-start.2
  20.2 0.0 copy-done.7
  20.3 2.2 %pick_inner.1.inner_ref = f32[4,1024]{1,0:T(4,128)S(1)} custom-call(s32[1,1024]{1,0:T(1,128)S(1)} %get-tuple-element.29.row_ref, s32[1,1024]{1,0:T(1,128)S(1)} %bitcast.20, f32[8,2,2,4,3,8,128]{6,5,4,3,2,1,0:T(8,128)} %inner.1.height_ref), custom_call_target="tpu_custom_call" | custom-call | tf_op jit(solution)/shard_map/pick_inner/pallas_call | solution.py:211
  22.5 0.0 copy-done.2
  22.5 0.8 fusion
  23.3 0.0 collective-permute-done.refs_2_.refs_4_
  23.3 0.9 collective-permute-done.1.refs_3_.refs_5_
  24.2 10.8 %outer.1.height_ref = f32[8,2,2,4,3,8,128]{6,5,4,3,2,1,0:T(8,128)} custom-call(f32[4,3,32,2048]{3,2,1,0:T(8,128)} %refs_0_.3, f32[32,2048]{1,0:T(8,128)} %refs_1_.3, f32[13,8,2048]{2,1,0:T(8,128)S(1)} %collective-permute-done.refs_2_.refs_4_, f32[13,8,2048]{2,1,0:T(8,128)} %collective-permute-done.1.refs_3_.refs_5_, ...), custom_call_target="tpu_custom_call" | custom-call | flops 23000000512 | bytes 74000000 | tf_op jit(solution)/shard_map/outer/pallas_call | solution.py:132
  35.0 2.2 %pick_outer.1 = f32[4,16,128]{2,1,0:T(8,128)S(1)} custom-call(s32[1,1024]{1,0:T(1,128)S(1)} %get-tuple-element.30.row_ref, s32[1,1024]{1,0:T(1,128)S(1)} %bitcast.21, f32[8,2,2,4,3,8,128]{6,5,4,3,2,1,0:T(8,128)} %outer.1.height_ref, f32[4,1024]{1,0:T(4,128)S(1)} %pick_inner.1.inner_ref, f32[1,1024]{1,0:T(1,128)S(1)} %bitcast.23), custom_call_target="tpu_custom_call" | custom-call | tf_op jit(solution)/shard_map/pick_outer/pallas_call | solution.py:226
  37.1 0.6 collective-permute-start.2
  37.8 0.9 collective-permute-done.2
  38.6 2.4 %collective-permute-start.3 = (f32[4,16,128]{2,1,0:T(8,128)S(1)}, f32[4,16,128]{2,1,0:T(8,128)S(1)}, u32[]{:S(2)}, u32[]{:S(2)}) collective-permute-start(f32[4,16,128]{2,1,0:T(8,128)S(1)} %add.36), channel_id=1, source_target_pairs={{0,2},{1,3},{2,0},{3,1},{4,6},{5,7},{6,4},{7,5},{8,10},{9,11},{10,... | collective-permute-start | bytes 98312 | tf_op jit(solution)/shard_map/ppermute | solution.py:254
  41.1 1.9 %collective-permute-done.3 = f32[4,16,128]{2,1,0:T(8,128)S(1)} collective-permute-done((f32[4,16,128]{2,1,0:T(8,128)S(1)}, f32[4,16,128]{2,1,0:T(8,128)S(1)}, u32[]{:S(2)}, u32[]{:S(2)}) %collective-permute-start.3) | collective-permute-done | bytes 32800 | tf_op jit(solution)/shard_map/ppermute | solution.py:254
  42.9 1.9 %collective-permute-start.4 = (f32[1,16,128]{2,1,0:T(8,128)S(1)}, f32[1,16,128]{2,1,0:T(8,128)S(1)}, u32[]{:S(2)}, u32[]{:S(2)}) collective-permute-start(f32[1,16,128]{2,1,0:T(8,128)S(1)} %get-tuple-element.24), channel_id=1, source_target_pairs={{0,4},{4,0},{8,12},{12,8},{16,20},{20,16},{24,28},{28,24},{1,5},{5... | collective-permute-start | bytes 24584 | tf_op jit(solution)/shard_map/ppermute | solution.py:254
  44.8 0.1 copy.28
  45.0 1.7 %collective-permute-done.4 = f32[1,16,128]{2,1,0:T(8,128)S(1)} collective-permute-done((f32[1,16,128]{2,1,0:T(8,128)S(1)}, f32[1,16,128]{2,1,0:T(8,128)S(1)}, u32[]{:S(2)}, u32[]{:S(2)}) %collective-permute-start.4) | collective-permute-done | bytes 8224 | tf_op jit(solution)/shard_map/ppermute | solution.py:254
  46.7 3.9 %collective-permute-start.7 = (f32[2,16,128]{2,1,0:T(8,128)S(1)}, f32[2,16,128]{2,1,0:T(8,128)S(1)}, u32[]{:S(2)}, u32[]{:S(2)}) collective-permute-start(f32[2,16,128]{2,1,0:T(8,128)S(1)} %pad_maximum_fusion.1), channel_id=1, source_target_pairs={{0,24},{4,28},{8,16},{12,20},{16,8},{20,12},{24,0},{28,4},{1,25},{... | collective-permute-start | bytes 49160 | tf_op jit(solution)/shard_map/ppermute | solution.py:254
  50.6 0.0 collective-permute-start.6
  50.6 0.6 collective-permute-start.5
  51.2 3.3 %collective-permute-done.5 = f32[2,16,128]{2,1,0:T(8,128)S(1)} collective-permute-done((f32[2,16,128]{2,1,0:T(8,128)S(1)}, f32[2,16,128]{2,1,0:T(8,128)S(1)}, u32[]{:S(2)}, u32[]{:S(2)}) %collective-permute-start.5) | collective-permute-done | bytes 16416 | tf_op jit(solution)/shard_map/ppermute | solution.py:254
  54.4 4.2 %collective-permute-done.6 = f32[2,16,128]{2,1,0:T(8,128)S(1)} collective-permute-done((f32[2,16,128]{2,1,0:T(8,128)S(1)}, f32[2,16,128]{2,1,0:T(8,128)S(1)}, u32[]{:S(2)}, u32[]{:S(2)}) %collective-permute-start.6) | collective-permute-done | bytes 16416 | tf_op jit(solution)/shard_map/ppermute | solution.py:254
  58.7 0.0 collective-permute-done.7
  58.7 0.0 all-to-all-done.1.state_ref
  58.7 3.8 %all-to-all-start = ((f32[8,2,2,4,3,8,128]{6,5,4,3,2,1,0:T(8,128)}), f32[8,2,2,4,3,8,128]{6,5,4,3,2,1,0:T(8,128)S(1)}, u32[]{:S(2)}, u32[]{:S(2)}) async-start(f32[8,2,2,4,3,8,128]{6,5,4,3,2,1,0:T(8,128)} %outer.1.height_ref), calls=%async_computation | async-start | bytes 3145728 | tf_op jit(solution)/shard_map/all_to_all | solution.py:772
  62.5 0.5 iota_multiply_fusion.tile_ref
  63.0 0.0 collective-permute-start.10
  63.0 1.3 %collective-permute-start.9 = (f32[1,8,16,128]{3,2,1,0:T(8,128)S(1)}, f32[1,8,16,128]{3,2,1,0:T(8,128)S(1)}, u32[]{:S(2)}, u32[]{:S(2)}) collective-permute-start(f32[1,8,16,128]{3,2,1,0:T(8,128)S(1)} %bitcast.25), channel_id=1, source_target_pairs={{0,2},{1,3},{2,0},{3,1},{4,6},{5,7},{6,4},{7,5},{8,10},{9,11},{10,... | collective-permute-start | bytes 196616 | tf_op jit(solution)/shard_map/ppermute | solution.py:254
  64.2 0.6 collective-permute-start.8
  64.8 0.1 pad_add_fusion.2.start_ref
  64.9 2.5 %collective-permute-done.10 = f32[1,8,16,128]{3,2,1,0:T(8,128)S(1)} collective-permute-done((f32[1,8,16,128]{3,2,1,0:T(8,128)S(1)}, f32[1,8,16,128]{3,2,1,0:T(8,128)S(1)}, u32[]{:S(2)}, u32[]{:S(2)}) %collective-permute-start.10) | collective-permute-done | bytes 65568 | tf_op jit(solution)/shard_map/ppermute | solution.py:254
  67.4 1.1 collective-permute-done.9
  68.4 0.0 collective-permute-done.8
  68.4 0.0 copy-start.5
  68.5 0.7 copy-done.5
  69.1 0.0 copy-start.6
  69.1 0.7 copy-done.6
  69.8 0.0 copy-start.3
  69.8 8.7 %chain.1 = (bf16[4,2,48,112]{3,2,1,0:T(8,128)(2,1)S(1)}, bf16[4,2,32,144]{3,2,1,0:T(8,128)(2,1)S(1)}, bf16[4,2,5,48,112]{4,3,2,1,0:T(8,128)(2,1)S(1)}, bf16[4,2,5,32,144]{4,3,2,1,0:T(8,128)(2,1)S(1)}, s32[4,2]{1,0:T(4,128)S(1)}) custom-call(s32[4]{0:T(128)S(1)} %pad_add_fusion.2.start_ref, f32[4,8,16,128]{3,2,1,0:T(8,128)S(1)} %pad_maximum_fusion.every_ref, ...), custom_call_target="tpu_custom_call" | custom-call | flops 25999998976 | bytes 85000000 | tf_op jit(solution)/shard_map/chain/pallas_call | solution.py:509
  78.6 0.0 copy-start
  78.6 0.8 copy-done
  79.4 0.0 copy-start.1
  79.4 0.8 copy-done.1
  80.2 0.0 copy-done.3
  80.2 0.0 copy-start.4
  80.2 8.9 %update.2.rest_0_ = f32[32,3,32,256]{3,2,1,0:T(8,128)} custom-call(s32[2]{0:T(128)S(1)} %copy-done.3, s32[4]{0:T(128)S(1)} %pad_add_fusion.2.start_ref, s32[4,2]{1,0:T(4,128)S(1)} %get-tuple-element.17.count_ref, f32[8,2,2,4,3,8,128]{6,5,4,3,2,1,0:T(8,128)S(1)} %all-to-all-done.1.state_ref, s32[32,256]{1,0:T(8,128)S(1)} %copy-done.2, ...), custom_call_target="tpu_custom_call" | custom-call | tf_op jit(solution)/shard_map/update/pallas_call | solution.py:674
  89.1 10.5 %all-to-all-done.state_ref = f32[8,2,2,4,3,8,128]{6,5,4,3,2,1,0:T(8,128)S(1)} async-done(((f32[8,2,2,4,3,8,128]{6,5,4,3,2,1,0:T(8,128)}), f32[8,2,2,4,3,8,128]{6,5,4,3,2,1,0:T(8,128)S(1)}, u32[]{:S(2)}, u32[]{:S(2)}) %all-to-all-start) | async-done | bytes 1572896 | tf_op jit(solution)/shard_map/all_to_all | solution.py:772
  99.6 0.0 copy-done.4
  99.6 8.9 %update.3 = f32[32,3,32,256]{3,2,1,0:T(8,128)} custom-call(s32[2]{0:T(128)S(1)} %copy-done.4, s32[4]{0:T(128)S(1)} %pad_add_fusion.2.start_ref, s32[4,2]{1,0:T(4,128)S(1)} %get-tuple-element.17.count_ref, f32[8,2,2,4,3,8,128]{6,5,4,3,2,1,0:T(8,128)S(1)} %all-to-all-done.state_ref, s32[32,256]{1,0:T(8,128)S(1)} %copy-done.2, ...), custom_call_target="tpu_custom_call", output_to_operand_aliasing={{}: (9, {})} | custom-call | tf_op jit(solution)/shard_map/update/pallas_call | solution.py:674
  (16 shorter events, 0.1 us)
Async XLA Ops:
  2.5 20.8 %collective-permute-start = (f32[13,8,2048]{2,1,0:T(8,128)}, f32[13,8,2048]{2,1,0:T(8,128)S(1)}, u32[]{:S(2)}, u32[]{:S(2)}) collective-permute-start(f32[13,8,2048]{2,1,0:T(8,128)} %get-tuple-element.14), channel_id=1, source_target_pairs={{0,1},{1,2},{2,3},{3,0},{4,5},{5,6},{6,7},{7,4},{8,9},{9,10},{10,1... | collective-permute-start | bytes 2555912 | tf_op jit(solution)/shard_map/ppermute | solution.py:729
  3.0 21.2 %collective-permute-start.1 = (f32[13,8,2048]{2,1,0:T(8,128)S(1)}, f32[13,8,2048]{2,1,0:T(8,128)}, u32[]{:S(2)}, u32[]{:S(2)}) collective-permute-start(f32[13,8,2048]{2,1,0:T(8,128)S(1)} %get-tuple-element.15), channel_id=1, source_target_pairs={{1,0},{2,1},{3,2},{0,3},{5,4},{6,5},{7,6},{4,7},{9,8},{10,9},{11,1... | collective-permute-start | bytes 2555912 | tf_op jit(solution)/shard_map/ppermute | solution.py:729
  13.6 6.7 %copy-start.7 = (s32[4,256]{1,0:T(4,128)S(1)}, s32[4,256]{1,0:T(4,128)}, u32[]{:S(2)}) copy-start(s32[4,256]{1,0:T(4,128)} %param.11) | copy-start | bytes 12292
  13.6 45.1 %all-to-all-start.1 = ((f32[8,2,2,4,3,8,128]{6,5,4,3,2,1,0:T(8,128)}), f32[8,2,2,4,3,8,128]{6,5,4,3,2,1,0:T(8,128)S(1)}, u32[]{:S(2)}, u32[]{:S(2)}) async-start(f32[8,2,2,4,3,8,128]{6,5,4,3,2,1,0:T(8,128)} %inner.1.height_ref), calls=%async_computation.1 | async-start | bytes 3145728 | tf_op jit(solution)/shard_map/all_to_all | solution.py:757
  20.2 2.3 %copy-start.2 = (s32[32,256]{1,0:T(8,128)S(1)}, s32[32,256]{1,0:T(8,128)}, u32[]{:S(2)}) copy-start(s32[32,256]{1,0:T(8,128)} %cutoff_ref.5) | copy-start | bytes 98308
  37.1 1.5 %collective-permute-start.2 = (f32[4,16,128]{2,1,0:T(8,128)S(1)}, f32[4,16,128]{2,1,0:T(8,128)S(1)}, u32[]{:S(2)}, u32[]{:S(2)}) collective-permute-start(f32[4,16,128]{2,1,0:T(8,128)S(1)} %pick_outer.1), channel_id=1, source_target_pairs={{0,1},{1,0},{2,3},{3,2},{4,5},{5,4},{6,7},{7,6},{8,9},{9,8},{10,11... | collective-permute-start | bytes 98312 | tf_op jit(solution)/shard_map/ppermute | solution.py:254
  38.6 4.3 %collective-permute-start.3 = (f32[4,16,128]{2,1,0:T(8,128)S(1)}, f32[4,16,128]{2,1,0:T(8,128)S(1)}, u32[]{:S(2)}, u32[]{:S(2)}) collective-permute-start(f32[4,16,128]{2,1,0:T(8,128)S(1)} %add.36), channel_id=1, source_target_pairs={{0,2},{1,3},{2,0},{3,1},{4,6},{5,7},{6,4},{7,5},{8,10},{9,11},{10,... | collective-permute-start | bytes 98312 | tf_op jit(solution)/shard_map/ppermute | solution.py:254
  42.9 3.7 %collective-permute-start.4 = (f32[1,16,128]{2,1,0:T(8,128)S(1)}, f32[1,16,128]{2,1,0:T(8,128)S(1)}, u32[]{:S(2)}, u32[]{:S(2)}) collective-permute-start(f32[1,16,128]{2,1,0:T(8,128)S(1)} %get-tuple-element.24), channel_id=1, source_target_pairs={{0,4},{4,0},{8,12},{12,8},{16,20},{20,16},{24,28},{28,24},{1,5},{5... | collective-permute-start | bytes 24584 | tf_op jit(solution)/shard_map/ppermute | solution.py:254
  46.7 12.0 %collective-permute-start.7 = (f32[2,16,128]{2,1,0:T(8,128)S(1)}, f32[2,16,128]{2,1,0:T(8,128)S(1)}, u32[]{:S(2)}, u32[]{:S(2)}) collective-permute-start(f32[2,16,128]{2,1,0:T(8,128)S(1)} %pad_maximum_fusion.1), channel_id=1, source_target_pairs={{0,24},{4,28},{8,16},{12,20},{16,8},{20,12},{24,0},{28,4},{1,25},{... | collective-permute-start | bytes 49160 | tf_op jit(solution)/shard_map/ppermute | solution.py:254
  50.6 8.1 %collective-permute-start.6 = (f32[2,16,128]{2,1,0:T(8,128)S(1)}, f32[2,16,128]{2,1,0:T(8,128)S(1)}, u32[]{:S(2)}, u32[]{:S(2)}) collective-permute-start(f32[2,16,128]{2,1,0:T(8,128)S(1)} %pad_maximum_fusion.1), channel_id=1, source_target_pairs={{0,16},{4,20},{8,24},{12,28},{16,0},{20,4},{24,8},{28,12},{1,17},{... | collective-permute-start | bytes 49160 | tf_op jit(solution)/shard_map/ppermute | solution.py:254
  50.6 3.8 %collective-permute-start.5 = (f32[2,16,128]{2,1,0:T(8,128)S(1)}, f32[2,16,128]{2,1,0:T(8,128)S(1)}, u32[]{:S(2)}, u32[]{:S(2)}) collective-permute-start(f32[2,16,128]{2,1,0:T(8,128)S(1)} %pad_maximum_fusion.1), channel_id=1, source_target_pairs={{0,8},{4,12},{8,0},{12,4},{16,24},{20,28},{24,16},{28,20},{1,9},{5... | collective-permute-start | bytes 49160 | tf_op jit(solution)/shard_map/ppermute | solution.py:254
  58.7 40.9 %all-to-all-start = ((f32[8,2,2,4,3,8,128]{6,5,4,3,2,1,0:T(8,128)}), f32[8,2,2,4,3,8,128]{6,5,4,3,2,1,0:T(8,128)S(1)}, u32[]{:S(2)}, u32[]{:S(2)}) async-start(f32[8,2,2,4,3,8,128]{6,5,4,3,2,1,0:T(8,128)} %outer.1.height_ref), calls=%async_computation | async-start | bytes 3145728 | tf_op jit(solution)/shard_map/all_to_all | solution.py:772
  63.0 4.4 %collective-permute-start.10 = (f32[1,8,16,128]{3,2,1,0:T(8,128)S(1)}, f32[1,8,16,128]{3,2,1,0:T(8,128)S(1)}, u32[]{:S(2)}, u32[]{:S(2)}) collective-permute-start(f32[1,8,16,128]{3,2,1,0:T(8,128)S(1)} %bitcast.24), channel_id=1, source_target_pairs={{0,3},{1,2},{2,1},{3,0},{4,7},{5,6},{6,5},{7,4},{8,11},{9,10},{10,... | collective-permute-start | bytes 196616 | tf_op jit(solution)/shard_map/ppermute | solution.py:254
  63.0 5.4 %collective-permute-start.9 = (f32[1,8,16,128]{3,2,1,0:T(8,128)S(1)}, f32[1,8,16,128]{3,2,1,0:T(8,128)S(1)}, u32[]{:S(2)}, u32[]{:S(2)}) collective-permute-start(f32[1,8,16,128]{3,2,1,0:T(8,128)S(1)} %bitcast.25), channel_id=1, source_target_pairs={{0,2},{1,3},{2,0},{3,1},{4,6},{5,7},{6,4},{7,5},{8,10},{9,11},{10,... | collective-permute-start | bytes 196616 | tf_op jit(solution)/shard_map/ppermute | solution.py:254
  64.2 4.2 %collective-permute-start.8 = (f32[1,8,16,128]{3,2,1,0:T(8,128)S(1)}, f32[1,8,16,128]{3,2,1,0:T(8,128)S(1)}, u32[]{:S(2)}, u32[]{:S(2)}) collective-permute-start(f32[1,8,16,128]{3,2,1,0:T(8,128)S(1)} %bitcast.26), channel_id=1, source_target_pairs={{0,1},{1,0},{2,3},{3,2},{4,5},{5,4},{6,7},{7,6},{8,9},{9,8},{10,11... | collective-permute-start | bytes 196616 | tf_op jit(solution)/shard_map/ppermute | solution.py:254
  68.4 0.7 copy-start.5
  69.1 0.7 copy-start.6
  69.8 10.4 %copy-start.3 = (s32[2]{0:T(128)S(1)}, s32[2]{0:T(128)}, u32[]{:S(2)}) copy-start(s32[2]{0:T(128)} %constant.63.clone.tile_ref) | copy-start | bytes 28
  78.6 0.8 copy-start
  79.4 0.8 copy-start.1
  80.2 19.4 %copy-start.4 = (s32[2]{0:T(128)S(1)}, s32[2]{0:T(128)}, u32[]{:S(2)}) copy-start(s32[2]{0:T(128)} %iota_multiply_fusion.tile_ref) | copy-start | bytes 28

commit v7 on v6

--- a/solution.py
+++ b/solution.py
@@ -730,8 +730,6 @@
 
 
 def local(ensemble, sea_depth, cutoff, obs_index, obs_value, obs_var):
-    ensemble = pltpu.with_memory_space_constraint(ensemble, pltpu.HBM)
-    sea_depth = pltpu.with_memory_space_constraint(sea_depth, pltpu.HBM)
     blocks = lax.axis_size("mem")
     subs = lax.axis_size("sub")
     local_members, fields, rows, size_y = ensemble.shape
@@ -748,7 +746,12 @@
     flat_x = obs_x.reshape(1, -1)
     flat_y = obs_y.reshape(1, -1)
 
-    halos = row_halos(ensemble, sea_depth, "sub") * 2
+    halos = row_halos(
+        pltpu.with_memory_space_constraint(ensemble, pltpu.HBM),
+        pltpu.with_memory_space_constraint(sea_depth, pltpu.HBM),
+        "sub",
+    )
+    halos *= 2
     radius_part = pick_radius(cutoff, flat_x[0], flat_y[0], x_start, y_start)[None]
 
     inner_rows = rows - 2 * HALO

time: 109 us -> 108 us (level)
  waiting for transfers between devices: 26.9 us -> 29.5 us
  Pallas kernels: 52.6 us -> 50.2 us
    pallas_call x2, Pallas kernels: 19.3 us -> 17.2 us  [forecast(): pl.pallas_call(functools.partial(forecast_kernel, bool(halos), kept), gri...]
    ppermute x1, waiting for transfers between devices: 0.88 us -> 2.46 us  [row_halos(): lax.ppermute(first, axis, backward)]
    all_to_all x1, waiting for transfers between devices: 10.5 us -> 11.9 us  [local(): lax.all_to_all(sent_outer, 'mem', split_axis=0, concat_axis=0, tiled=True)]
    unnamed x23 -> x27, local copies, waits for them, and re-layouts: 3.03 us -> 2.83 us
  transfers between devices with their start and end apart: 13 -> 13, of which waited for: 9 -> 9; matrix products, arithmetic and copies ran while one was open for 1% -> 1% of each run, Pallas kernels for 38% -> 36%
where the time goes in v7:
time: 108 us
  Pallas kernels  50.2 us (46%)
  waiting for transfers between devices  29.5 us (27%)
  starting transfers between devices  23.9 us (22%)
  local copies, waits for them, and re-layouts  2.95 us (3%)
    pallas_call x2, Pallas kernels, update(): pl.pallas_call(functools.partial(update_kernel, sizes, begun is not None)...  18.1 us
    pallas_call x2, Pallas kernels, forecast(): pl.pallas_call(functools.partial(forecast_kernel, bool(halos), kept), gri...  17.2 us
    ppermute x9, waiting for transfers between devices, exchange(): return lax.ppermute(value, axis, [(i, i ^ distance) for i in range(size)])  15.1 us
    all_to_all x1, waiting for transfers between devices, local(): lax.all_to_all(sent_outer, 'mem', split_axis=0, concat_axis=0, tiled=True)  11.9 us
    ppermute x9, starting transfers between devices, exchange(): return lax.ppermute(value, axis, [(i, i ^ distance) for i in range(size)])  10.9 us
    pallas_call x1, Pallas kernels, chain(): pl.pallas_call(functools.partial(chain_kernel, members, sizes), in_specs=...  8.73 us
    all_to_all x1, starting transfers between devices, local(): lax.all_to_all(sent_inner, 'mem', split_axis=0, concat_axis=0, tiled=True)  6.66 us
    all_to_all x1, starting transfers between devices, local(): lax.all_to_all(sent_outer, 'mem', split_axis=0, concat_axis=0, tiled=True)  3.77 us
  transfers between devices with their start and end apart: 13, of which 9 were waited for; matrix products, arithmetic and copies ran while one was open for 1% of the time, Pallas kernels for 36%

profile of v7, /device:TPU:0, one launch (start us, length us, event | category | flops | bytes accessed | tf_op | source)
XLA Modules:
  0.0 107.9 jit_solution(2091051949569073475)
XLA Ops:
  0.0 0.0 copy-start.4
  0.0 0.0 copy-start
  0.0 2.9 %edges.1 = (f32[13,8,2048]{2,1,0:T(8,128)}, f32[13,8,2048]{2,1,0:T(8,128)}) custom-call(f32[4,3,32,2048]{3,2,1,0:T(8,128)} %refs_0_.3, f32[32,2048]{1,0:T(8,128)} %refs_1_.3), custom_call_target="tpu_custom_call" | custom-call | tf_op jit(solution)/shard_map/edges/pallas_call | solution.py:720
  2.9 0.5 collective-permute-start
  3.4 2.0 %collective-permute-start.1 = (f32[13,8,2048]{2,1,0:T(8,128)}, f32[13,8,2048]{2,1,0:T(8,128)}, u32[]{:S(2)}, u32[]{:S(2)}) collective-permute-start(f32[13,8,2048]{2,1,0:T(8,128)} %get-tuple-element.15), channel_id=1, source_target_pairs={{1,0},{2,1},{3,2},{0,3},{5,4},{6,5},{7,6},{4,7},{9,8},{10,9},{11,1... | collective-permute-start | bytes 2555912 | tf_op jit(solution)/shard_map/ppermute | solution.py:729
  5.4 0.0 copy-done.4
  5.4 0.0 copy-done
  5.4 7.3 %inner.1.height_ref = f32[8,2,2,4,3,8,128]{6,5,4,3,2,1,0:T(8,128)} custom-call(f32[4,3,32,2048]{3,2,1,0:T(8,128)S(1)} %copy-done, f32[32,2048]{1,0:T(8,128)S(1)} %copy-done.4), custom_call_target="tpu_custom_call" | custom-call | tf_op jit(solution)/shard_map/inner/pallas_call | solution.py:132
  12.8 0.0 copy-start.9
  12.8 6.7 %all-to-all-start.1 = ((f32[8,2,2,4,3,8,128]{6,5,4,3,2,1,0:T(8,128)}), f32[8,2,2,4,3,8,128]{6,5,4,3,2,1,0:T(8,128)}, u32[]{:S(2)}, u32[]{:S(2)}) async-start(f32[8,2,2,4,3,8,128]{6,5,4,3,2,1,0:T(8,128)} %inner.1.height_ref), calls=%async_computation.1 | async-start | bytes 3145728 | tf_op jit(solution)/shard_map/all_to_all | solution.py:760
  19.4 0.0 copy-start.5
  19.4 0.0 copy-done.9
  19.5 2.2 %pick_inner.1.inner_ref = f32[4,1024]{1,0:T(4,128)S(1)} custom-call(s32[1,1024]{1,0:T(1,128)S(1)} %get-tuple-element.29.row_ref, s32[1,1024]{1,0:T(1,128)S(1)} %bitcast.20, f32[8,2,2,4,3,8,128]{6,5,4,3,2,1,0:T(8,128)} %inner.1.height_ref), custom_call_target="tpu_custom_call" | custom-call | tf_op jit(solution)/shard_map/pick_inner/pallas_call | solution.py:211
  21.7 0.0 copy-done.5
  21.7 0.8 fusion
  22.5 0.0 collective-permute-done.refs_2_.refs_4_
  22.5 2.5 %collective-permute-done.1.refs_3_.refs_5_ = f32[13,8,2048]{2,1,0:T(8,128)} collective-permute-done((f32[13,8,2048]{2,1,0:T(8,128)}, f32[13,8,2048]{2,1,0:T(8,128)}, u32[]{:S(2)}, u32[]{:S(2)}) %collective-permute-start.1) | collective-permute-done | bytes 852000 | tf_op jit(solution)/shard_map/ppermute | solution.py:729
  25.0 9.9 %outer.1.height_ref = f32[8,2,2,4,3,8,128]{6,5,4,3,2,1,0:T(8,128)S(1)} custom-call(f32[4,3,32,2048]{3,2,1,0:T(8,128)S(1)} %copy-done, f32[32,2048]{1,0:T(8,128)S(1)} %copy-done.4, f32[13,8,2048]{2,1,0:T(8,128)} %collective-permute-done.refs_2_.refs_4_, f32[13,8,2048]{2,1,0:T(8,128)} %collective-permute-done.1.refs_3_.refs_5_, ...), custom_call_target="tpu_custom_call" | custom-call | flops 23000000512 | bytes 74000000 | tf_op jit(solution)/shard_map/outer/pallas_call | solution.py:132
  34.9 1.1 %pick_outer.1 = f32[4,16,128]{2,1,0:T(8,128)S(1)} custom-call(s32[1,1024]{1,0:T(1,128)S(1)} %get-tuple-element.30.row_ref, s32[1,1024]{1,0:T(1,128)S(1)} %bitcast.21, f32[8,2,2,4,3,8,128]{6,5,4,3,2,1,0:T(8,128)S(1)} %outer.1.height_ref, f32[4,1024]{1,0:T(4,128)S(1)} %pick_inner.1.inner_ref, f32[1,1024]{1,0:T(1,128)S(1)} %bitcast.23), custom_call_target="tpu_custom_call" | custom-call | tf_op jit(solution)/shard_map/pick_outer/pallas_call | solution.py:226
  36.0 0.0 copy-start.1
  36.0 1.1 %copy-done.1 = f32[8,2,2,4,3,8,128]{6,5,4,3,2,1,0:T(8,128)} copy-done((f32[8,2,2,4,3,8,128]{6,5,4,3,2,1,0:T(8,128)}, f32[8,2,2,4,3,8,128]{6,5,4,3,2,1,0:T(8,128)S(1)}, u32[]{:S(2)}) %copy-start.1) | copy-done | bytes 1572888
  37.1 0.3 collective-permute-start.2
  37.4 0.9 collective-permute-done.2
  38.4 2.4 %collective-permute-start.3 = (f32[4,16,128]{2,1,0:T(8,128)S(1)}, f32[4,16,128]{2,1,0:T(8,128)S(1)}, u32[]{:S(2)}, u32[]{:S(2)}) collective-permute-start(f32[4,16,128]{2,1,0:T(8,128)S(1)} %add.36), channel_id=1, source_target_pairs={{0,2},{1,3},{2,0},{3,1},{4,6},{5,7},{6,4},{7,5},{8,10},{9,11},{10,... | collective-permute-start | bytes 98312 | tf_op jit(solution)/shard_map/ppermute | solution.py:254
  40.8 1.9 %collective-permute-done.3 = f32[4,16,128]{2,1,0:T(8,128)S(1)} collective-permute-done((f32[4,16,128]{2,1,0:T(8,128)S(1)}, f32[4,16,128]{2,1,0:T(8,128)S(1)}, u32[]{:S(2)}, u32[]{:S(2)}) %collective-permute-start.3) | collective-permute-done | bytes 32800 | tf_op jit(solution)/shard_map/ppermute | solution.py:254
  42.7 1.8 %collective-permute-start.4 = (f32[1,16,128]{2,1,0:T(8,128)S(1)}, f32[1,16,128]{2,1,0:T(8,128)S(1)}, u32[]{:S(2)}, u32[]{:S(2)}) collective-permute-start(f32[1,16,128]{2,1,0:T(8,128)S(1)} %get-tuple-element.24), channel_id=1, source_target_pairs={{0,4},{4,0},{8,12},{12,8},{16,20},{20,16},{24,28},{28,24},{1,5},{5... | collective-permute-start | bytes 24584 | tf_op jit(solution)/shard_map/ppermute | solution.py:254
  44.5 0.1 copy.28
  44.6 1.7 %collective-permute-done.4 = f32[1,16,128]{2,1,0:T(8,128)S(1)} collective-permute-done((f32[1,16,128]{2,1,0:T(8,128)S(1)}, f32[1,16,128]{2,1,0:T(8,128)S(1)}, u32[]{:S(2)}, u32[]{:S(2)}) %collective-permute-start.4) | collective-permute-done | bytes 8224 | tf_op jit(solution)/shard_map/ppermute | solution.py:254
  46.4 3.9 %collective-permute-start.7 = (f32[2,16,128]{2,1,0:T(8,128)S(1)}, f32[2,16,128]{2,1,0:T(8,128)S(1)}, u32[]{:S(2)}, u32[]{:S(2)}) collective-permute-start(f32[2,16,128]{2,1,0:T(8,128)S(1)} %pad_maximum_fusion.1), channel_id=1, source_target_pairs={{0,24},{4,28},{8,16},{12,20},{16,8},{20,12},{24,0},{28,4},{1,25},{... | collective-permute-start | bytes 49160 | tf_op jit(solution)/shard_map/ppermute | solution.py:254
  50.3 0.0 collective-permute-start.6
  50.3 0.6 collective-permute-start.5
  50.8 3.3 %collective-permute-done.5 = f32[2,16,128]{2,1,0:T(8,128)S(1)} collective-permute-done((f32[2,16,128]{2,1,0:T(8,128)S(1)}, f32[2,16,128]{2,1,0:T(8,128)S(1)}, u32[]{:S(2)}, u32[]{:S(2)}) %collective-permute-start.5) | collective-permute-done | bytes 16416 | tf_op jit(solution)/shard_map/ppermute | solution.py:254
  54.1 3.8 %collective-permute-done.6 = f32[2,16,128]{2,1,0:T(8,128)S(1)} collective-permute-done((f32[2,16,128]{2,1,0:T(8,128)S(1)}, f32[2,16,128]{2,1,0:T(8,128)S(1)}, u32[]{:S(2)}, u32[]{:S(2)}) %collective-permute-start.6) | collective-permute-done | bytes 16416 | tf_op jit(solution)/shard_map/ppermute | solution.py:254
  57.9 0.0 collective-permute-done.7
  57.9 0.0 copy-start.7
  57.9 0.0 copy-start.8
  58.0 0.0 all-to-all-done.1.state_ref
  58.0 3.8 %all-to-all-start = ((f32[8,2,2,4,3,8,128]{6,5,4,3,2,1,0:T(8,128)}), f32[8,2,2,4,3,8,128]{6,5,4,3,2,1,0:T(8,128)S(1)}, u32[]{:S(2)}, u32[]{:S(2)}) async-start(f32[8,2,2,4,3,8,128]{6,5,4,3,2,1,0:T(8,128)} %copy-done.1), calls=%async_computation | async-start | bytes 3145728 | tf_op jit(solution)/shard_map/all_to_all | solution.py:775
  61.8 0.1 collective-permute-start.10
  61.8 1.3 %collective-permute-start.9 = (f32[1,8,16,128]{3,2,1,0:T(8,128)S(1)}, f32[1,8,16,128]{3,2,1,0:T(8,128)S(1)}, u32[]{:S(2)}, u32[]{:S(2)}) collective-permute-start(f32[1,8,16,128]{3,2,1,0:T(8,128)S(1)} %bitcast.25), channel_id=1, source_target_pairs={{0,2},{1,3},{2,0},{3,1},{4,6},{5,7},{6,4},{7,5},{8,10},{9,11},{10,... | collective-permute-start | bytes 196616 | tf_op jit(solution)/shard_map/ppermute | solution.py:254
  63.1 0.6 collective-permute-start.8
  63.7 0.1 pad_add_fusion.2.start_ref
  63.8 2.5 %collective-permute-done.10 = f32[1,8,16,128]{3,2,1,0:T(8,128)S(1)} collective-permute-done((f32[1,8,16,128]{3,2,1,0:T(8,128)S(1)}, f32[1,8,16,128]{3,2,1,0:T(8,128)S(1)}, u32[]{:S(2)}, u32[]{:S(2)}) %collective-permute-start.10) | collective-permute-done | bytes 65568 | tf_op jit(solution)/shard_map/ppermute | solution.py:254
  66.2 1.0 collective-permute-done.9
  67.3 0.0 collective-permute-done.8
  67.3 0.0 copy-done.7
  67.3 0.0 copy-done.8
  67.3 0.0 copy-start.6
  67.3 8.7 %chain.1 = (bf16[4,2,48,112]{3,2,1,0:T(8,128)(2,1)S(1)}, bf16[4,2,32,144]{3,2,1,0:T(8,128)(2,1)S(1)}, bf16[4,2,5,48,112]{4,3,2,1,0:T(8,128)(2,1)S(1)}, bf16[4,2,5,32,144]{4,3,2,1,0:T(8,128)(2,1)S(1)}, s32[4,2]{1,0:T(4,128)S(1)}) custom-call(s32[4]{0:T(128)S(1)} %pad_add_fusion.2.start_ref, f32[4,8,16,128]{3,2,1,0:T(8,128)S(1)} %pad_maximum_fusion.every_ref, ...), custom_call_target="tpu_custom_call" | custom-call | flops 25999998976 | bytes 85000000 | tf_op jit(solution)/shard_map/chain/pallas_call | solution.py:509
  76.1 0.0 copy-start.2
  76.1 0.8 copy-done.2
  76.9 0.0 copy-start.3
  76.9 0.8 copy-done.3
  77.7 0.0 copy-done.6
  77.7 9.2 %update.2.rest_0_ = f32[32,3,32,256]{3,2,1,0:T(8,128)} custom-call(s32[2]{0:T(128)S(1)} %copy-done.6, s32[4]{0:T(128)S(1)} %pad_add_fusion.2.start_ref, s32[4,2]{1,0:T(4,128)S(1)} %get-tuple-element.17.count_ref, f32[8,2,2,4,3,8,128]{6,5,4,3,2,1,0:T(8,128)} %all-to-all-done.1.state_ref, s32[32,256]{1,0:T(8,128)S(1)} %copy-done.5, ...), custom_call_target="tpu_custom_call" | custom-call | tf_op jit(solution)/shard_map/update/pallas_call | solution.py:674
  86.9 11.9 %all-to-all-done.state_ref = f32[8,2,2,4,3,8,128]{6,5,4,3,2,1,0:T(8,128)S(1)} async-done(((f32[8,2,2,4,3,8,128]{6,5,4,3,2,1,0:T(8,128)}), f32[8,2,2,4,3,8,128]{6,5,4,3,2,1,0:T(8,128)S(1)}, u32[]{:S(2)}, u32[]{:S(2)}) %all-to-all-start) | async-done | bytes 1572896 | tf_op jit(solution)/shard_map/all_to_all | solution.py:775
  98.8 8.9 %update.3 = f32[32,3,32,256]{3,2,1,0:T(8,128)} custom-call(s32[2]{0:T(128)S(1)} %iota_multiply_fusion.tile_ref, s32[4]{0:T(128)S(1)} %pad_add_fusion.2.start_ref, s32[4,2]{1,0:T(4,128)S(1)} %get-tuple-element.17.count_ref, f32[8,2,2,4,3,8,128]{6,5,4,3,2,1,0:T(8,128)S(1)} %all-to-all-done.state_ref, ...), custom_call_target="tpu_custom_call", output_to_operand_aliasing={{}: (9, {})} | custom-call | tf_op jit(solution)/shard_map/update/pallas_call | solution.py:674
  (17 shorter events, 0.1 us)
Async XLA Ops:
  0.0 5.4 %copy-start.4 = (f32[32,2048]{1,0:T(8,128)S(1)}, f32[32,2048]{1,0:T(8,128)}, u32[]{:S(2)}) copy-start(f32[32,2048]{1,0:T(8,128)} %refs_1_.3) | copy-start | bytes 786436
  0.0 5.4 %copy-start = (f32[4,3,32,2048]{3,2,1,0:T(8,128)S(1)}, f32[4,3,32,2048]{3,2,1,0:T(8,128)}, u32[]{:S(2)}) copy-start(f32[4,3,32,2048]{3,2,1,0:T(8,128)} %refs_0_.3) | copy-start | bytes 9437188
  2.9 19.6 %collective-permute-start = (f32[13,8,2048]{2,1,0:T(8,128)}, f32[13,8,2048]{2,1,0:T(8,128)}, u32[]{:S(2)}, u32[]{:S(2)}) collective-permute-start(f32[13,8,2048]{2,1,0:T(8,128)} %get-tuple-element.14), channel_id=1, source_target_pairs={{0,1},{1,2},{2,3},{3,0},{4,5},{5,6},{6,7},{7,4},{8,9},{9,10},{10,1... | collective-permute-start | bytes 2555912 | tf_op jit(solution)/shard_map/ppermute | solution.py:729
  3.4 21.6 %collective-permute-start.1 = (f32[13,8,2048]{2,1,0:T(8,128)}, f32[13,8,2048]{2,1,0:T(8,128)}, u32[]{:S(2)}, u32[]{:S(2)}) collective-permute-start(f32[13,8,2048]{2,1,0:T(8,128)} %get-tuple-element.15), channel_id=1, source_target_pairs={{1,0},{2,1},{3,2},{0,3},{5,4},{6,5},{7,6},{4,7},{9,8},{10,9},{11,1... | collective-permute-start | bytes 2555912 | tf_op jit(solution)/shard_map/ppermute | solution.py:729
  12.8 6.7 %copy-start.9 = (s32[4,256]{1,0:T(4,128)S(1)}, s32[4,256]{1,0:T(4,128)}, u32[]{:S(2)}) copy-start(s32[4,256]{1,0:T(4,128)} %param.11) | copy-start | bytes 12292
  12.8 45.2 %all-to-all-start.1 = ((f32[8,2,2,4,3,8,128]{6,5,4,3,2,1,0:T(8,128)}), f32[8,2,2,4,3,8,128]{6,5,4,3,2,1,0:T(8,128)}, u32[]{:S(2)}, u32[]{:S(2)}) async-start(f32[8,2,2,4,3,8,128]{6,5,4,3,2,1,0:T(8,128)} %inner.1.height_ref), calls=%async_computation.1 | async-start | bytes 3145728 | tf_op jit(solution)/shard_map/all_to_all | solution.py:760
  19.4 2.3 %copy-start.5 = (s32[32,256]{1,0:T(8,128)S(1)}, s32[32,256]{1,0:T(8,128)}, u32[]{:S(2)}) copy-start(s32[32,256]{1,0:T(8,128)} %cutoff_ref.5) | copy-start | bytes 98308
  36.0 1.2 %copy-start.1 = (f32[8,2,2,4,3,8,128]{6,5,4,3,2,1,0:T(8,128)}, f32[8,2,2,4,3,8,128]{6,5,4,3,2,1,0:T(8,128)S(1)}, u32[]{:S(2)}) copy-start(f32[8,2,2,4,3,8,128]{6,5,4,3,2,1,0:T(8,128)S(1)} %outer.1.height_ref) | copy-start | bytes 4718596
  37.1 1.2 %collective-permute-start.2 = (f32[4,16,128]{2,1,0:T(8,128)S(1)}, f32[4,16,128]{2,1,0:T(8,128)S(1)}, u32[]{:S(2)}, u32[]{:S(2)}) collective-permute-start(f32[4,16,128]{2,1,0:T(8,128)S(1)} %pick_outer.1), channel_id=1, source_target_pairs={{0,1},{1,0},{2,3},{3,2},{4,5},{5,4},{6,7},{7,6},{8,9},{9,8},{10,11... | collective-permute-start | bytes 98312 | tf_op jit(solution)/shard_map/ppermute | solution.py:254
  38.4 4.3 %collective-permute-start.3 = (f32[4,16,128]{2,1,0:T(8,128)S(1)}, f32[4,16,128]{2,1,0:T(8,128)S(1)}, u32[]{:S(2)}, u32[]{:S(2)}) collective-permute-start(f32[4,16,128]{2,1,0:T(8,128)S(1)} %add.36), channel_id=1, source_target_pairs={{0,2},{1,3},{2,0},{3,1},{4,6},{5,7},{6,4},{7,5},{8,10},{9,11},{10,... | collective-permute-start | bytes 98312 | tf_op jit(solution)/shard_map/ppermute | solution.py:254
  42.7 3.7 %collective-permute-start.4 = (f32[1,16,128]{2,1,0:T(8,128)S(1)}, f32[1,16,128]{2,1,0:T(8,128)S(1)}, u32[]{:S(2)}, u32[]{:S(2)}) collective-permute-start(f32[1,16,128]{2,1,0:T(8,128)S(1)} %get-tuple-element.24), channel_id=1, source_target_pairs={{0,4},{4,0},{8,12},{12,8},{16,20},{20,16},{24,28},{28,24},{1,5},{5... | collective-permute-start | bytes 24584 | tf_op jit(solution)/shard_map/ppermute | solution.py:254
  46.4 11.5 %collective-permute-start.7 = (f32[2,16,128]{2,1,0:T(8,128)S(1)}, f32[2,16,128]{2,1,0:T(8,128)S(1)}, u32[]{:S(2)}, u32[]{:S(2)}) collective-permute-start(f32[2,16,128]{2,1,0:T(8,128)S(1)} %pad_maximum_fusion.1), channel_id=1, source_target_pairs={{0,24},{4,28},{8,16},{12,20},{16,8},{20,12},{24,0},{28,4},{1,25},{... | collective-permute-start | bytes 49160 | tf_op jit(solution)/shard_map/ppermute | solution.py:254
  50.3 7.7 %collective-permute-start.6 = (f32[2,16,128]{2,1,0:T(8,128)S(1)}, f32[2,16,128]{2,1,0:T(8,128)S(1)}, u32[]{:S(2)}, u32[]{:S(2)}) collective-permute-start(f32[2,16,128]{2,1,0:T(8,128)S(1)} %pad_maximum_fusion.1), channel_id=1, source_target_pairs={{0,16},{4,20},{8,24},{12,28},{16,0},{20,4},{24,8},{28,12},{1,17},{... | collective-permute-start | bytes 49160 | tf_op jit(solution)/shard_map/ppermute | solution.py:254
  50.3 3.8 %collective-permute-start.5 = (f32[2,16,128]{2,1,0:T(8,128)S(1)}, f32[2,16,128]{2,1,0:T(8,128)S(1)}, u32[]{:S(2)}, u32[]{:S(2)}) collective-permute-start(f32[2,16,128]{2,1,0:T(8,128)S(1)} %pad_maximum_fusion.1), channel_id=1, source_target_pairs={{0,8},{4,12},{8,0},{12,4},{16,24},{20,28},{24,16},{28,20},{1,9},{5... | collective-permute-start | bytes 49160 | tf_op jit(solution)/shard_map/ppermute | solution.py:254
  57.9 9.4 %copy-start.7 = (f32[4,256]{1,0:T(4,128)S(1)}, f32[4,256]{1,0:T(4,128)}, u32[]{:S(2)}) copy-start(f32[4,256]{1,0:T(4,128)} %value_ref.1) | copy-start | bytes 12292
  57.9 9.4 %copy-start.8 = (f32[4,256]{1,0:T(4,128)S(1)}, f32[4,256]{1,0:T(4,128)}, u32[]{:S(2)}) copy-start(f32[4,256]{1,0:T(4,128)} %variance_ref.1) | copy-start | bytes 12292
  58.0 40.9 %all-to-all-start = ((f32[8,2,2,4,3,8,128]{6,5,4,3,2,1,0:T(8,128)}), f32[8,2,2,4,3,8,128]{6,5,4,3,2,1,0:T(8,128)S(1)}, u32[]{:S(2)}, u32[]{:S(2)}) async-start(f32[8,2,2,4,3,8,128]{6,5,4,3,2,1,0:T(8,128)} %copy-done.1), calls=%async_computation | async-start | bytes 3145728 | tf_op jit(solution)/shard_map/all_to_all | solution.py:775
  61.8 4.5 %collective-permute-start.10 = (f32[1,8,16,128]{3,2,1,0:T(8,128)S(1)}, f32[1,8,16,128]{3,2,1,0:T(8,128)S(1)}, u32[]{:S(2)}, u32[]{:S(2)}) collective-permute-start(f32[1,8,16,128]{3,2,1,0:T(8,128)S(1)} %bitcast.24), channel_id=1, source_target_pairs={{0,3},{1,2},{2,1},{3,0},{4,7},{5,6},{6,5},{7,4},{8,11},{9,10},{10,... | collective-permute-start | bytes 196616 | tf_op jit(solution)/shard_map/ppermute | solution.py:254
  61.8 5.4 %collective-permute-start.9 = (f32[1,8,16,128]{3,2,1,0:T(8,128)S(1)}, f32[1,8,16,128]{3,2,1,0:T(8,128)S(1)}, u32[]{:S(2)}, u32[]{:S(2)}) collective-permute-start(f32[1,8,16,128]{3,2,1,0:T(8,128)S(1)} %bitcast.25), channel_id=1, source_target_pairs={{0,2},{1,3},{2,0},{3,1},{4,6},{5,7},{6,4},{7,5},{8,10},{9,11},{10,... | collective-permute-start | bytes 196616 | tf_op jit(solution)/shard_map/ppermute | solution.py:254
  63.1 4.2 %collective-permute-start.8 = (f32[1,8,16,128]{3,2,1,0:T(8,128)S(1)}, f32[1,8,16,128]{3,2,1,0:T(8,128)S(1)}, u32[]{:S(2)}, u32[]{:S(2)}) collective-permute-start(f32[1,8,16,128]{3,2,1,0:T(8,128)S(1)} %bitcast.26), channel_id=1, source_target_pairs={{0,1},{1,0},{2,3},{3,2},{4,5},{5,4},{6,7},{7,6},{8,9},{9,8},{10,11... | collective-permute-start | bytes 196616 | tf_op jit(solution)/shard_map/ppermute | solution.py:254
  67.3 10.4 %copy-start.6 = (s32[2]{0:T(128)S(1)}, s32[2]{0:T(128)}, u32[]{:S(2)}) copy-start(s32[2]{0:T(128)} %constant.63.clone.tile_ref) | copy-start | bytes 28
  76.1 0.8 copy-start.2
  76.9 0.8 copy-start.3

commit v8 on v7

--- a/solution.py
+++ b/solution.py
@@ -10,7 +10,7 @@
 STEPS = 4
 HALO = 2 * STEPS
 LANES = 128
-OBS_BLOCK = 48
+OBS_BLOCK = 64
 ROW_TILE = 8
 OUTER_COST = pl.CostEstimate(flops=23 * 10**9, bytes_accessed=74 * 10**6, transcendentals=0)
 CHAIN_COST = pl.CostEstimate(flops=26 * 10**9, bytes_accessed=85 * 10**6, transcendentals=0)

time: 108 us -> 109 us (level)
  no operation moved by 1% of the time
where the time goes in v8:
time: 109 us; the launch traced here: 108 us
  Pallas kernels  50.4 us (46%)
  waiting for transfers between devices  29.6 us (27%)
  starting transfers between devices  23.9 us (22%)
  local copies, waits for them, and re-layouts  2.82 us (3%)
    pallas_call x2, Pallas kernels, update(): pl.pallas_call(functools.partial(update_kernel, sizes, begun is not None)...  18.3 us
    pallas_call x2, Pallas kernels, forecast(): pl.pallas_call(functools.partial(forecast_kernel, bool(halos), kept), gri...  17.2 us
    ppermute x9, waiting for transfers between devices, exchange(): return lax.ppermute(value, axis, [(i, i ^ distance) for i in range(size)])  15.1 us
    all_to_all x1, waiting for transfers between devices, local(): lax.all_to_all(sent_outer, 'mem', split_axis=0, concat_axis=0, tiled=True)  12 us
    ppermute x9, starting transfers between devices, exchange(): return lax.ppermute(value, axis, [(i, i ^ distance) for i in range(size)])  10.9 us
    pallas_call x1, Pallas kernels, chain(): pl.pallas_call(functools.partial(chain_kernel, members, sizes), in_specs=...  8.76 us
    all_to_all x1, starting transfers between devices, local(): lax.all_to_all(sent_inner, 'mem', split_axis=0, concat_axis=0, tiled=True)  6.66 us
    all_to_all x1, starting transfers between devices, local(): lax.all_to_all(sent_outer, 'mem', split_axis=0, concat_axis=0, tiled=True)  3.77 us
  transfers between devices with their start and end apart: 13, of which 9 were waited for; matrix products, arithmetic and copies ran while one was open for 1% of the time, Pallas kernels for 36%

profile of v8, /device:TPU:0, one launch (start us, length us, event | category | flops | bytes accessed | tf_op | source)
XLA Modules:
  0.0 108.2 jit_solution(5271728175983045673)
XLA Ops:
  0.0 0.0 copy-start.4
  0.0 0.0 copy-start
  0.0 2.9 %edges.1 = (f32[13,8,2048]{2,1,0:T(8,128)}, f32[13,8,2048]{2,1,0:T(8,128)}) custom-call(f32[4,3,32,2048]{3,2,1,0:T(8,128)} %refs_0_.3, f32[32,2048]{1,0:T(8,128)} %refs_1_.3), custom_call_target="tpu_custom_call" | custom-call | tf_op jit(solution)/shard_map/edges/pallas_call | solution.py:720
  2.9 0.5 collective-permute-start
  3.4 2.0 %collective-permute-start.1 = (f32[13,8,2048]{2,1,0:T(8,128)}, f32[13,8,2048]{2,1,0:T(8,128)}, u32[]{:S(2)}, u32[]{:S(2)}) collective-permute-start(f32[13,8,2048]{2,1,0:T(8,128)} %get-tuple-element.15), channel_id=1, source_target_pairs={{1,0},{2,1},{3,2},{0,3},{5,4},{6,5},{7,6},{4,7},{9,8},{10,9},{11,1... | collective-permute-start | bytes 2555912 | tf_op jit(solution)/shard_map/ppermute | solution.py:729
  5.4 0.0 copy-done.4
  5.4 0.0 copy-done
  5.4 7.3 %inner.1.height_ref = f32[8,2,2,4,3,8,128]{6,5,4,3,2,1,0:T(8,128)} custom-call(f32[4,3,32,2048]{3,2,1,0:T(8,128)S(1)} %copy-done, f32[32,2048]{1,0:T(8,128)S(1)} %copy-done.4), custom_call_target="tpu_custom_call" | custom-call | tf_op jit(solution)/shard_map/inner/pallas_call | solution.py:132
  12.8 0.0 copy-start.9
  12.8 6.7 %all-to-all-start.1 = ((f32[8,2,2,4,3,8,128]{6,5,4,3,2,1,0:T(8,128)}), f32[8,2,2,4,3,8,128]{6,5,4,3,2,1,0:T(8,128)}, u32[]{:S(2)}, u32[]{:S(2)}) async-start(f32[8,2,2,4,3,8,128]{6,5,4,3,2,1,0:T(8,128)} %inner.1.height_ref), calls=%async_computation.1 | async-start | bytes 3145728 | tf_op jit(solution)/shard_map/all_to_all | solution.py:760
  19.4 0.0 copy-start.5
  19.4 0.0 copy-done.9
  19.5 2.2 %pick_inner.1.inner_ref = f32[4,1024]{1,0:T(4,128)S(1)} custom-call(s32[1,1024]{1,0:T(1,128)S(1)} %get-tuple-element.29.row_ref, s32[1,1024]{1,0:T(1,128)S(1)} %bitcast.20, f32[8,2,2,4,3,8,128]{6,5,4,3,2,1,0:T(8,128)} %inner.1.height_ref), custom_call_target="tpu_custom_call" | custom-call | tf_op jit(solution)/shard_map/pick_inner/pallas_call | solution.py:211
  21.7 0.0 copy-done.5
  21.7 0.8 fusion
  22.5 0.0 collective-permute-done.refs_2_.refs_4_
  22.5 2.5 %collective-permute-done.1.refs_3_.refs_5_ = f32[13,8,2048]{2,1,0:T(8,128)} collective-permute-done((f32[13,8,2048]{2,1,0:T(8,128)}, f32[13,8,2048]{2,1,0:T(8,128)}, u32[]{:S(2)}, u32[]{:S(2)}) %collective-permute-start.1) | collective-permute-done | bytes 852000 | tf_op jit(solution)/shard_map/ppermute | solution.py:729
  25.0 9.9 %outer.1.height_ref = f32[8,2,2,4,3,8,128]{6,5,4,3,2,1,0:T(8,128)S(1)} custom-call(f32[4,3,32,2048]{3,2,1,0:T(8,128)S(1)} %copy-done, f32[32,2048]{1,0:T(8,128)S(1)} %copy-done.4, f32[13,8,2048]{2,1,0:T(8,128)} %collective-permute-done.refs_2_.refs_4_, f32[13,8,2048]{2,1,0:T(8,128)} %collective-permute-done.1.refs_3_.refs_5_, ...), custom_call_target="tpu_custom_call" | custom-call | flops 23000000512 | bytes 74000000 | tf_op jit(solution)/shard_map/outer/pallas_call | solution.py:132
  34.9 1.1 %pick_outer.1 = f32[4,16,128]{2,1,0:T(8,128)S(1)} custom-call(s32[1,1024]{1,0:T(1,128)S(1)} %get-tuple-element.30.row_ref, s32[1,1024]{1,0:T(1,128)S(1)} %bitcast.21, f32[8,2,2,4,3,8,128]{6,5,4,3,2,1,0:T(8,128)S(1)} %outer.1.height_ref, f32[4,1024]{1,0:T(4,128)S(1)} %pick_inner.1.inner_ref, f32[1,1024]{1,0:T(1,128)S(1)} %bitcast.23), custom_call_target="tpu_custom_call" | custom-call | tf_op jit(solution)/shard_map/pick_outer/pallas_call | solution.py:226
  36.0 0.0 copy-start.1
  36.0 1.1 %copy-done.1 = f32[8,2,2,4,3,8,128]{6,5,4,3,2,1,0:T(8,128)} copy-done((f32[8,2,2,4,3,8,128]{6,5,4,3,2,1,0:T(8,128)}, f32[8,2,2,4,3,8,128]{6,5,4,3,2,1,0:T(8,128)S(1)}, u32[]{:S(2)}) %copy-start.1) | copy-done | bytes 1572888
  37.1 0.3 collective-permute-start.2
  37.4 0.9 collective-permute-done.2
  38.4 2.4 %collective-permute-start.3 = (f32[4,16,128]{2,1,0:T(8,128)S(1)}, f32[4,16,128]{2,1,0:T(8,128)S(1)}, u32[]{:S(2)}, u32[]{:S(2)}) collective-permute-start(f32[4,16,128]{2,1,0:T(8,128)S(1)} %add.36), channel_id=1, source_target_pairs={{0,2},{1,3},{2,0},{3,1},{4,6},{5,7},{6,4},{7,5},{8,10},{9,11},{10,... | collective-permute-start | bytes 98312 | tf_op jit(solution)/shard_map/ppermute | solution.py:254
  40.8 1.9 %collective-permute-done.3 = f32[4,16,128]{2,1,0:T(8,128)S(1)} collective-permute-done((f32[4,16,128]{2,1,0:T(8,128)S(1)}, f32[4,16,128]{2,1,0:T(8,128)S(1)}, u32[]{:S(2)}, u32[]{:S(2)}) %collective-permute-start.3) | collective-permute-done | bytes 32800 | tf_op jit(solution)/shard_map/ppermute | solution.py:254
  42.7 1.8 %collective-permute-start.4 = (f32[1,16,128]{2,1,0:T(8,128)S(1)}, f32[1,16,128]{2,1,0:T(8,128)S(1)}, u32[]{:S(2)}, u32[]{:S(2)}) collective-permute-start(f32[1,16,128]{2,1,0:T(8,128)S(1)} %get-tuple-element.24), channel_id=1, source_target_pairs={{0,4},{4,0},{8,12},{12,8},{16,20},{20,16},{24,28},{28,24},{1,5},{5... | collective-permute-start | bytes 24584 | tf_op jit(solution)/shard_map/ppermute | solution.py:254
  44.5 0.1 copy.28
  44.6 1.7 %collective-permute-done.4 = f32[1,16,128]{2,1,0:T(8,128)S(1)} collective-permute-done((f32[1,16,128]{2,1,0:T(8,128)S(1)}, f32[1,16,128]{2,1,0:T(8,128)S(1)}, u32[]{:S(2)}, u32[]{:S(2)}) %collective-permute-start.4) | collective-permute-done | bytes 8224 | tf_op jit(solution)/shard_map/ppermute | solution.py:254
  46.4 3.9 %collective-permute-start.7 = (f32[2,16,128]{2,1,0:T(8,128)S(1)}, f32[2,16,128]{2,1,0:T(8,128)S(1)}, u32[]{:S(2)}, u32[]{:S(2)}) collective-permute-start(f32[2,16,128]{2,1,0:T(8,128)S(1)} %pad_maximum_fusion.1), channel_id=1, source_target_pairs={{0,24},{4,28},{8,16},{12,20},{16,8},{20,12},{24,0},{28,4},{1,25},{... | collective-permute-start | bytes 49160 | tf_op jit(solution)/shard_map/ppermute | solution.py:254
  50.3 0.0 collective-permute-start.6
  50.3 0.6 collective-permute-start.5
  50.8 3.3 %collective-permute-done.5 = f32[2,16,128]{2,1,0:T(8,128)S(1)} collective-permute-done((f32[2,16,128]{2,1,0:T(8,128)S(1)}, f32[2,16,128]{2,1,0:T(8,128)S(1)}, u32[]{:S(2)}, u32[]{:S(2)}) %collective-permute-start.5) | collective-permute-done | bytes 16416 | tf_op jit(solution)/shard_map/ppermute | solution.py:254
  54.1 3.8 %collective-permute-done.6 = f32[2,16,128]{2,1,0:T(8,128)S(1)} collective-permute-done((f32[2,16,128]{2,1,0:T(8,128)S(1)}, f32[2,16,128]{2,1,0:T(8,128)S(1)}, u32[]{:S(2)}, u32[]{:S(2)}) %collective-permute-start.6) | collective-permute-done | bytes 16416 | tf_op jit(solution)/shard_map/ppermute | solution.py:254
  57.9 0.0 collective-permute-done.7
  57.9 0.0 copy-start.7
  57.9 0.0 copy-start.8
  58.0 0.0 all-to-all-done.1.state_ref
  58.0 3.8 %all-to-all-start = ((f32[8,2,2,4,3,8,128]{6,5,4,3,2,1,0:T(8,128)}), f32[8,2,2,4,3,8,128]{6,5,4,3,2,1,0:T(8,128)S(1)}, u32[]{:S(2)}, u32[]{:S(2)}) async-start(f32[8,2,2,4,3,8,128]{6,5,4,3,2,1,0:T(8,128)} %copy-done.1), calls=%async_computation | async-start | bytes 3145728 | tf_op jit(solution)/shard_map/all_to_all | solution.py:775
  61.8 0.1 collective-permute-start.10
  61.8 1.3 %collective-permute-start.9 = (f32[1,8,16,128]{3,2,1,0:T(8,128)S(1)}, f32[1,8,16,128]{3,2,1,0:T(8,128)S(1)}, u32[]{:S(2)}, u32[]{:S(2)}) collective-permute-start(f32[1,8,16,128]{3,2,1,0:T(8,128)S(1)} %bitcast.25), channel_id=1, source_target_pairs={{0,2},{1,3},{2,0},{3,1},{4,6},{5,7},{6,4},{7,5},{8,10},{9,11},{10,... | collective-permute-start | bytes 196616 | tf_op jit(solution)/shard_map/ppermute | solution.py:254
  63.1 0.6 collective-permute-start.8
  63.7 0.1 pad_add_fusion.2.start_ref
  63.8 2.5 %collective-permute-done.10 = f32[1,8,16,128]{3,2,1,0:T(8,128)S(1)} collective-permute-done((f32[1,8,16,128]{3,2,1,0:T(8,128)S(1)}, f32[1,8,16,128]{3,2,1,0:T(8,128)S(1)}, u32[]{:S(2)}, u32[]{:S(2)}) %collective-permute-start.10) | collective-permute-done | bytes 65568 | tf_op jit(solution)/shard_map/ppermute | solution.py:254
  66.2 1.0 collective-permute-done.9
  67.3 0.0 collective-permute-done.8
  67.3 0.0 copy-done.7
  67.3 0.0 copy-done.8
  67.3 0.0 copy-start.6
  67.3 8.8 %chain.1 = (bf16[4,2,64,112]{3,2,1,0:T(8,128)(2,1)S(1)}, bf16[4,2,32,192]{3,2,1,0:T(8,128)(2,1)S(1)}, bf16[4,2,3,64,112]{4,3,2,1,0:T(8,128)(2,1)S(1)}, bf16[4,2,3,32,192]{4,3,2,1,0:T(8,128)(2,1)S(1)}, s32[4,2]{1,0:T(4,128)S(1)}) custom-call(s32[4]{0:T(128)S(1)} %pad_add_fusion.2.start_ref, f32[4,8,16,128]{3,2,1,0:T(8,128)S(1)} %pad_maximum_fusion.every_ref, ...), custom_call_target="tpu_custom_call" | custom-call | flops 25999998976 | bytes 85000000 | tf_op jit(solution)/shard_map/chain/pallas_call | solution.py:509
  76.1 0.0 copy-start.2
  76.1 0.7 copy-done.2
  76.8 0.0 copy-start.3
  76.8 0.8 copy-done.3
  77.6 0.0 copy-done.6
  77.6 9.2 %update.2.rest_0_ = f32[32,3,32,256]{3,2,1,0:T(8,128)} custom-call(s32[2]{0:T(128)S(1)} %copy-done.6, s32[4]{0:T(128)S(1)} %pad_add_fusion.2.start_ref, s32[4,2]{1,0:T(4,128)S(1)} %get-tuple-element.17.count_ref, f32[8,2,2,4,3,8,128]{6,5,4,3,2,1,0:T(8,128)} %all-to-all-done.1.state_ref, s32[32,256]{1,0:T(8,128)S(1)} %copy-done.5, ...), custom_call_target="tpu_custom_call" | custom-call | tf_op jit(solution)/shard_map/update/pallas_call | solution.py:674
  86.8 12.0 %all-to-all-done.state_ref = f32[8,2,2,4,3,8,128]{6,5,4,3,2,1,0:T(8,128)S(1)} async-done(((f32[8,2,2,4,3,8,128]{6,5,4,3,2,1,0:T(8,128)}), f32[8,2,2,4,3,8,128]{6,5,4,3,2,1,0:T(8,128)S(1)}, u32[]{:S(2)}, u32[]{:S(2)}) %all-to-all-start) | async-done | bytes 1572896 | tf_op jit(solution)/shard_map/all_to_all | solution.py:775
  98.8 9.1 %update.3 = f32[32,3,32,256]{3,2,1,0:T(8,128)} custom-call(s32[2]{0:T(128)S(1)} %iota_multiply_fusion.tile_ref, s32[4]{0:T(128)S(1)} %pad_add_fusion.2.start_ref, s32[4,2]{1,0:T(4,128)S(1)} %get-tuple-element.17.count_ref, f32[8,2,2,4,3,8,128]{6,5,4,3,2,1,0:T(8,128)S(1)} %all-to-all-done.state_ref, ...), custom_call_target="tpu_custom_call", output_to_operand_aliasing={{}: (9, {})} | custom-call | tf_op jit(solution)/shard_map/update/pallas_call | solution.py:674
  (17 shorter events, 0.1 us)
Async XLA Ops:
  0.0 5.4 %copy-start.4 = (f32[32,2048]{1,0:T(8,128)S(1)}, f32[32,2048]{1,0:T(8,128)}, u32[]{:S(2)}) copy-start(f32[32,2048]{1,0:T(8,128)} %refs_1_.3) | copy-start | bytes 786436
  0.0 5.4 %copy-start = (f32[4,3,32,2048]{3,2,1,0:T(8,128)S(1)}, f32[4,3,32,2048]{3,2,1,0:T(8,128)}, u32[]{:S(2)}) copy-start(f32[4,3,32,2048]{3,2,1,0:T(8,128)} %refs_0_.3) | copy-start | bytes 9437188
  2.9 19.6 %collective-permute-start = (f32[13,8,2048]{2,1,0:T(8,128)}, f32[13,8,2048]{2,1,0:T(8,128)}, u32[]{:S(2)}, u32[]{:S(2)}) collective-permute-start(f32[13,8,2048]{2,1,0:T(8,128)} %get-tuple-element.14), channel_id=1, source_target_pairs={{0,1},{1,2},{2,3},{3,0},{4,5},{5,6},{6,7},{7,4},{8,9},{9,10},{10,1... | collective-permute-start | bytes 2555912 | tf_op jit(solution)/shard_map/ppermute | solution.py:729
  3.4 21.6 %collective-permute-start.1 = (f32[13,8,2048]{2,1,0:T(8,128)}, f32[13,8,2048]{2,1,0:T(8,128)}, u32[]{:S(2)}, u32[]{:S(2)}) collective-permute-start(f32[13,8,2048]{2,1,0:T(8,128)} %get-tuple-element.15), channel_id=1, source_target_pairs={{1,0},{2,1},{3,2},{0,3},{5,4},{6,5},{7,6},{4,7},{9,8},{10,9},{11,1... | collective-permute-start | bytes 2555912 | tf_op jit(solution)/shard_map/ppermute | solution.py:729
  12.8 6.7 %copy-start.9 = (s32[4,256]{1,0:T(4,128)S(1)}, s32[4,256]{1,0:T(4,128)}, u32[]{:S(2)}) copy-start(s32[4,256]{1,0:T(4,128)} %param.11) | copy-start | bytes 12292
  12.8 45.2 %all-to-all-start.1 = ((f32[8,2,2,4,3,8,128]{6,5,4,3,2,1,0:T(8,128)}), f32[8,2,2,4,3,8,128]{6,5,4,3,2,1,0:T(8,128)}, u32[]{:S(2)}, u32[]{:S(2)}) async-start(f32[8,2,2,4,3,8,128]{6,5,4,3,2,1,0:T(8,128)} %inner.1.height_ref), calls=%async_computation.1 | async-start | bytes 3145728 | tf_op jit(solution)/shard_map/all_to_all | solution.py:760
  19.4 2.3 %copy-start.5 = (s32[32,256]{1,0:T(8,128)S(1)}, s32[32,256]{1,0:T(8,128)}, u32[]{:S(2)}) copy-start(s32[32,256]{1,0:T(8,128)} %cutoff_ref.5) | copy-start | bytes 98308
  36.0 1.2 %copy-start.1 = (f32[8,2,2,4,3,8,128]{6,5,4,3,2,1,0:T(8,128)}, f32[8,2,2,4,3,8,128]{6,5,4,3,2,1,0:T(8,128)S(1)}, u32[]{:S(2)}) copy-start(f32[8,2,2,4,3,8,128]{6,5,4,3,2,1,0:T(8,128)S(1)} %outer.1.height_ref) | copy-start | bytes 4718596
  37.1 1.2 %collective-permute-start.2 = (f32[4,16,128]{2,1,0:T(8,128)S(1)}, f32[4,16,128]{2,1,0:T(8,128)S(1)}, u32[]{:S(2)}, u32[]{:S(2)}) collective-permute-start(f32[4,16,128]{2,1,0:T(8,128)S(1)} %pick_outer.1), channel_id=1, source_target_pairs={{0,1},{1,0},{2,3},{3,2},{4,5},{5,4},{6,7},{7,6},{8,9},{9,8},{10,11... | collective-permute-start | bytes 98312 | tf_op jit(solution)/shard_map/ppermute | solution.py:254
  38.4 4.3 %collective-permute-start.3 = (f32[4,16,128]{2,1,0:T(8,128)S(1)}, f32[4,16,128]{2,1,0:T(8,128)S(1)}, u32[]{:S(2)}, u32[]{:S(2)}) collective-permute-start(f32[4,16,128]{2,1,0:T(8,128)S(1)} %add.36), channel_id=1, source_target_pairs={{0,2},{1,3},{2,0},{3,1},{4,6},{5,7},{6,4},{7,5},{8,10},{9,11},{10,... | collective-permute-start | bytes 98312 | tf_op jit(solution)/shard_map/ppermute | solution.py:254
  42.7 3.7 %collective-permute-start.4 = (f32[1,16,128]{2,1,0:T(8,128)S(1)}, f32[1,16,128]{2,1,0:T(8,128)S(1)}, u32[]{:S(2)}, u32[]{:S(2)}) collective-permute-start(f32[1,16,128]{2,1,0:T(8,128)S(1)} %get-tuple-element.24), channel_id=1, source_target_pairs={{0,4},{4,0},{8,12},{12,8},{16,20},{20,16},{24,28},{28,24},{1,5},{5... | collective-permute-start | bytes 24584 | tf_op jit(solution)/shard_map/ppermute | solution.py:254
  46.4 11.5 %collective-permute-start.7 = (f32[2,16,128]{2,1,0:T(8,128)S(1)}, f32[2,16,128]{2,1,0:T(8,128)S(1)}, u32[]{:S(2)}, u32[]{:S(2)}) collective-permute-start(f32[2,16,128]{2,1,0:T(8,128)S(1)} %pad_maximum_fusion.1), channel_id=1, source_target_pairs={{0,24},{4,28},{8,16},{12,20},{16,8},{20,12},{24,0},{28,4},{1,25},{... | collective-permute-start | bytes 49160 | tf_op jit(solution)/shard_map/ppermute | solution.py:254
  50.3 7.7 %collective-permute-start.6 = (f32[2,16,128]{2,1,0:T(8,128)S(1)}, f32[2,16,128]{2,1,0:T(8,128)S(1)}, u32[]{:S(2)}, u32[]{:S(2)}) collective-permute-start(f32[2,16,128]{2,1,0:T(8,128)S(1)} %pad_maximum_fusion.1), channel_id=1, source_target_pairs={{0,16},{4,20},{8,24},{12,28},{16,0},{20,4},{24,8},{28,12},{1,17},{... | collective-permute-start | bytes 49160 | tf_op jit(solution)/shard_map/ppermute | solution.py:254
  50.3 3.8 %collective-permute-start.5 = (f32[2,16,128]{2,1,0:T(8,128)S(1)}, f32[2,16,128]{2,1,0:T(8,128)S(1)}, u32[]{:S(2)}, u32[]{:S(2)}) collective-permute-start(f32[2,16,128]{2,1,0:T(8,128)S(1)} %pad_maximum_fusion.1), channel_id=1, source_target_pairs={{0,8},{4,12},{8,0},{12,4},{16,24},{20,28},{24,16},{28,20},{1,9},{5... | collective-permute-start | bytes 49160 | tf_op jit(solution)/shard_map/ppermute | solution.py:254
  57.9 9.4 %copy-start.7 = (f32[4,256]{1,0:T(4,128)S(1)}, f32[4,256]{1,0:T(4,128)}, u32[]{:S(2)}) copy-start(f32[4,256]{1,0:T(4,128)} %value_ref.1) | copy-start | bytes 12292
  57.9 9.4 %copy-start.8 = (f32[4,256]{1,0:T(4,128)S(1)}, f32[4,256]{1,0:T(4,128)}, u32[]{:S(2)}) copy-start(f32[4,256]{1,0:T(4,128)} %variance_ref.1) | copy-start | bytes 12292
  58.0 40.9 %all-to-all-start = ((f32[8,2,2,4,3,8,128]{6,5,4,3,2,1,0:T(8,128)}), f32[8,2,2,4,3,8,128]{6,5,4,3,2,1,0:T(8,128)S(1)}, u32[]{:S(2)}, u32[]{:S(2)}) async-start(f32[8,2,2,4,3,8,128]{6,5,4,3,2,1,0:T(8,128)} %copy-done.1), calls=%async_computation | async-start | bytes 3145728 | tf_op jit(solution)/shard_map/all_to_all | solution.py:775
  61.8 4.5 %collective-permute-start.10 = (f32[1,8,16,128]{3,2,1,0:T(8,128)S(1)}, f32[1,8,16,128]{3,2,1,0:T(8,128)S(1)}, u32[]{:S(2)}, u32[]{:S(2)}) collective-permute-start(f32[1,8,16,128]{3,2,1,0:T(8,128)S(1)} %bitcast.24), channel_id=1, source_target_pairs={{0,3},{1,2},{2,1},{3,0},{4,7},{5,6},{6,5},{7,4},{8,11},{9,10},{10,... | collective-permute-start | bytes 196616 | tf_op jit(solution)/shard_map/ppermute | solution.py:254
  61.8 5.4 %collective-permute-start.9 = (f32[1,8,16,128]{3,2,1,0:T(8,128)S(1)}, f32[1,8,16,128]{3,2,1,0:T(8,128)S(1)}, u32[]{:S(2)}, u32[]{:S(2)}) collective-permute-start(f32[1,8,16,128]{3,2,1,0:T(8,128)S(1)} %bitcast.25), channel_id=1, source_target_pairs={{0,2},{1,3},{2,0},{3,1},{4,6},{5,7},{6,4},{7,5},{8,10},{9,11},{10,... | collective-permute-start | bytes 196616 | tf_op jit(solution)/shard_map/ppermute | solution.py:254
  63.1 4.2 %collective-permute-start.8 = (f32[1,8,16,128]{3,2,1,0:T(8,128)S(1)}, f32[1,8,16,128]{3,2,1,0:T(8,128)S(1)}, u32[]{:S(2)}, u32[]{:S(2)}) collective-permute-start(f32[1,8,16,128]{3,2,1,0:T(8,128)S(1)} %bitcast.26), channel_id=1, source_target_pairs={{0,1},{1,0},{2,3},{3,2},{4,5},{5,4},{6,7},{7,6},{8,9},{9,8},{10,11... | collective-permute-start | bytes 196616 | tf_op jit(solution)/shard_map/ppermute | solution.py:254
  67.3 10.3 %copy-start.6 = (s32[2]{0:T(128)S(1)}, s32[2]{0:T(128)}, u32[]{:S(2)}) copy-start(s32[2]{0:T(128)} %constant.63.clone.tile_ref) | copy-start | bytes 28
  76.1 0.7 copy-start.2
  76.8 0.8 copy-start.3
